TPU v7x, 512 devices: a whole 4x4x16 slice. The times are simulated.
512 devices in a mesh: lat: 32 (over z_lo, x), lon: 16 (over y, z_hi, core).
Axes of the slice: x: 4, y: 4, z: 16 (z_hi: 2, z_lo: 8; z = z_hi * 8 + z_lo), core: 2. Of those that a mesh axis runs over, the one named last changes fastest.
Arguments:
- grid_field: bfloat16 [512, 2880, 64], P('lat', 'lon'), may hold values from -6 to 6
- disco_reach: int32 [512], P('lat'), may hold values from 1 to 20, as said below
- disco_taps: float32 [512, 492], P('lat'), may hold values from -1 to 1
- disco_weight: bfloat16 [4, 64, 64], replicated, may hold values from -0.375 to 0.375
- legendre: bfloat16 [512, 32, 768], P('lat', 'lon'), may hold values from -0.25 to 0.25
- spectral_mixing_weight: bfloat16 [768, 2, 64, 64], P('lat'), may hold values from -0.5 to 0.5
Outputs:
- block_out: bfloat16 [512, 2880, 64], P('lat', 'lon')
Inputs may be any that keep to these rules, and one draw needn't show every extreme that they name: `disco_reach`: the rows at both poles reach 20.
All inputs are finite; a program needn't handle non-finite values.
Results may differ from a plain program's by a relative error of at most 0.02.
Values may be sent and summed in bfloat16 or wider, within the bound.
No kernel may reach another device: no remote copies, remote signals or barrier semaphores. Data moves between devices by JAX's collectives and lax.ppermute only.
A program may use at most 128 MiB of HBM per device.

v0:
```python
import math

import jax
import jax.numpy as jnp
from jax import lax
from jax.sharding import PartitionSpec as P

NLON = 2880
HMAX = 20
BASES = 4


def padded(cells, sides, width, closed):
    for axis, dim in sides:
        count = lax.axis_size(axis)
        ends = count if closed else count - 1
        head = lax.slice_in_dim(cells, 0, width, axis=dim)
        tail = lax.slice_in_dim(cells, cells.shape[dim] - width, cells.shape[dim], axis=dim)
        cells = jnp.concatenate(
            [
                lax.ppermute(tail, axis, [(i, (i + 1) % count) for i in range(ends)]),
                cells,
                lax.ppermute(head, axis, [((i + 1) % count, i) for i in range(ends)]),
            ],
            axis=dim,
        )
    return cells


def angles(columns, orders):
    residues = columns[:, None] * orders[None, :] % NLON
    return residues.astype(jnp.float32) * (2.0 * math.pi / NLON)


def forward_table(columns, orders):
    phases = angles(columns, orders)
    factor = 1.0 / math.sqrt(NLON)
    return jnp.stack([jnp.cos(phases) * factor, -jnp.sin(phases) * factor], axis=1).astype(
        jnp.bfloat16
    )


def inverse_table(orders, columns, mode_count):
    phases = angles(columns, orders)
    factor = 1.0 / math.sqrt(mode_count)
    return jnp.stack([jnp.cos(phases).T * factor, -jnp.sin(phases).T * factor], axis=0).astype(
        jnp.bfloat16
    )


def disco(grid_field, disco_reach, disco_taps, disco_weight):
    lat_rows, lon_cols, channels = grid_field.shape
    tap_count = 2 * HMAX + 1
    widened = padded(grid_field, (("lon", 1),), HMAX, True)
    extended = padded(widened, (("lat", 0),), 1, False)
    flattened = extended.reshape(lat_rows + 2, (lon_cols + 2 * HMAX) * channels)
    offsets = jnp.abs(jnp.arange(tap_count, dtype=jnp.int32) - HMAX)
    within = offsets[None, :] <= disco_reach[:, None]
    kernel_coef = jnp.where(
        within[:, None, None, :], disco_taps.reshape(lat_rows, BASES, 3, tap_count), 0.0
    )
    running_totals = [
        jnp.zeros((lat_rows, lon_cols * channels), jnp.float32) for kernel in range(BASES)
    ]
    for lat_step in range(3):
        for lon_step in range(tap_count):
            window = flattened[
                lat_step : lat_step + lat_rows,
                lon_step * channels : (lon_step + lon_cols) * channels,
            ].astype(jnp.float32)
            for kernel in range(BASES):
                running_totals[kernel] = (
                    running_totals[kernel]
                    + kernel_coef[:, kernel, lat_step, lon_step][:, None] * window
                )
    basis_sums = (
        jnp.stack(running_totals, axis=1)
        .astype(jnp.bfloat16)
        .reshape(lat_rows, BASES, lon_cols, channels)
    )
    return jnp.einsum("rkjc,kcd->rjd", basis_sums, disco_weight, preferred_element_type=jnp.float32)


def per_device(grid_field, disco_reach, disco_taps, disco_weight, legendre, spectral_mixing_weight):
    lat_rows, lon_cols, channels = grid_field.shape
    orders_dev = legendre.shape[1]
    lon_count = lax.axis_size("lon")
    lat_count = lax.axis_size("lat")
    mode_count = orders_dev * lon_count
    harmonic_degree_rows = legendre.shape[2] // lat_count
    lon_place = lax.axis_index("lon")
    disco_out = disco(grid_field, disco_reach, disco_taps, disco_weight)
    mode_index = jnp.arange(mode_count, dtype=jnp.int32)
    own_columns = lon_place * lon_cols + jnp.arange(lon_cols, dtype=jnp.int32)
    full_table = forward_table(jnp.arange(NLON, dtype=jnp.int32), mode_index)
    row_spectra = jnp.einsum(
        "blv,lis->bsiv",
        lax.all_to_all(grid_field, "lon", split_axis=0, concat_axis=1, tiled=True),
        full_table,
        preferred_element_type=jnp.float32,
    ).astype(jnp.bfloat16)
    spectra = lax.all_to_all(row_spectra, "lon", split_axis=1, concat_axis=0, tiled=True).reshape(
        lat_rows, orders_dev, 2 * channels
    )
    orders_global = lon_place * orders_dev + jnp.arange(orders_dev, dtype=jnp.int32)

    def masked(amount):
        degree = jnp.arange(amount, dtype=jnp.int32)
        within = degree[None, :] >= orders_global[:, None]
        return jnp.where(within[None], legendre, jnp.zeros((), jnp.bfloat16))

    coeffs = lax.psum_scatter(
        jnp.einsum(
            "iml,imc->lmc",
            masked(harmonic_degree_rows * lax.axis_size("lat")),
            spectra,
            preferred_element_type=jnp.float32,
        ).astype(jnp.bfloat16),
        "lat",
        scatter_dimension=0,
        tiled=True,
    )
    real_part = spectral_mixing_weight[:, 0]
    imag_part = spectral_mixing_weight[:, 1]
    upper = jnp.concatenate([real_part, imag_part], axis=2)
    lower = jnp.concatenate([-imag_part, real_part], axis=2)
    complex_block = jnp.concatenate([upper, lower], axis=1)
    mixed_modes = jnp.einsum(
        "lmc,lcd->lmd", coeffs, complex_block, preferred_element_type=jnp.float32
    ).astype(jnp.bfloat16)
    portion = lax.all_gather(mixed_modes, "lat", axis=0, tiled=True)
    grid_modes = jnp.einsum(
        "iml,lmc->imc", masked(portion.shape[0]), portion, preferred_element_type=jnp.float32
    ).astype(jnp.bfloat16)
    own_inverse = inverse_table(mode_index, own_columns, mode_count)
    portion = lax.all_gather(grid_modes, "lon", axis=1, tiled=True)
    amount = portion.shape[1]
    shaped = portion.reshape(lat_rows, amount, 2, channels)
    spectral_out = jnp.einsum(
        "impc,pmj->ijc", shaped, own_inverse, preferred_element_type=jnp.float32
    ).astype(jnp.bfloat16)
    combined = spectral_out.astype(jnp.float32) + disco_out
    return (grid_field.astype(jnp.float32) + jax.nn.gelu(combined, approximate=True)).astype(
        jnp.bfloat16
    )


def solution(mesh):
    in_specs = (
        P("lat", "lon", None),
        P("lat"),
        P("lat", None),
        P(),
        P("lat", "lon", None),
        P("lat", None, None, None),
    )
    out_specs = P("lat", "lon", None)
    return jax.shard_map(
        per_device, mesh=mesh, in_specs=in_specs, out_specs=out_specs, check_vma=False
    )
```

profile of v0, /device:TPU:1, one launch (start us, length us, event | category | flops | bytes accessed | tf_op | source)
XLA Modules:
  0.0 830.0 jit_solution(7017814243375401134)
XLA Ops:
  6.5 19.4 %all-to-all-start = ((bf16[16,180,64]{1,2,0:T(8,128)(2,1)}), bf16[16,180,64]{1,2,0:T(8,128)(2,1)S(1)}, u32[]{:S(2)}, u32[]{:S(2)}) async-start(bf16[16,180,64]{1,2,0:T(8,128)(2,1)} %param.6), calls=%async_computation | async-start | bytes 1048576 | tf_op jit(solution)/shard_map/all_to_all | solution.py:98
  26.8 12.2 %collective-permute-start = (bf16[16,20,64]{1,2,0:T(8,128)(2,1)}, bf16[16,20,64]{1,2,0:T(8,128)(2,1)S(1)}, u32[]{:S(2)}, u32[]{:S(2)}) collective-permute-start(bf16[16,20,64]{1,2,0:T(8,128)(2,1)} %get-tuple-element.501), channel_id=1, source_target_pairs={{0,1},{1,2},{2,3},{3,4},{4,5},{5,6},{6,7},{7,8},{8,9},{9,10},{10,1... | collective-permute-start | bytes 122888 | tf_op jit(solution)/shard_map/ppermute | solution.py:21
  39.0 1.9 collective-permute-start.1
  41.3 1.5 slice_reduce_fusion.486
  44.2 1.5 slice_reduce_fusion.490
  45.7 1.5 slice_reduce_fusion.489
  47.2 1.5 slice_reduce_fusion.488
  51.4 1.5 slice_reduce_fusion.363
  53.0 1.5 slice_reduce_fusion.362
  55.9 1.5 slice_reduce_fusion.360
  57.4 1.5 slice_reduce_fusion.359
  61.6 1.5 slice_reduce_fusion.235
  63.1 1.5 slice_reduce_fusion.234
  64.6 1.7 slice_reduce_fusion.233
  67.7 1.5 slice_reduce_fusion.231
  70.7 1.5 slice_reduce_fusion.107
  72.2 1.5 slice_reduce_fusion.106
  75.1 1.5 slice_reduce_fusion.104
  76.6 1.5 slice_reduce_fusion.103
  78.1 2.3 multiply_convert_fusion
  83.9 3.1 collective-permute-start.2
  87.0 1.7 collective-permute-start.3
  94.5 32.1 %fusion.533 = bf16[16,11520]{1,0:T(8,128)(2,1)S(1)} fusion(f32[16]{0:T(128)S(1)} %copy-done.117, f32[16]{0:T(128)S(1)} %copy-done.118, f32[16]{0:T(128)S(1)} %copy-done.119, f32[16]{0:T(128)S(1)} %copy-done.120, f32[16]{0:T(128)S(1)} %copy-done.121, f32[16]{0:T(128)S(1)} %copy-done.122, f32[16]{0:T(128)S(1)} %copy-done.123, f32[16]{0:T(128)S(1)} %copy-done.124, ...), kind=kLoop, calls=%fused_computation.1021 | loop fusion | flops 68014080 | bytes 45719232 | tf_op jit(solution)/shard_map/convert.8
  126.7 33.0 %fusion.532 = bf16[16,11520]{1,0:T(8,128)(2,1)} fusion(f32[16]{0:T(128)S(1)} %copy-done.89, f32[16]{0:T(128)S(1)} %copy-done.90, f32[16]{0:T(128)S(1)} %copy-done.91, f32[16]{0:T(128)S(1)} %copy-done.92, f32[16]{0:T(128)S(1)} %copy-done.93, f32[16]{0:T(128)S(1)} %copy-done.94, f32[16]{0:T(128)S(1)} %copy-done.95, f32[16]{0:T(128)S(1)} %copy-done.96, ...), kind=kLoop, calls=%fused_computation.1020 | loop fusion | flops 68014080 | bytes 45719232 | tf_op jit(solution)/shard_map/convert.7
  163.2 15.7 %all-to-all-start.1 = ((bf16[16,2,128]{2,1,0:T(2,128)(2,1)}), bf16[16,2,128]{2,1,0:T(2,128)(2,1)S(1)}, u32[]{:S(2)}, u32[]{:S(2)}) async-start(bf16[16,2,128]{2,1,0:T(2,128)(2,1)} %reshape.1243), calls=%async_computation.1 | async-start | bytes 16384 | tf_op jit(solution)/shard_map/all_to_all | solution.py:102
  179.4 31.8 %fusion.531 = bf16[16,11520]{1,0:T(8,128)(2,1)S(1)} fusion(f32[16]{0:T(128)S(1)} %copy-done.50, f32[16]{0:T(128)S(1)} %copy-done.51, f32[16]{0:T(128)S(1)} %copy-done.52, f32[16]{0:T(128)S(1)} %copy-done.54, f32[16]{0:T(128)S(1)} %copy-done.55, f32[16]{0:T(128)S(1)} %copy-done.56, f32[16]{0:T(128)S(1)} %copy-done.57, f32[16]{0:T(128)S(1)} %copy-done.58, ...), kind=kLoop, calls=%fused_computation.1019 | loop fusion | flops 68014080 | bytes 45719232 | tf_op jit(solution)/shard_map/convert.6
  213.6 31.9 %fusion.530 = bf16[16,11520]{1,0:T(8,128)(2,1)S(1)} fusion(f32[16]{0:T(128)S(1)} %copy-done.10, f32[16]{0:T(128)S(1)} %copy-done.11, f32[16]{0:T(128)S(1)} %copy-done.12, f32[16]{0:T(128)S(1)} %copy-done.13, f32[16]{0:T(128)S(1)} %copy-done.14, f32[16]{0:T(128)S(1)} %copy-done.15, f32[16]{0:T(128)S(1)} %copy-done.16, f32[16]{0:T(128)S(1)} %copy-done.17, ...), kind=kLoop, calls=%fused_computation.1018 | loop fusion | flops 68014080 | bytes 45719232 | tf_op jit(solution)/shard_map/convert.5
  251.3 384.7 %all-reduce.3.cloned.1.call-done = bf16[768,2,128]{2,1,0:T(2,128)(2,1)} async-done(((bf16[768,2,128]{2,1,0:T(2,128)(2,1)}), bf16[768,2,128]{2,1,0:T(2,128)(2,1)}) %all-reduce.3.cloned.1.call-update) | async-done | bytes 393232
  636.1 1.7 convolution_convert_fusion.2
  637.7 107.0 %all_gather.6 = bf16[768,2,128]{2,1,0:T(2,128)(2,1)S(1)} all-gather(bf16[24,2,128]{2,1,0:T(2,128)(2,1)S(1)} %convolution_convert_fusion.2), channel_id=1, replica_groups=mesh['lat'=32,'lon'=16] {'lat'}, dimensions={0}, use_global_device_ids=true | all-gather | bytes 405504 | tf_op jit(solution)/shard_map/all_gather | solution.py:131
  744.9 74.4 %all_gather.7 = bf16[16,32,128]{2,0,1:T(8,128)(2,1)S(1)} all-gather(bf16[16,2,128]{2,0,1:T(8,128)(2,1)S(1)} %fusion.19), channel_id=1, replica_groups=mesh['lat'=32,'lon'=16] {'lon'}, dimensions={1}, use_global_device_ids=true | all-gather | bytes 139264 | tf_op jit(solution)/shard_map/all_gather | solution.py:136
  819.8 2.9 fusion.32
  (312 shorter events, 33.5 us)
Async XLA Ops:
  6.5 813.2 %copy-start = (bf16[4,64,64]{2,1,0:T(8,128)(2,1)S(1)}, bf16[4,64,64]{2,1,0:T(8,128)(2,1)}, u32[]{:S(2)}) copy-start(bf16[4,64,64]{2,1,0:T(8,128)(2,1)} %param.9) | copy-start | bytes 98308
  6.5 19.4 %copy-start.1 = (bf16[16,180,64]{1,2,0:T(8,128)(2,1)S(1)}, bf16[16,180,64]{1,2,0:T(8,128)(2,1)}, u32[]{:S(2)}) copy-start(bf16[16,180,64]{1,2,0:T(8,128)(2,1)} %param.6) | copy-start | bytes 1105924
  6.5 34.4 %copy-start.9 = (f32[16,492]{1,0:T(8,128)S(1)}, f32[16,492]{1,0:T(8,128)}, u32[]{:S(2)}) copy-start(f32[16,492]{1,0:T(8,128)} %param.8) | copy-start | bytes 94468
  6.5 34.6 %copy-start.127 = (s32[16]{0:T(128)S(1)}, s32[16]{0:T(128)}, u32[]{:S(2)}) copy-start(s32[16]{0:T(128)} %param.7) | copy-start | bytes 196
  6.5 153.2 %all-to-all-start = ((bf16[16,180,64]{1,2,0:T(8,128)(2,1)}), bf16[16,180,64]{1,2,0:T(8,128)(2,1)S(1)}, u32[]{:S(2)}, u32[]{:S(2)}) async-start(bf16[16,180,64]{1,2,0:T(8,128)(2,1)} %param.6), calls=%async_computation | async-start | bytes 1048576 | tf_op jit(solution)/shard_map/all_to_all | solution.py:98
  26.8 57.0 %collective-permute-start = (bf16[16,20,64]{1,2,0:T(8,128)(2,1)}, bf16[16,20,64]{1,2,0:T(8,128)(2,1)S(1)}, u32[]{:S(2)}, u32[]{:S(2)}) collective-permute-start(bf16[16,20,64]{1,2,0:T(8,128)(2,1)} %get-tuple-element.501), channel_id=1, source_target_pairs={{0,1},{1,2},{2,3},{3,4},{4,5},{5,6},{6,7},{7,8},{8,9},{9,10},{10,1... | collective-permute-start | bytes 122888 | tf_op jit(solution)/shard_map/ppermute | solution.py:21
  39.0 44.7 %collective-permute-start.1 = (bf16[16,20,64]{1,2,0:T(8,128)(2,1)S(1)}, bf16[16,20,64]{1,2,0:T(8,128)(2,1)S(1)}, u32[]{:S(2)}, u32[]{:S(2)}) collective-permute-start(bf16[16,20,64]{1,2,0:T(8,128)(2,1)S(1)} %get-tuple-element.502), channel_id=1, source_target_pairs={{1,0},{2,1},{3,2},{4,3},{5,4},{6,5},{7,6},{8,7},{9,8},{10,9},{11,1... | collective-permute-start | bytes 122888 | tf_op jit(solution)/shard_map/ppermute | solution.py:23
  83.9 8.0 collective-permute-start.2
  87.0 4.9 collective-permute-start.3
  94.4 32.2 %copy-start.88 = (f32[16]{0:T(128)S(1)}, f32[16]{0:T(128)}, u32[]{:S(2)}) copy-start(f32[16]{0:T(128)} %get-tuple-element.133) | copy-start | bytes 196
  94.4 32.2 %copy-start.89 = (f32[16]{0:T(128)S(1)}, f32[16]{0:T(128)}, u32[]{:S(2)}) copy-start(f32[16]{0:T(128)} %get-tuple-element.144) | copy-start | bytes 196
  94.4 32.2 %copy-start.90 = (f32[16]{0:T(128)S(1)}, f32[16]{0:T(128)}, u32[]{:S(2)}) copy-start(f32[16]{0:T(128)} %get-tuple-element.145) | copy-start | bytes 196
  94.5 32.2 %copy-start.91 = (f32[16]{0:T(128)S(1)}, f32[16]{0:T(128)}, u32[]{:S(2)}) copy-start(f32[16]{0:T(128)} %get-tuple-element.146) | copy-start | bytes 196
  94.5 32.2 %copy-start.92 = (f32[16]{0:T(128)S(1)}, f32[16]{0:T(128)}, u32[]{:S(2)}) copy-start(f32[16]{0:T(128)} %get-tuple-element.147) | copy-start | bytes 196
  94.5 32.2 %copy-start.93 = (f32[16]{0:T(128)S(1)}, f32[16]{0:T(128)}, u32[]{:S(2)}) copy-start(f32[16]{0:T(128)} %get-tuple-element.148) | copy-start | bytes 196
  94.5 32.2 %copy-start.94 = (f32[16]{0:T(128)S(1)}, f32[16]{0:T(128)}, u32[]{:S(2)}) copy-start(f32[16]{0:T(128)} %get-tuple-element.149) | copy-start | bytes 196
  94.5 32.2 %copy-start.95 = (f32[16]{0:T(128)S(1)}, f32[16]{0:T(128)}, u32[]{:S(2)}) copy-start(f32[16]{0:T(128)} %get-tuple-element.150) | copy-start | bytes 196
  94.5 32.2 %copy-start.96 = (f32[16]{0:T(128)S(1)}, f32[16]{0:T(128)}, u32[]{:S(2)}) copy-start(f32[16]{0:T(128)} %get-tuple-element.151) | copy-start | bytes 196
  94.5 32.2 %copy-start.126 = (f32[16]{0:T(128)S(1)}, f32[16]{0:T(128)}, u32[]{:S(2)}) copy-start(f32[16]{0:T(128)} %get-tuple-element.152) | copy-start | bytes 196
  160.1 18.9 %copy-start.49 = (f32[16]{0:T(128)S(1)}, f32[16]{0:T(128)}, u32[]{:S(2)}) copy-start(f32[16]{0:T(128)} %get-tuple-element.261) | copy-start | bytes 196
  160.1 18.9 %copy-start.50 = (f32[16]{0:T(128)S(1)}, f32[16]{0:T(128)}, u32[]{:S(2)}) copy-start(f32[16]{0:T(128)} %get-tuple-element.277) | copy-start | bytes 196
  160.1 18.9 %copy-start.51 = (f32[16]{0:T(128)S(1)}, f32[16]{0:T(128)}, u32[]{:S(2)}) copy-start(f32[16]{0:T(128)} %get-tuple-element.278) | copy-start | bytes 196
  160.1 18.9 %copy-start.52 = (f32[16]{0:T(128)S(1)}, f32[16]{0:T(128)}, u32[]{:S(2)}) copy-start(f32[16]{0:T(128)} %get-tuple-element.279) | copy-start | bytes 196
  160.1 18.9 %copy-start.53 = (f32[16]{0:T(128)S(1)}, f32[16]{0:T(128)}, u32[]{:S(2)}) copy-start(f32[16]{0:T(128)} %get-tuple-element.280) | copy-start | bytes 196
  160.2 18.9 %copy-start.54 = (f32[16]{0:T(128)S(1)}, f32[16]{0:T(128)}, u32[]{:S(2)}) copy-start(f32[16]{0:T(128)} %get-tuple-element.281) | copy-start | bytes 196
  160.2 18.9 %copy-start.55 = (f32[16]{0:T(128)S(1)}, f32[16]{0:T(128)}, u32[]{:S(2)}) copy-start(f32[16]{0:T(128)} %get-tuple-element.282) | copy-start | bytes 196
  163.2 48.4 %all-to-all-start.1 = ((bf16[16,2,128]{2,1,0:T(2,128)(2,1)}), bf16[16,2,128]{2,1,0:T(2,128)(2,1)S(1)}, u32[]{:S(2)}, u32[]{:S(2)}) async-start(bf16[16,2,128]{2,1,0:T(2,128)(2,1)} %reshape.1243), calls=%async_computation.1 | async-start | bytes 16384 | tf_op jit(solution)/shard_map/all_to_all | solution.py:102
  178.9 457.2 %all-reduce.3.cloned.1.call-start = ((), (), s32[]{:S(2)}) async-start(), calls=%async_computation.2 | async-start | bytes 786432
  249.7 386.4 %copy-start.6 = (bf16[24,64,64]{2,1,0:T(8,128)(2,1)S(1)}, bf16[24,64,64]{2,1,0:T(8,128)(2,1)}, u32[]{:S(2)}) copy-start(bf16[24,64,64]{2,1,0:T(8,128)(2,1)} %fusion.561) | copy-start | bytes 589828
  250.2 385.9 %copy-start.7 = (bf16[24,64,64]{2,1,0:T(8,128)(2,1)S(1)}, bf16[24,64,64]{2,1,0:T(8,128)(2,1)}, u32[]{:S(2)}) copy-start(bf16[24,64,64]{2,1,0:T(8,128)(2,1)} %get-tuple-element.499) | copy-start | bytes 589828
  744.9 74.9 %copy-start.4 = (bf16[16,1,180,64]{2,3,1,0:T(8,128)(2,1)S(1)}, bf16[16,1,180,64]{2,3,1,0:T(8,128)(2,1)}, u32[]{:S(2)}) copy-start(bf16[16,1,180,64]{2,3,1,0:T(8,128)(2,1)} %copy.68) | copy-start | bytes 1105924
  744.9 74.9 %copy-start.5 = (bf16[16,1,180,64]{2,3,1,0:T(8,128)(2,1)S(1)}, bf16[16,1,180,64]{2,3,1,0:T(8,128)(2,1)}, u32[]{:S(2)}) copy-start(bf16[16,1,180,64]{2,3,1,0:T(8,128)(2,1)} %copy.69) | copy-start | bytes 1105924
  (103 other events, 736.1 us)
Sparse Core Ops, SparseCore 0:
  213.3 422.7 all-reduce.2
where the time goes:
time: 839 us; the launch traced here: 830 us
  waiting for transfers between devices  385 us (46%)
  blocking collectives  181 us (22%)
  other arithmetic  133 us (16%)
  starting transfers between devices  54.1 us (6%)
  local copies, waits for them, and re-layouts  53.6 us (6%)
  between operations  16.6 us (2%)
    unnamed x2, waiting for transfers between devices  385 us
    another operation x6, other arithmetic  131 us
    all_gather x1, blocking collectives, per_device(): portion = lax.all_gather(mixed_modes, 'lat', axis=0, tiled=True)  107 us
    all_gather x1, blocking collectives, per_device(): portion = lax.all_gather(grid_modes, 'lon', axis=1, tiled=True)  74.4 us
    slice x27, local copies, waits for them, and re-layouts, disco(): kernel_coef[:, kernel, lat_step, lon_step][:, None] * window  39.3 us
    all_to_all x1, starting transfers between devices, per_device(): lax.all_to_all(grid_field, 'lon', split_axis=0, concat_axis=1, tiled=True)  19.4 us
  transfers between devices with their start and end apart: 7, of which 1 were waited for; matrix products, arithmetic and copies ran while one was open for 22% of the time, Pallas kernels for 0%

commit v1 on v0

v1 whole, which is shorter than its diff:
```python
import math

import jax
import jax.numpy as jnp
import numpy as np
from jax import lax
from jax.experimental import pallas as pl
from jax.experimental.pallas import tpu as pltpu
from jax.sharding import Mesh
from jax.sharding import PartitionSpec as P

NLON = 2880
MODES = 32
HMAX = 20
TAPS = 2 * HMAX + 1
BASES = 4
LANES = 128
BF16 = jnp.bfloat16
F32 = jnp.float32
PLANE = ("x", "y", "core")
LINE = ("zh", "zl")
ORDER_GROUP = ("y", "core")


def orders_by_group():
    out = np.zeros((8, 4), np.int64)
    for y in range(4):
        for core in range(2):
            for zh in range(2):
                for odd in range(2):
                    out[y * 2 + core, zh * 2 + odd] = (y * 4 + zh * 2 + core) * 2 + odd
    return out.reshape(-1)


def tables(lon_cols):
    residues = (orders_by_group()[:, None] * np.arange(NLON)[None, :]) % NLON
    phases = residues.astype(np.float32) * np.float32(2.0 * math.pi / NLON)
    waves = np.stack([np.cos(phases), -np.sin(phases)], axis=1).astype(np.float32)
    waves = waves.reshape(MODES, 2, NLON // lon_cols, lon_cols).transpose(2, 0, 1, 3)
    forward = (waves * np.float32(1.0 / math.sqrt(NLON))).astype(BF16)
    inverse = (waves * np.float32(1.0 / math.sqrt(MODES))).astype(BF16)
    return forward, inverse


def toeplitz_kernel(ext_ref, base_ref, weight_ref, out_ref, band_ref):
    row = pl.program_id(0)

    @pl.when(row == 0)
    def _():
        band_ref[...] = jnp.zeros_like(band_ref)

    r = lax.broadcasted_iota(jnp.int32, (LANES, LANES), 0)
    s = lax.broadcasted_iota(jnp.int32, (LANES, LANES), 1)
    for a in range(3):
        for k in range(BASES):
            line = jnp.broadcast_to(base_ref[0, k * 3 + a][None, :], (LANES, LANES))
            circ = pltpu.roll(line, 0, 1, stride=1, stride_axis=0)
            near = jnp.where(s <= r, circ, 0.0).astype(BF16)
            far = jnp.where(s > r, circ, 0.0)[:48].astype(BF16)
            band_ref[a * 256 : a * 256 + LANES, k * LANES : (k + 1) * LANES] = near
            band_ref[a * 256 + LANES : a * 256 + LANES + 48, k * LANES : (k + 1) * LANES] = far
    rows = [ext_ref[row + a] for a in range(3)]
    zeros = jnp.zeros((64, LANES), BF16)
    upper = jnp.concatenate(rows, axis=1)
    lower = jnp.concatenate([p for v in rows for p in (v[:, LANES:], zeros)], axis=1)
    sums = jnp.dot(
        jnp.concatenate([upper, lower], axis=0), band_ref[...], preferred_element_type=F32
    ).astype(BF16)
    stacked = jnp.concatenate(
        [
            jnp.concatenate(
                [sums[u * 64 : (u + 1) * 64, k * LANES : (k + 1) * LANES] for u in range(2)], axis=1
            )
            for k in range(BASES)
        ],
        axis=0,
    )
    mixed = jnp.dot(weight_ref[...], stacked, preferred_element_type=F32)
    out_ref[0] = mixed[:, : out_ref.shape[2]]


def disco(field, disco_reach, disco_taps, disco_weight):
    lat_rows, channels, lon_cols = field.shape
    core = lax.axis_index("core")
    even_row = lax.axis_index("x") % 2 == 0
    head, tail = field[:, :, :HMAX], field[:, :, lon_cols - HMAX :]
    lon = ("y", "zh", "core")
    near_pairs = [(i, i ^ 1) for i in range(16)]
    far_pairs = [(i, (i + 1) % 16 if i % 2 else (i - 1) % 16) for i in range(16)]
    near = lax.ppermute(jnp.where(core == 0, tail, head), lon, near_pairs)
    far = lax.ppermute(jnp.where(core == 0, head, tail), lon, far_pairs)
    left = jnp.where(core == 0, far, near)
    right = jnp.where(core == 0, near, far)
    blank = jnp.zeros((lat_rows, channels, 256 - lon_cols - 2 * HMAX), BF16)
    wide = jnp.concatenate([left, field, right, blank], axis=2)
    lat = ("zl", "x")
    even_pairs = [(i, i ^ 1) for i in range(32)]
    odd_pairs = [(i, i + 1 if i % 2 else i - 1) for i in range(1, 31)]
    first, last = wide[:1], wide[lat_rows - 1 :]
    one = lax.ppermute(jnp.where(even_row, last, first), lat, even_pairs)
    two = lax.ppermute(jnp.where(even_row, first, last), lat, odd_pairs)
    extended = jnp.concatenate(
        [jnp.where(even_row, two, one), wide, jnp.where(even_row, one, two)], axis=0
    )
    offsets = jnp.abs(jnp.arange(TAPS, dtype=jnp.int32) - HMAX)
    within = offsets[None, :] <= disco_reach[:, None]
    coef = jnp.where(
        within[:, None, :], disco_taps.reshape(lat_rows, BASES * 3, TAPS), 0.0
    )
    base = jnp.concatenate(
        [
            coef[:, :, :1],
            jnp.zeros((lat_rows, BASES * 3, LANES - TAPS), F32),
            coef[:, :, :0:-1],
        ],
        axis=2,
    )
    weight = disco_weight.transpose(2, 0, 1).reshape(channels, BASES * channels)
    return pl.pallas_call(
        toeplitz_kernel,
        grid=(lat_rows,),
        in_specs=[
            pl.BlockSpec(extended.shape, lambda i: (0, 0, 0)),
            pl.BlockSpec((1, BASES * 3, LANES), lambda i: (i, 0, 0)),
            pl.BlockSpec(weight.shape, lambda i: (0, 0)),
        ],
        out_specs=pl.BlockSpec((1, channels, lon_cols), lambda i: (i, 0, 0)),
        out_shape=jax.ShapeDtypeStruct((lat_rows, channels, lon_cols), F32),
        scratch_shapes=[pltpu.VMEM((768, BASES * LANES), BF16)],
        cost_estimate=pl.CostEstimate(
            flops=2 * lat_rows * 128 * 768 * 512, bytes_accessed=2**21, transcendentals=0
        ),
    )(extended, base, weight)


def exchange(cells, axes):
    return lax.all_to_all(cells, axes, split_axis=0, concat_axis=0, tiled=True)


def per_device(grid_field, disco_reach, disco_taps, disco_weight, legendre, mixing):
    lat_rows, lon_cols, channels = grid_field.shape
    wide = 2 * channels
    lon_place = lax.axis_index(("y", "zh", "core"))
    forward, inverse = tables(lon_cols)
    forward = lax.dynamic_index_in_dim(jnp.asarray(forward), lon_place, 0, keepdims=False)
    inverse = lax.dynamic_index_in_dim(jnp.asarray(inverse), lon_place, 0, keepdims=False)

    degrees = jnp.arange(legendre.shape[2], dtype=jnp.int32)
    orders = lon_place * 2 + jnp.arange(2, dtype=jnp.int32)
    masked = jnp.where(degrees[None, None, :] >= orders[None, :, None], legendre, jnp.zeros((), BF16))
    own = mixing.shape[0]
    masked = masked.reshape(lat_rows, 2, 8, 4, own).transpose(3, 1, 0, 2, 4)
    masked = masked.reshape(4, 1, 2, lat_rows, 8 * own)
    masked = jnp.broadcast_to(masked, (4, 2, 2, lat_rows, 8 * own)).reshape(8, 2, lat_rows, 8 * own)
    leg = exchange(masked, ("x", "zh")).reshape(4, 4, lat_rows, 8 * own)

    waves = jnp.einsum(
        "ijc,gqpj->gqipc",
        grid_field,
        forward.reshape(8, 4, 2, lon_cols),
        preferred_element_type=F32,
    ).astype(BF16)
    waves = waves.reshape(1, 8, 4 * lat_rows, wide)
    waves = jnp.broadcast_to(waves, (4, 8, 4 * lat_rows, wide)).reshape(32, 4 * lat_rows, wide)
    waves = exchange(waves, PLANE).reshape(4, 8, 4, lat_rows, wide)
    spectra = waves.astype(F32).sum(axis=1).astype(BF16)
    coeffs = jnp.einsum("xqil,xqiv->qlv", leg, spectra, preferred_element_type=F32).astype(BF16)
    coeffs = coeffs.reshape(2, 2, 8, own, wide).transpose(0, 2, 1, 3, 4).reshape(16, 2 * own, wide)
    coeffs = exchange(coeffs, LINE).astype(F32).sum(axis=0).astype(BF16).reshape(2, own, wide)
    real, imag = mixing[:, 0], mixing[:, 1]
    block = jnp.concatenate(
        [jnp.concatenate([real, imag], axis=2), jnp.concatenate([-imag, real], axis=2)], axis=1
    )
    mixed = jnp.einsum("qlv,lvw->qlw", coeffs, block, preferred_element_type=F32).astype(BF16)
    mixed = jnp.broadcast_to(mixed.reshape(1, 2 * own, wide), (16, 2 * own, wide))
    mixed = exchange(mixed, LINE).reshape(2, 8, 2, own, wide).transpose(0, 2, 1, 3, 4)
    mixed = mixed.reshape(4, 8 * own, wide)
    modes = jnp.einsum("xqil,qlv->xqiv", leg, mixed, preferred_element_type=F32).astype(BF16)
    modes = modes.reshape(4, 1, 4 * lat_rows, wide)
    modes = jnp.broadcast_to(modes, (4, 8, 4 * lat_rows, wide)).reshape(32, 4 * lat_rows, wide)
    modes = exchange(modes, PLANE).reshape(4, 8, 4, lat_rows, 2, channels)
    modes = modes.astype(F32).sum(axis=0).astype(BF16)
    spectral_out = jnp.einsum(
        "gqipc,gqpj->icj",
        modes,
        inverse.reshape(8, 4, 2, lon_cols),
        preferred_element_type=F32,
    ).astype(BF16)
    field = grid_field.transpose(0, 2, 1)
    disco_out = disco(field, disco_reach, disco_taps, disco_weight)
    combined = spectral_out.astype(F32) + disco_out
    out = (field.astype(F32) + jax.nn.gelu(combined, approximate=True)).astype(BF16)
    return out.transpose(0, 2, 1)


def solution(mesh):
    fine = Mesh(mesh.devices.reshape(8, 4, 4, 2, 2), ("zl", "x", "y", "zh", "core"))
    lat, lon = ("zl", "x"), ("y", "zh", "core")
    in_specs = (
        P(lat, lon, None),
        P(lat),
        P(lat, None),
        P(),
        P(lat, lon, None),
        P(lat, None, None, None),
    )
    return jax.shard_map(
        per_device, mesh=fine, in_specs=in_specs, out_specs=P(lat, lon, None), check_vma=False
    )
```

time: 839 us -> 140 us (0.17)
  waiting for transfers between devices: 385 us -> 43.7 us
  blocking collectives: 181 us -> 0 us
  other arithmetic: 133 us -> 7.7 us
  local copies, waits for them, and re-layouts: 53.6 us -> 8.11 us
  between operations: 16.6 us -> 0.35 us
  Pallas kernels: 0 us -> 11.4 us
  starting transfers between devices: 54.1 us -> 64.4 us
    unnamed x2 -> x0, waiting for transfers between devices: 385 us -> none
    all_gather x2 -> x0, blocking collectives: 181 us -> none  [the longest x1 107 us: per_device(): portion = lax.all_gather(mixed_modes, 'lat', axis=0, tiled=True)]
    another operation x6 -> x0, other arithmetic: 131 us -> none
    all_to_all x2 -> x5, waiting for transfers between devices: 0.01 us -> 43.7 us  [exchange(): return lax.all_to_all(cells, axes, split_axis=0, concat_axis=0, tiled=True)]
    slice x28 -> x1, local copies, waits for them, and re-layouts: 40.2 us -> 0.09 us  [disco(): coef[:, :, :0:-1]]
    pallas_call x0 -> x1, Pallas kernels: none -> 11.4 us  [disco(): pl.pallas_call(toeplitz_kernel, grid=(lat_rows,), in_specs=[pl.BlockSpec(...]
    all_to_all x2 -> x5, starting transfers between devices: 35.1 us -> 46 us  [exchange(): return lax.all_to_all(cells, axes, split_axis=0, concat_axis=0, tiled=True)]
  transfers between devices with their start and end apart: 7 -> 9, of which waited for: 1 -> 3; matrix products, arithmetic and copies ran while one was open for 22% -> 7% of each run, Pallas kernels for 0% -> 8%
where the time goes in v1:
time: 140 us; the launch traced here: 139 us
  starting transfers between devices  64.4 us (46%)
  waiting for transfers between devices  43.7 us (31%)
  Pallas kernels  11.4 us (8%)
  local copies, waits for them, and re-layouts  8.11 us (6%)
  other arithmetic  7.7 us (6%)
  matrix products  2.78 us (2%)
    all_to_all x5, starting transfers between devices, exchange(): return lax.all_to_all(cells, axes, split_axis=0, concat_axis=0, tiled=True)  46 us
    all_to_all x5, waiting for transfers between devices, exchange(): return lax.all_to_all(cells, axes, split_axis=0, concat_axis=0, tiled=True)  43.7 us
    ppermute x1, starting transfers between devices, disco(): far = lax.ppermute(jnp.where(core == 0, head, tail), lon, far_pairs)  12.7 us
    pallas_call x1, Pallas kernels, disco(): pl.pallas_call(toeplitz_kernel, grid=(lat_rows,), in_specs=[pl.BlockSpec(...  11.4 us
  transfers between devices with their start and end apart: 9, of which 3 were waited for; matrix products, arithmetic and copies ran while one was open for 7% of the time, Pallas kernels for 8%

profile of v1, /device:TPU:1, one launch (start us, length us, event | category | flops | bytes accessed | tf_op | source)
XLA Modules:
  0.0 138.6 jit_solution(1216401180038362873)
XLA Ops:
  0.0 0.8 constant_dynamic-slice_fusion.1
  0.8 1.4 %fusion.3 = bf16[8,4,16,2,64]{4,0,2,3,1:T(8,128)(2,1)S(1)} fusion(bf16[16,180,64]{1,2,0:T(8,128)(2,1)} %param.8, bf16[8,4,2,180,1]{3,2,1,0,4:T(2,128)(2,1)S(1)} %bitcast.97), kind=kOutput, calls=%fused_computation.7 | convolution fusion | flops 23658496 | bytes 522752 | tf_op jit(solution)/shard_map/ijc,gqpj->gqipc/dot_general | solution.py:157
  2.6 0.9 broadcast_in_dim.68
  3.6 10.4 %all-to-all-start.1 = ((bf16[32,64,128]{2,1,0:T(8,128)(2,1)}), bf16[32,64,128]{2,1,0:T(8,128)(2,1)S(1)}, u32[]{:S(2)}, u32[]{:S(2)}) async-start(bf16[32,64,128]{2,1,0:T(8,128)(2,1)} %bitcast.11), calls=%async_computation.1 | async-start | bytes 1048576 | tf_op jit(solution)/shard_map/all_to_all | solution.py:137
  14.2 0.4 reshape.113
  14.8 11.0 %all-to-all-done.1 = bf16[32,64,128]{2,1,0:T(8,128)(2,1)S(1)} async-done(((bf16[32,64,128]{2,1,0:T(8,128)(2,1)}), bf16[32,64,128]{2,1,0:T(8,128)(2,1)S(1)}, u32[]{:S(2)}, u32[]{:S(2)}) %all-to-all-start.1) | async-done | bytes 524320 | tf_op jit(solution)/shard_map/all_to_all | solution.py:137
  25.7 0.7 broadcast_in_dim.66
  26.4 13.7 %all-to-all-start = ((bf16[8,2,16,192]{3,2,1,0:T(8,128)(2,1)}), bf16[8,2,16,192]{3,2,1,0:T(8,128)(2,1)S(1)}, u32[]{:S(2)}, u32[]{:S(2)}) async-start(bf16[8,2,16,192]{3,2,1,0:T(8,128)(2,1)} %bitcast.4), calls=%async_computation | async-start | bytes 262144 | tf_op jit(solution)/shard_map/all_to_all | solution.py:137
  40.1 0.9 broadcast_select_fusion.3
  41.0 12.7 %collective-permute-start = (bf16[16,64,20]{2,1,0:T(8,128)(2,1)}, bf16[16,64,20]{2,1,0:T(8,128)(2,1)S(1)}, u32[]{:S(2)}, u32[]{:S(2)}) collective-permute-start(bf16[16,64,20]{2,1,0:T(8,128)(2,1)} %get-tuple-element.12), channel_id=1, source_target_pairs={{0,15},{1,2},{2,1},{3,4},{4,3},{5,6},{6,5},{7,8},{8,7},{9,10},{10,... | collective-permute-start | bytes 122888 | tf_op jit(solution)/shard_map/ppermute | solution.py:91
  53.7 2.3 %collective-permute-start.1 = (bf16[16,64,20]{2,1,0:T(8,128)(2,1)}, bf16[16,64,20]{2,1,0:T(8,128)(2,1)}, u32[]{:S(2)}, u32[]{:S(2)}) collective-permute-start(bf16[16,64,20]{2,1,0:T(8,128)(2,1)} %get-tuple-element.13), channel_id=1, source_target_pairs={{0,1},{1,0},{2,3},{3,2},{4,5},{5,4},{6,7},{7,6},{8,9},{9,8},{10,11... | collective-permute-start | bytes 122888 | tf_op jit(solution)/shard_map/ppermute | solution.py:90
  56.5 0.7 copy.45
  57.2 4.9 %all-to-all-start.2 = ((bf16[16,48,128]{2,1,0:T(8,128)(2,1)}), bf16[16,48,128]{2,1,0:T(8,128)(2,1)S(1)}, u32[]{:S(2)}, u32[]{:S(2)}) async-start(bf16[16,48,128]{2,1,0:T(8,128)(2,1)} %bitcast.16), calls=%async_computation.2 | async-start | bytes 393216 | tf_op jit(solution)/shard_map/all_to_all | solution.py:137
  62.7 25.7 %all-to-all-done.2 = bf16[16,48,128]{2,1,0:T(8,128)(2,1)S(1)} async-done(((bf16[16,48,128]{2,1,0:T(8,128)(2,1)}), bf16[16,48,128]{2,1,0:T(8,128)(2,1)S(1)}, u32[]{:S(2)}, u32[]{:S(2)}) %all-to-all-start.2) | async-done | bytes 196640 | tf_op jit(solution)/shard_map/all_to_all | solution.py:137
  88.4 0.5 fusion.5
  89.0 0.7 broadcast_in_dim.70
  89.7 5.0 %all-to-all-start.3 = ((bf16[16,48,128]{2,1,0:T(8,128)(2,1)}), bf16[16,48,128]{2,1,0:T(8,128)(2,1)S(1)}, u32[]{:S(2)}, u32[]{:S(2)}) async-start(bf16[16,48,128]{2,1,0:T(8,128)(2,1)} %broadcast_in_dim.70), calls=%async_computation.3 | async-start | bytes 393216 | tf_op jit(solution)/shard_map/all_to_all | solution.py:137
  94.7 0.8 pad_maximum_fusion.1.base_ref
  95.4 1.0 broadcast_select_fusion.1
  96.6 2.7 %collective-permute-start.3 = (bf16[1,64,256]{2,1,0:T(8,128)(2,1)S(1)}, bf16[1,64,256]{2,1,0:T(8,128)(2,1)S(1)}, u32[]{:S(2)}, u32[]{:S(2)}) collective-permute-start(bf16[1,64,256]{2,1,0:T(8,128)(2,1)S(1)} %broadcast_select_fusion.8), channel_id=1, source_target_pairs={{0,16},{16,0},{32,48},{48,32},{64,80},{80,64},{96,112},{112,96},{1... | collective-permute-start | bytes 98312 | tf_op jit(solution)/shard_map/ppermute | solution.py:100
  99.3 0.7 collective-permute-start.2
  100.0 7.0 %all-to-all-done.3 = bf16[16,48,128]{2,1,0:T(8,128)(2,1)S(1)} async-done(((bf16[16,48,128]{2,1,0:T(8,128)(2,1)}), bf16[16,48,128]{2,1,0:T(8,128)(2,1)S(1)}, u32[]{:S(2)}, u32[]{:S(2)}) %all-to-all-start.3) | async-done | bytes 196640 | tf_op jit(solution)/shard_map/all_to_all | solution.py:137
  107.3 0.9 broadcast_in_dim.72
  108.2 12.1 %all-to-all-start.4 = ((bf16[32,64,128]{2,1,0:T(8,128)(2,1)}), bf16[32,64,128]{2,1,0:T(8,128)(2,1)S(1)}, u32[]{:S(2)}, u32[]{:S(2)}) async-start(bf16[32,64,128]{2,1,0:T(8,128)(2,1)} %bitcast.27), calls=%async_computation.4 | async-start | bytes 1048576 | tf_op jit(solution)/shard_map/all_to_all | solution.py:137
  120.3 0.8 constant_dynamic-slice_fusion
  121.1 0.7 copy.61.weight_ref
  121.8 1.3 pad_maximum_fusion.ext_ref
  123.1 11.4 %shard_map.82 = f32[16,64,180]{2,1,0:T(8,128)} custom-call(bf16[18,64,256]{2,1,0:T(8,128)(2,1)} %pad_maximum_fusion.ext_ref, f32[16,12,128]{2,1,0:T(8,128)} %pad_maximum_fusion.1.base_ref, bf16[64,256]{1,0:T(8,128)(2,1)} %copy.61.weight_ref), custom_call_target="tpu_custom_call" | custom-call | flops 1610612736 | bytes 2097152 | tf_op jit(solution)/shard_map/pallas_call | solution.py:119
  134.5 0.4 reshape.125
  134.9 2.0 %reduce_sum.38 = bf16[8,4,16,2,64]{4,3,2,1,0:T(2,128)(2,1)S(1)} reduce(bf16[4,8,4,16,2,64]{5,4,3,2,1,0:T(2,128)(2,1)S(1)} %reshape.125, bf16[]{:T(256)} %constant.51.clone.1), dimensions={0}, to_apply=%region_2.3 | reduce | flops 196608 | bytes 655362 | tf_op jit(solution)/shard_map/reduce_sum | solution.py:182
  136.9 0.4 fusion.1
  137.3 1.2 fusion.23
  (48 shorter events, 2.2 us)
Async XLA Ops:
  2.5 11.6 %copy-start.4 = (bf16[16,2,768]{2,1,0:T(2,128)(2,1)S(1)}, bf16[16,2,768]{2,1,0:T(2,128)(2,1)}, u32[]{:S(2)}) copy-start(bf16[16,2,768]{2,1,0:T(2,128)(2,1)} %param.12) | copy-start | bytes 147460
  3.6 22.2 %all-to-all-start.1 = ((bf16[32,64,128]{2,1,0:T(8,128)(2,1)}), bf16[32,64,128]{2,1,0:T(8,128)(2,1)S(1)}, u32[]{:S(2)}, u32[]{:S(2)}) async-start(bf16[32,64,128]{2,1,0:T(8,128)(2,1)} %bitcast.11), calls=%async_computation.1 | async-start | bytes 1048576 | tf_op jit(solution)/shard_map/all_to_all | solution.py:137
  14.0 26.1 %copy-start = (bf16[16,180,64]{1,2,0:T(8,128)(2,1)S(1)}, bf16[16,180,64]{1,2,0:T(8,128)(2,1)}, u32[]{:S(2)}) copy-start(bf16[16,180,64]{1,2,0:T(8,128)(2,1)} %param.8) | copy-start | bytes 1105924
  26.4 29.8 %all-to-all-start = ((bf16[8,2,16,192]{3,2,1,0:T(8,128)(2,1)}), bf16[8,2,16,192]{3,2,1,0:T(8,128)(2,1)S(1)}, u32[]{:S(2)}, u32[]{:S(2)}) async-start(bf16[8,2,16,192]{3,2,1,0:T(8,128)(2,1)} %bitcast.4), calls=%async_computation | async-start | bytes 262144 | tf_op jit(solution)/shard_map/all_to_all | solution.py:137
  41.0 21.0 %copy-start.6 = (s32[16]{0:T(128)S(1)}, s32[16]{0:T(128)}, u32[]{:S(2)}) copy-start(s32[16]{0:T(128)} %param.9) | copy-start | bytes 196
  41.0 21.1 %copy-start.5 = (f32[16,492]{1,0:T(8,128)S(1)}, f32[16,492]{1,0:T(8,128)}, u32[]{:S(2)}) copy-start(f32[16,492]{1,0:T(8,128)} %param.10) | copy-start | bytes 94468
  41.0 54.4 %collective-permute-start = (bf16[16,64,20]{2,1,0:T(8,128)(2,1)}, bf16[16,64,20]{2,1,0:T(8,128)(2,1)S(1)}, u32[]{:S(2)}, u32[]{:S(2)}) collective-permute-start(bf16[16,64,20]{2,1,0:T(8,128)(2,1)} %get-tuple-element.12), channel_id=1, source_target_pairs={{0,15},{1,2},{2,1},{3,4},{4,3},{5,6},{6,5},{7,8},{8,7},{9,10},{10,... | collective-permute-start | bytes 122888 | tf_op jit(solution)/shard_map/ppermute | solution.py:91
  53.7 41.7 %collective-permute-start.1 = (bf16[16,64,20]{2,1,0:T(8,128)(2,1)}, bf16[16,64,20]{2,1,0:T(8,128)(2,1)}, u32[]{:S(2)}, u32[]{:S(2)}) collective-permute-start(bf16[16,64,20]{2,1,0:T(8,128)(2,1)} %get-tuple-element.13), channel_id=1, source_target_pairs={{0,1},{1,0},{2,3},{3,2},{4,5},{5,4},{6,7},{7,6},{8,9},{9,8},{10,11... | collective-permute-start | bytes 122888 | tf_op jit(solution)/shard_map/ppermute | solution.py:90
  56.2 6.4 %copy-start.1 = (bf16[24,2,64,64]{3,2,1,0:T(8,128)(2,1)S(1)}, bf16[24,2,64,64]{3,2,1,0:T(8,128)(2,1)}, u32[]{:S(2)}) copy-start(bf16[24,2,64,64]{3,2,1,0:T(8,128)(2,1)} %param.13) | copy-start | bytes 1179652
  57.2 31.2 %all-to-all-start.2 = ((bf16[16,48,128]{2,1,0:T(8,128)(2,1)}), bf16[16,48,128]{2,1,0:T(8,128)(2,1)S(1)}, u32[]{:S(2)}, u32[]{:S(2)}) async-start(bf16[16,48,128]{2,1,0:T(8,128)(2,1)} %bitcast.16), calls=%async_computation.2 | async-start | bytes 393216 | tf_op jit(solution)/shard_map/all_to_all | solution.py:137
  89.7 17.3 %all-to-all-start.3 = ((bf16[16,48,128]{2,1,0:T(8,128)(2,1)}), bf16[16,48,128]{2,1,0:T(8,128)(2,1)S(1)}, u32[]{:S(2)}, u32[]{:S(2)}) async-start(bf16[16,48,128]{2,1,0:T(8,128)(2,1)} %broadcast_in_dim.70), calls=%async_computation.3 | async-start | bytes 393216 | tf_op jit(solution)/shard_map/all_to_all | solution.py:137
  96.6 25.2 %collective-permute-start.3 = (bf16[1,64,256]{2,1,0:T(8,128)(2,1)S(1)}, bf16[1,64,256]{2,1,0:T(8,128)(2,1)S(1)}, u32[]{:S(2)}, u32[]{:S(2)}) collective-permute-start(bf16[1,64,256]{2,1,0:T(8,128)(2,1)S(1)} %broadcast_select_fusion.8), channel_id=1, source_target_pairs={{0,16},{16,0},{32,48},{48,32},{64,80},{80,64},{96,112},{112,96},{1... | collective-permute-start | bytes 98312 | tf_op jit(solution)/shard_map/ppermute | solution.py:100
  99.3 22.4 %collective-permute-start.2 = (bf16[1,64,256]{2,1,0:T(8,128)(2,1)S(1)}, bf16[1,64,256]{2,1,0:T(8,128)(2,1)S(1)}, u32[]{:S(2)}, u32[]{:S(2)}) collective-permute-start(bf16[1,64,256]{2,1,0:T(8,128)(2,1)S(1)} %get-tuple-element.5), channel_id=1, source_target_pairs={{16,32},{32,16},{48,64},{64,48},{80,96},{96,80},{112,128},{128,112... | collective-permute-start | bytes 98312 | tf_op jit(solution)/shard_map/ppermute | solution.py:101
  107.0 14.0 %copy-start.3 = (bf16[4,64,64]{2,1,0:T(8,128)(2,1)S(1)}, bf16[4,64,64]{2,1,0:T(8,128)(2,1)}, u32[]{:S(2)}) copy-start(bf16[4,64,64]{2,1,0:T(8,128)(2,1)} %param.11) | copy-start | bytes 98308
  108.2 26.3 %all-to-all-start.4 = ((bf16[32,64,128]{2,1,0:T(8,128)(2,1)}), bf16[32,64,128]{2,1,0:T(8,128)(2,1)S(1)}, u32[]{:S(2)}, u32[]{:S(2)}) async-start(bf16[32,64,128]{2,1,0:T(8,128)(2,1)} %bitcast.27), calls=%async_computation.4 | async-start | bytes 1048576 | tf_op jit(solution)/shard_map/all_to_all | solution.py:137
  134.9 2.4 %copy-start.2 = (f32[16,64,180]{2,1,0:T(8,128)S(1)}, f32[16,64,180]{2,1,0:T(8,128)}, u32[]{:S(2)}) copy-start(f32[16,64,180]{2,1,0:T(8,128)} %shard_map.82) | copy-start | bytes 2211844

commit v2 on v1

v2 whole, which is shorter than its diff:
```python
import math

import jax
import jax.numpy as jnp
import numpy as np
from jax import lax
from jax.experimental import pallas as pl
from jax.experimental.pallas import tpu as pltpu
from jax.sharding import Mesh
from jax.sharding import PartitionSpec as P

NLON = 2880
MODES = 32
HMAX = 20
TAPS = 2 * HMAX + 1
BASES = 4
LANES = 128
BF16 = jnp.bfloat16
F32 = jnp.float32
LON = ("y", "zh", "core")


def table(lon_cols, scale):
    residues = (np.arange(MODES)[:, None] * np.arange(NLON)[None, :]) % NLON
    phases = residues.astype(np.float32) * np.float32(2.0 * math.pi / NLON)
    waves = np.stack([np.cos(phases), -np.sin(phases)], axis=0).astype(np.float32)
    waves = waves.reshape(2 * MODES, NLON // lon_cols, lon_cols).transpose(1, 0, 2)
    return (waves * np.float32(scale)).astype(BF16)


def first_half(shape):
    return lax.broadcasted_iota(jnp.int32, shape, len(shape) - 1) < 64


def forward_kernel(field_ref, table_ref, out_ref, rows_ref):
    rows = field_ref.shape[0]
    field = field_ref[...].reshape(rows * 64, field_ref.shape[2])
    waves = lax.dot_general(
        table_ref[...], field, (((1,), (1,)), ((), ())), preferred_element_type=F32
    )
    half = first_half((MODES, LANES))
    for m in range(rows // 2):
        re = waves[:MODES, m * LANES : (m + 1) * LANES]
        im = waves[MODES:, m * LANES : (m + 1) * LANES]
        rows_ref[pl.ds(2 * m, MODES, stride=rows), :] = jnp.where(half, re, pltpu.roll(im, 64, 1))
        rows_ref[pl.ds(2 * m + 1, MODES, stride=rows), :] = jnp.where(
            half, pltpu.roll(re, 64, 1), im
        )
    out_ref[...] = rows_ref[...].astype(BF16).reshape(out_ref.shape)


def spectra_kernel(waves_ref, leg_ref, out_ref):
    total = waves_ref[0].astype(F32)
    for n in range(1, waves_ref.shape[0]):
        total += waves_ref[n].astype(F32)
    spectra = total.astype(BF16)
    for x in range(4):
        out_ref[x, :, :LANES] = spectra
        out_ref[x, :, LANES:] = leg_ref[x]


def analysis_kernel(got_ref, coeff_ref, leg_ref):
    parts = []
    for q in range(2):
        pieces = [got_ref[x, q * 16 : (q + 1) * 16, :] for x in range(4)]
        both = jnp.concatenate(pieces, axis=0)
        leg_ref[q] = both[:, LANES:]
        parts.append(
            lax.dot_general(
                both[:, LANES:],
                both[:, :LANES],
                (((0,), (0,)), ((), ())),
                preferred_element_type=F32,
            )
        )
    for n in range(8):
        rows = jnp.concatenate([p[n * 24 : (n + 1) * 24] for p in parts], axis=0)
        coeff_ref[n] = rows.astype(BF16)


def mixing_kernel(coeff_ref, weight_ref, out_ref):
    total = coeff_ref[0].astype(F32)
    for n in range(1, coeff_ref.shape[0]):
        total += coeff_ref[n].astype(F32)
    lhs = jnp.concatenate([total[:, :64], total[:, 64:]], axis=0).astype(BF16)
    degree = lax.broadcasted_iota(jnp.int32, (96, LANES), 0) % 24
    acc = jnp.zeros((96, LANES), F32)
    for l in range(24):
        acc = jnp.where(
            degree == l, jnp.dot(lhs, weight_ref[l], preferred_element_type=F32), acc
        )
    turned = pltpu.roll(acc[48:], 64, 1)
    mixed = acc[:48] + jnp.where(first_half((48, LANES)), -turned, turned)
    mixed = mixed.astype(BF16)
    for n in range(out_ref.shape[0]):
        out_ref[n] = mixed


def synthesis_kernel(mixed_ref, leg_ref, out_ref):
    blocks = [mixed_ref[n].astype(F32) for n in range(8)]
    for q in range(2):
        mixed = jnp.concatenate([v[q * 24 : (q + 1) * 24] for v in blocks], axis=0)
        modes = jnp.dot(
            leg_ref[q][:, :192], mixed.astype(BF16), preferred_element_type=F32
        ).astype(BF16)
        for x in range(4):
            out_ref[x, q * 16 : (q + 1) * 16, :] = modes[x * 16 : (x + 1) * 16]


def modes_kernel(parts_ref, out_ref):
    total = parts_ref[0].astype(F32)
    for n in range(1, parts_ref.shape[0]):
        total += parts_ref[n].astype(F32)
    modes = total.astype(BF16)
    for n in range(out_ref.shape[0]):
        out_ref[n] = modes


def final_kernel(modes_ref, table_ref, disco_ref, field_ref, out_ref, rows_ref):
    rows, channels, cols = field_ref.shape
    for n in range(16):
        rows_ref[n * 32 : (n + 1) * 32, :] = modes_ref[n].astype(F32)
    half = first_half((MODES, LANES))
    for m in range(rows // 2):
        one = rows_ref[pl.ds(2 * m, MODES, stride=rows), :]
        two = rows_ref[pl.ds(2 * m + 1, MODES, stride=rows), :]
        re = jnp.where(half, one, pltpu.roll(two, 64, 1))
        im = jnp.where(half, pltpu.roll(one, 64, 1), two)
        spectral = lax.dot_general(
            jnp.concatenate([re, im], axis=0).astype(BF16),
            table_ref[...],
            (((0,), (0,)), ((), ())),
            preferred_element_type=F32,
        ).astype(BF16)
        for u in range(2):
            v = spectral[u * 64 : (u + 1) * 64].astype(F32) + disco_ref[2 * m + u]
            inner = math.sqrt(2.0 / math.pi) * (v + 0.044715 * (v * v * v))
            act = 0.5 * v * (1.0 + jnp.tanh(inner))
            out_ref[2 * m + u] = (field_ref[2 * m + u].astype(F32) + act).astype(BF16)


def call(kernel, out, *args, scratch=(), flops=10**7, smem=0):
    nbytes = sum(a.size * a.dtype.itemsize for a in args)
    vmem = pl.BlockSpec(memory_space=pltpu.VMEM)
    scalar = pl.BlockSpec(memory_space=pltpu.SMEM)
    return pl.pallas_call(
        kernel,
        out_shape=out,
        in_specs=[scalar] * smem + [vmem] * (len(args) - smem),
        out_specs=jax.tree.map(lambda _: vmem, out),
        scratch_shapes=scratch,
        compiler_params=pltpu.CompilerParams(vmem_limit_bytes=16 * 2**20),
        cost_estimate=pl.CostEstimate(flops=flops, bytes_accessed=nbytes, transcendentals=0),
    )(*args)


def struct(dtype, *shape):
    return jax.ShapeDtypeStruct(shape, dtype)


def halves(row):
    v = row.astype(F32)
    blank = jnp.zeros((v.shape[0], 2 * LANES - v.shape[1]), F32)
    return v[:, :LANES], jnp.concatenate([v[:, LANES:], blank], axis=1)


def edges_kernel(core_ref, field_ref, near_ref, far_ref):
    rows, channels, cols = field_ref.shape
    lane = lax.broadcasted_iota(jnp.int32, (channels, LANES), 1)
    first = core_ref[0] == 0
    for g in range(3):
        head = jnp.zeros((channels, LANES), F32)
        tail = jnp.zeros((channels, LANES), F32)
        for m in range(min(6, rows - 6 * g)):
            low, high = halves(field_ref[g * 6 + m])
            inside = (lane >= HMAX * m) & (lane < HMAX * (m + 1))
            low = pltpu.roll(low, HMAX * m, 1) if m else low
            high = pltpu.roll(high, (HMAX * m - (cols - HMAX - LANES)) % LANES, 1)
            head = jnp.where(inside, low, head)
            tail = jnp.where(inside, high, tail)
        near_ref[g] = jnp.where(first, tail, head).astype(BF16)
        far_ref[g] = jnp.where(first, head, tail).astype(BF16)


def widened(row, left, right, m):
    cols = row.shape[1]
    edge = HMAX + cols - LANES
    lane = lax.broadcasted_iota(jnp.int32, left.shape, 1)
    low, high = (pltpu.roll(v, HMAX, 1) for v in halves(row))
    before = pltpu.roll(left, (-HMAX * m) % LANES, 1) if m else left
    after = pltpu.roll(right, (edge - HMAX * m) % LANES, 1)
    one = jnp.where(lane < HMAX, before, low)
    two = jnp.where(lane < HMAX, low, high)
    return one, jnp.where(lane < edge, two, jnp.where(lane < edge + HMAX, after, 0.0))


def sides(core_ref, near, far):
    near, far = near.astype(F32), far.astype(F32)
    first = core_ref[0] == 0
    return jnp.where(first, far, near), jnp.where(first, near, far)


def rows_kernel(core_ref, even_ref, field_ref, near_ref, far_ref, one_ref, two_ref):
    rows = field_ref.shape[0]
    ends = []
    for r in (0, rows - 1):
        left, right = sides(core_ref, near_ref[r // 6], far_ref[r // 6])
        ends.append(jnp.concatenate(widened(field_ref[r], left, right, r % 6), axis=1))
    even = even_ref[0] == 1
    one_ref[0] = jnp.where(even, ends[1], ends[0]).astype(BF16)
    two_ref[0] = jnp.where(even, ends[0], ends[1]).astype(BF16)


def toeplitz_kernel(
    core_ref, even_ref, field_ref, near_ref, far_ref, one_ref, two_ref, base_ref, weight_ref,
    out_ref, ext_ref, rest_ref, band_ref,
):
    rows, channels, cols = field_ref.shape
    lane = lax.broadcasted_iota(jnp.int32, (channels, LANES), 1)
    even = even_ref[0] == 1
    for r in range(rows + 2):
        if r in (0, rows + 1):
            a, b = (one_ref, two_ref) if r else (two_ref, one_ref)
            row = jnp.where(even, a[0].astype(F32), b[0].astype(F32))
            one, two = row[:, :LANES], row[:, LANES:]
        else:
            g, m = divmod(r - 1, 6)
            left, right = sides(core_ref, near_ref[g], far_ref[g])
            one, two = widened(field_ref[r - 1], left, right, m)
        ext_ref[r, :, :LANES] = one.astype(BF16)
        ext_ref[r, :, LANES:] = two.astype(BF16)
        for a in range(3):
            i = r - a
            if 0 <= i < rows:
                part = pltpu.roll(two, 2 * HMAX * a, 1) if a else two
                inside = (lane >= 2 * HMAX * a) & (lane < 2 * HMAX * (a + 1))
                rest_ref[i] = jnp.where(inside, part, rest_ref[i] if a else 0.0)

    r = lax.broadcasted_iota(jnp.int32, (LANES, LANES), 0)
    s = lax.broadcasted_iota(jnp.int32, (LANES, LANES), 1)

    @pl.loop(0, rows)
    def _(row):
        for k in range(BASES):
            cols_k = slice(k * LANES, (k + 1) * LANES)
            spill = []
            for a in range(3):
                line = base_ref[row, k * 3 + a : k * 3 + a + 1, :]
                circ = pltpu.roll(
                    jnp.broadcast_to(line, (LANES, LANES)), 0, 1, stride=1, stride_axis=0
                )
                band_ref[a * LANES : (a + 1) * LANES, cols_k] = jnp.where(s <= r, circ, 0.0).astype(
                    BF16
                )
                spill.append(jnp.where(s > r, circ, 0.0)[: 2 * HMAX])
            spill.append(jnp.zeros((LANES - 6 * HMAX, LANES), F32))
            band_ref[3 * LANES :, cols_k] = jnp.concatenate(spill, axis=0).astype(BF16)
        lines = [ext_ref[row + a] for a in range(3)]
        upper = [v[:, :LANES] for v in lines] + [rest_ref[row].astype(BF16)]
        lower = [v[:, LANES:] for v in lines] + [jnp.zeros((channels, LANES), BF16)]
        lhs = jnp.concatenate(
            [jnp.concatenate(upper, axis=1), jnp.concatenate(lower, axis=1)], axis=0
        )
        sums = jnp.dot(lhs, band_ref[...], preferred_element_type=F32).astype(BF16)
        stacked = jnp.concatenate(
            [
                jnp.concatenate(
                    [
                        sums[u * channels : (u + 1) * channels, k * LANES : (k + 1) * LANES]
                        for u in range(2)
                    ],
                    axis=1,
                )
                for k in range(BASES)
            ],
            axis=0,
        )
        mixed = jnp.dot(weight_ref[...], stacked, preferred_element_type=F32)
        out_ref[row] = mixed[:, :cols]


def halo(field):
    channels = field.shape[1]
    core = lax.axis_index("core").reshape(1)
    even = (1 - lax.axis_index("x") % 2).reshape(1)
    near_pairs = [(i, i ^ 1) for i in range(16)]
    far_pairs = [(i, (i + 1) % 16 if i % 2 else (i - 1) % 16) for i in range(16)]
    lat = ("zl", "x")
    even_pairs = [(i, i ^ 1) for i in range(32)]
    odd_pairs = [(i, i + 1 if i % 2 else i - 1) for i in range(1, 31)]
    packed = struct(BF16, 3, channels, LANES)
    near, far = call(edges_kernel, (packed, packed), core, field, smem=1)
    far = lax.ppermute(far, LON, far_pairs)
    near, far = lax.optimization_barrier((near, far))
    near = lax.ppermute(near, LON, near_pairs)
    row = struct(BF16, 1, channels, 2 * LANES)
    one, two = call(rows_kernel, (row, row), core, even, field, near, far, smem=2)
    one = lax.ppermute(one, lat, even_pairs)
    two = lax.ppermute(two, lat, odd_pairs)
    return core, even, near, far, one, two


def disco(field, around, disco_reach, disco_taps, disco_weight):
    lat_rows, channels, lon_cols = field.shape
    core, even, near, far, one, two = around
    offsets = jnp.abs(jnp.arange(TAPS, dtype=jnp.int32) - HMAX)
    within = offsets[None, :] <= disco_reach[:, None]
    coef = jnp.where(
        within[:, None, :], disco_taps.reshape(lat_rows, BASES * 3, TAPS), 0.0
    )
    base = jnp.concatenate(
        [
            coef[:, :, :1],
            jnp.zeros((lat_rows, BASES * 3, LANES - TAPS), F32),
            coef[:, :, :0:-1],
        ],
        axis=2,
    )
    weight = disco_weight.transpose(2, 0, 1).reshape(channels, BASES * channels)
    return call(
        toeplitz_kernel,
        struct(F32, lat_rows, channels, lon_cols),
        core,
        even,
        field,
        near,
        far,
        one,
        two,
        base,
        weight,
        smem=2,
        flops=2 * lat_rows * 128 * 512 * 512,
        scratch=[
            pltpu.VMEM((lat_rows + 2, channels, 2 * LANES), BF16),
            pltpu.VMEM((lat_rows, channels, LANES), F32),
            pltpu.VMEM((4 * LANES, BASES * LANES), BF16),
        ],
    )


def exchange(cells, axes):
    return lax.all_to_all(cells, axes, split_axis=0, concat_axis=0, tiled=True)


def per_device(grid_field, disco_reach, disco_taps, disco_weight, legendre, mixing):
    lat_rows, lon_cols, channels = grid_field.shape
    wide = 2 * channels
    own = mixing.shape[0]
    place = lax.axis_index(LON)
    field = grid_field.transpose(0, 2, 1)
    forward = jnp.asarray(table(lon_cols, 1.0 / math.sqrt(NLON)))
    forward = lax.dynamic_index_in_dim(forward, place, 0, keepdims=False)
    inverse = jnp.asarray(table(lon_cols, 1.0 / math.sqrt(MODES)))
    inverse = lax.dynamic_index_in_dim(inverse, place, 0, keepdims=False)
    spread = [pltpu.VMEM((MODES * lat_rows, wide), F32)]

    waves = call(
        forward_kernel, struct(BF16, 16, 2 * lat_rows, wide), field, forward, scratch=spread
    )
    degrees = jnp.arange(legendre.shape[2], dtype=jnp.int32)
    orders = place * 2 + jnp.arange(2, dtype=jnp.int32)
    masked = jnp.where(degrees[None, None, :] >= orders[None, :, None], legendre, jnp.zeros((), BF16))
    masked = masked.reshape(lat_rows, 2, 8, 4, own).transpose(3, 1, 0, 2, 4)
    masked = masked.reshape(4, 2 * lat_rows, 8 * own)
    masked = jnp.pad(masked, ((0, 0), (0, 0), (0, 256 - 8 * own)))
    weight = jnp.concatenate([mixing[:, 0], mixing[:, 1]], axis=2)

    core, even, near, far, one, two = halo(field)
    waves = exchange(waves, LON)
    message = call(spectra_kernel, struct(BF16, 4, 2 * lat_rows, 384), waves, masked)
    message = exchange(message, ("x",))
    message, near = lax.optimization_barrier((message, near))
    coeffs, leg = call(
        analysis_kernel,
        (struct(BF16, 8, 2 * own, wide), struct(BF16, 2, 4 * lat_rows, 256)),
        message,
    )
    coeffs = exchange(coeffs, ("zl",))
    mixed = call(mixing_kernel, struct(BF16, 8, 2 * own, wide), coeffs, weight)
    mixed = exchange(mixed, ("zl",))
    mixed, one, two = lax.optimization_barrier((mixed, one, two))
    parts = call(synthesis_kernel, struct(BF16, 4, 2 * lat_rows, wide), mixed, leg)
    parts = exchange(parts, ("x",))
    modes = call(modes_kernel, struct(BF16, 16, 2 * lat_rows, wide), parts)
    modes = exchange(modes, LON)
    disco_out = disco(field, (core, even, near, far, one, two), disco_reach, disco_taps, disco_weight)
    out = call(
        final_kernel,
        struct(BF16, lat_rows, channels, lon_cols),
        modes,
        inverse,
        disco_out,
        field,
        scratch=spread,
    )
    return out.transpose(0, 2, 1)


def solution(mesh):
    fine = Mesh(mesh.devices.reshape(8, 4, 4, 2, 2), ("zl", "x", "y", "zh", "core"))
    lat, lon = ("zl", "x"), LON
    in_specs = (
        P(lat, lon, None),
        P(lat),
        P(lat, None),
        P(),
        P(lat, lon, None),
        P(lat, None, None, None),
    )
    return jax.shard_map(
        per_device, mesh=fine, in_specs=in_specs, out_specs=P(lat, lon, None), check_vma=False
    )
```

time: 140 us -> 121 us (0.86)
  waiting for transfers between devices: 43.7 us -> 26.4 us
  other arithmetic: 7.7 us -> 0.54 us
  starting transfers between devices: 64.4 us -> 71 us
  Pallas kernels: 11.4 us -> 16.6 us
  local copies, waits for them, and re-layouts: 8.11 us -> 4.5 us
  matrix products: 2.78 us -> 0 us
    all_to_all x5 -> x6, waiting for transfers between devices: 43.7 us -> 25 us  [exchange(): return lax.all_to_all(cells, axes, split_axis=0, concat_axis=0, tiled=True)]
    all_to_all x5 -> x6, starting transfers between devices: 46 us -> 51.6 us  [exchange(): return lax.all_to_all(cells, axes, split_axis=0, concat_axis=0, tiled=True)]
    pallas_call x1 -> x10, Pallas kernels: 11.4 us -> 16.6 us  [call(): pl.pallas_call(kernel, out_shape=out, in_specs=[scalar] * smem + [vmem] *...]
    broadcast_in_dim x7 -> x0, local copies, waits for them, and re-layouts: 3.58 us -> none  [the longest x2 1.06 us: per_device(): jnp.broadcast_to(waves, (4, 8, 4 * lat_rows, wide))]
    dot_general x5 -> x0, matrix products: 2.78 us -> none  [the longest x1 1.41 us: per_device(): jnp.einsum('ijc,gqpj->gqipc', grid_field, forward.reshape(8, 4, 2, lon_co...]
    reduce_sum x3 -> x0, other arithmetic: 2.1 us -> none  [the longest x1 1.98 us: per_device(): modes = modes.astype(F32).sum(axis=0).astype(BF16)]
    select_n x5 -> x0, other arithmetic: 2.04 us -> none  [the longest x1 0.99 us: disco(): left = jnp.where(core == 0, far, near)]
    unnamed x14, local copies, waits for them, and re-layouts: 0.04 us -> 1.87 us
  transfers between devices with their start and end apart: 9 -> 10, of which waited for: 3 -> 8; matrix products, arithmetic and copies ran while one was open for 7% -> 2% of each run, Pallas kernels for 8% -> 9%
where the time goes in v2:
time: 121 us; the launch traced here: 119 us
  starting transfers between devices  71 us (59%)
  waiting for transfers between devices  26.4 us (22%)
  Pallas kernels  16.6 us (14%)
  local copies, waits for them, and re-layouts  4.5 us (4%)
    all_to_all x6, starting transfers between devices, exchange(): return lax.all_to_all(cells, axes, split_axis=0, concat_axis=0, tiled=True)  51.6 us
    all_to_all x6, waiting for transfers between devices, exchange(): return lax.all_to_all(cells, axes, split_axis=0, concat_axis=0, tiled=True)  25 us
    pallas_call x10, Pallas kernels, call(): pl.pallas_call(kernel, out_shape=out, in_specs=[scalar] * smem + [vmem] *...  16.6 us
    ppermute x1, starting transfers between devices, halo(): far = lax.ppermute(far, LON, far_pairs)  12.3 us
    ppermute x1, starting transfers between devices, halo(): one = lax.ppermute(one, lat, even_pairs)  3.64 us
    ppermute x1, starting transfers between devices, halo(): near = lax.ppermute(near, LON, near_pairs)  2.84 us
  transfers between devices with their start and end apart: 10, of which 8 were waited for; matrix products, arithmetic and copies ran while one was open for 2% of the time, Pallas kernels for 9%

profile of v2, /device:TPU:1, one launch (start us, length us, event | category | flops | bytes accessed | tf_op | source)
XLA Modules:
  0.0 119.3 jit_solution(11906305955515965675)
XLA Ops:
  0.0 0.8 dynamic-slice_bitcast_fusion.1.table_ref
  0.8 1.0 copy-done
  1.8 1.0 shard_map.82
  2.8 19.2 %all-to-all-start = ((bf16[16,32,128]{2,1,0:T(8,128)(2,1)}), bf16[16,32,128]{2,1,0:T(8,128)(2,1)S(1)}, u32[]{:S(2)}, u32[]{:S(2)}) async-start(bf16[16,32,128]{2,1,0:T(8,128)(2,1)} %shard_map.82), calls=%async_computation | async-start | bytes 262144 | tf_op jit(solution)/shard_map/all_to_all | solution.py:343
  22.3 12.3 %collective-permute-start = (bf16[3,64,128]{2,1,0:T(8,128)(2,1)S(1)}, bf16[3,64,128]{2,1,0:T(8,128)(2,1)S(1)}, u32[]{:S(2)}, u32[]{:S(2)}) collective-permute-start(bf16[3,64,128]{2,1,0:T(8,128)(2,1)S(1)} %get-tuple-element.19), channel_id=1, source_target_pairs={{0,15},{1,2},{2,1},{3,4},{4,3},{5,6},{6,5},{7,8},{8,7},{9,10},{10,... | collective-permute-start | bytes 147464 | tf_op jit(solution)/shard_map/ppermute | solution.py:293
  34.7 0.4 reshape.73
  35.3 1.9 %all-to-all-done.waves_ref = bf16[16,32,128]{2,1,0:T(8,128)(2,1)S(1)} async-done(((bf16[16,32,128]{2,1,0:T(8,128)(2,1)}), bf16[16,32,128]{2,1,0:T(8,128)(2,1)S(1)}, u32[]{:S(2)}, u32[]{:S(2)}) %all-to-all-start) | async-done | bytes 131104 | tf_op jit(solution)/shard_map/all_to_all | solution.py:343
  37.3 0.7 shard_map.83
  37.9 4.0 %all-to-all-start.1 = ((bf16[4,32,384]{2,1,0:T(8,128)(2,1)}), bf16[4,32,384]{2,1,0:T(8,128)(2,1)S(1)}, u32[]{:S(2)}, u32[]{:S(2)}) async-start(bf16[4,32,384]{2,1,0:T(8,128)(2,1)} %shard_map.83), calls=%async_computation.1 | async-start | bytes 196608 | tf_op jit(solution)/shard_map/all_to_all | solution.py:343
  41.9 2.8 %collective-permute-start.1 = (bf16[3,64,128]{2,1,0:T(8,128)(2,1)S(1)}, bf16[3,64,128]{2,1,0:T(8,128)(2,1)S(1)}, u32[]{:S(2)}, u32[]{:S(2)}) collective-permute-start(bf16[3,64,128]{2,1,0:T(8,128)(2,1)S(1)} %get-tuple-element.20), channel_id=1, source_target_pairs={{0,1},{1,0},{2,3},{3,2},{4,5},{5,4},{6,7},{7,6},{8,9},{9,8},{10,11... | collective-permute-start | bytes 147464 | tf_op jit(solution)/shard_map/ppermute | solution.py:295
  44.8 0.9 collective-permute-done.1.near_ref
  45.6 0.9 all-to-all-done.1.got_ref
  46.6 0.8 shard_map.85
  47.4 10.8 %all-to-all-start.2 = ((bf16[8,48,128]{2,1,0:T(8,128)(2,1)}), bf16[8,48,128]{2,1,0:T(8,128)(2,1)S(1)}, u32[]{:S(2)}, u32[]{:S(2)}) async-start(bf16[8,48,128]{2,1,0:T(8,128)(2,1)} %get-tuple-element.22), calls=%async_computation.2 | async-start | bytes 196608 | tf_op jit(solution)/shard_map/all_to_all | solution.py:343
  58.3 0.2 pad_maximum_fusion.weight_ref
  58.5 9.7 %all-to-all-done.2.coeff_ref = bf16[8,48,128]{2,1,0:T(8,128)(2,1)S(1)} async-done(((bf16[8,48,128]{2,1,0:T(8,128)(2,1)}), bf16[8,48,128]{2,1,0:T(8,128)(2,1)S(1)}, u32[]{:S(2)}, u32[]{:S(2)}) %all-to-all-start.2) | async-done | bytes 98336 | tf_op jit(solution)/shard_map/all_to_all | solution.py:343
  68.2 1.1 shard_map.86
  69.3 3.4 %all-to-all-start.3 = ((bf16[8,48,128]{2,1,0:T(8,128)(2,1)}), bf16[8,48,128]{2,1,0:T(8,128)(2,1)S(1)}, u32[]{:S(2)}, u32[]{:S(2)}) async-start(bf16[8,48,128]{2,1,0:T(8,128)(2,1)} %shard_map.86), calls=%async_computation.3 | async-start | bytes 196608 | tf_op jit(solution)/shard_map/all_to_all | solution.py:343
  72.8 3.6 %collective-permute-start.2 = (bf16[1,64,256]{2,1,0:T(8,128)(2,1)S(1)}, bf16[1,64,256]{2,1,0:T(8,128)(2,1)S(1)}, u32[]{:S(2)}, u32[]{:S(2)}) collective-permute-start(bf16[1,64,256]{2,1,0:T(8,128)(2,1)S(1)} %get-tuple-element.24), channel_id=1, source_target_pairs={{0,16},{16,0},{32,48},{48,32},{64,80},{80,64},{96,112},{112,96},{1... | collective-permute-start | bytes 98312 | tf_op jit(solution)/shard_map/ppermute | solution.py:298
  76.5 0.7 collective-permute-start.3
  77.2 0.6 collective-permute-done.2.one_ref
  77.8 4.9 %all-to-all-done.3.mixed_ref = bf16[8,48,128]{2,1,0:T(8,128)(2,1)S(1)} async-done(((bf16[8,48,128]{2,1,0:T(8,128)(2,1)}), bf16[8,48,128]{2,1,0:T(8,128)(2,1)S(1)}, u32[]{:S(2)}, u32[]{:S(2)}) %all-to-all-start.3) | async-done | bytes 98336 | tf_op jit(solution)/shard_map/all_to_all | solution.py:343
  82.6 0.8 shard_map.88
  83.4 6.0 %all-to-all-start.4 = ((bf16[4,32,128]{2,1,0:T(8,128)(2,1)}), bf16[4,32,128]{2,1,0:T(8,128)(2,1)S(1)}, u32[]{:S(2)}, u32[]{:S(2)}) async-start(bf16[4,32,128]{2,1,0:T(8,128)(2,1)} %shard_map.88), calls=%async_computation.4 | async-start | bytes 65536 | tf_op jit(solution)/shard_map/all_to_all | solution.py:343
  89.6 4.1 %all-to-all-done.4.parts_ref = bf16[4,32,128]{2,1,0:T(8,128)(2,1)S(1)} async-done(((bf16[4,32,128]{2,1,0:T(8,128)(2,1)}), bf16[4,32,128]{2,1,0:T(8,128)(2,1)S(1)}, u32[]{:S(2)}, u32[]{:S(2)}) %all-to-all-start.4) | async-done | bytes 32800 | tf_op jit(solution)/shard_map/all_to_all | solution.py:343
  93.8 0.7 shard_map.89
  94.4 8.2 %all-to-all-start.5 = ((bf16[16,32,128]{2,1,0:T(8,128)(2,1)}), bf16[16,32,128]{2,1,0:T(8,128)(2,1)S(1)}, u32[]{:S(2)}, u32[]{:S(2)}) async-start(bf16[16,32,128]{2,1,0:T(8,128)(2,1)} %shard_map.89), calls=%async_computation.5 | async-start | bytes 262144 | tf_op jit(solution)/shard_map/all_to_all | solution.py:343
  102.7 0.8 copy-done.3
  103.9 0.8 dynamic-slice_bitcast_fusion.table_ref
  104.7 9.6 %shard_map.90.disco_ref = f32[16,64,180]{2,1,0:T(8,128)S(1)} custom-call(s32[1]{0:T(128)} %bitcast.3.core_ref, s32[1]{0:T(128)} %bitcast.6.even_ref, bf16[16,64,180]{2,1,0:T(8,128)(2,1)S(1)} %bitcast.28, bf16[3,64,128]{2,1,0:T(8,128)(2,1)S(1)} %collective-permute-done.1.near_ref, bf16[3,64,128]{2,1,0:T(8,128)(2,1)S(1)} %collective-permute-done.far_ref, ...), custom_call_target="tpu_custom_call" | custom-call | flops 1073741824 | bytes 663560 | tf_op jit(solution)/shard_map/pallas_call | solution.py:146
  114.3 3.4 %all-to-all-done.5.modes_ref = bf16[16,32,128]{2,1,0:T(8,128)(2,1)S(1)} async-done(((bf16[16,32,128]{2,1,0:T(8,128)(2,1)}), bf16[16,32,128]{2,1,0:T(8,128)(2,1)S(1)}, u32[]{:S(2)}, u32[]{:S(2)}) %all-to-all-start.5) | async-done | bytes 131104 | tf_op jit(solution)/shard_map/all_to_all | solution.py:343
  117.8 1.6 %shard_map.91 = bf16[16,64,180]{2,1,0:T(8,128)(2,1)} custom-call(bf16[16,32,128]{2,1,0:T(8,128)(2,1)S(1)} %all-to-all-done.5.modes_ref, bf16[64,180]{1,0:T(8,128)(2,1)S(1)} %dynamic-slice_bitcast_fusion.table_ref, f32[16,64,180]{2,1,0:T(8,128)S(1)} %shard_map.90.disco_ref, bf16[16,64,180]{2,1,0:T(8,128)(2,1)S(1)} %bitcast.29), custom_call_target="tpu_custom_call" | custom-call | flops 10000000 | bytes 1260032 | tf_op jit(solution)/shard_map/pallas_call | solution.py:146
  (33 shorter events, 1.4 us)
Async XLA Ops:
  0.8 1.0 copy-start
  1.8 20.3 %copy-start.1 = (bf16[16,180,64]{1,2,0:T(8,128)(2,1)S(1)}, bf16[16,180,64]{1,2,0:T(8,128)(2,1)}, u32[]{:S(2)}) copy-start(bf16[16,180,64]{1,2,0:T(8,128)(2,1)} %param.8) | copy-start | bytes 1105924
  2.8 34.4 %all-to-all-start = ((bf16[16,32,128]{2,1,0:T(8,128)(2,1)}), bf16[16,32,128]{2,1,0:T(8,128)(2,1)S(1)}, u32[]{:S(2)}, u32[]{:S(2)}) async-start(bf16[16,32,128]{2,1,0:T(8,128)(2,1)} %shard_map.82), calls=%async_computation | async-start | bytes 262144 | tf_op jit(solution)/shard_map/all_to_all | solution.py:343
  22.1 12.6 %copy-start.4 = (bf16[16,2,768]{2,1,0:T(2,128)(2,1)S(1)}, bf16[16,2,768]{2,1,0:T(2,128)(2,1)}, u32[]{:S(2)}) copy-start(bf16[16,2,768]{2,1,0:T(2,128)(2,1)} %param.12) | copy-start | bytes 147460
  22.3 19.6 %collective-permute-start = (bf16[3,64,128]{2,1,0:T(8,128)(2,1)S(1)}, bf16[3,64,128]{2,1,0:T(8,128)(2,1)S(1)}, u32[]{:S(2)}, u32[]{:S(2)}) collective-permute-start(bf16[3,64,128]{2,1,0:T(8,128)(2,1)S(1)} %get-tuple-element.19), channel_id=1, source_target_pairs={{0,15},{1,2},{2,1},{3,4},{4,3},{5,6},{6,5},{7,8},{8,7},{9,10},{10,... | collective-permute-start | bytes 147464 | tf_op jit(solution)/shard_map/ppermute | solution.py:293
  35.1 23.1 %copy-start.2 = (bf16[24,2,64,64]{3,2,1,0:T(8,128)(2,1)S(1)}, bf16[24,2,64,64]{3,2,1,0:T(8,128)(2,1)}, u32[]{:S(2)}) copy-start(bf16[24,2,64,64]{3,2,1,0:T(8,128)(2,1)} %param.13) | copy-start | bytes 1179652
  37.9 8.7 %all-to-all-start.1 = ((bf16[4,32,384]{2,1,0:T(8,128)(2,1)}), bf16[4,32,384]{2,1,0:T(8,128)(2,1)S(1)}, u32[]{:S(2)}, u32[]{:S(2)}) async-start(bf16[4,32,384]{2,1,0:T(8,128)(2,1)} %shard_map.83), calls=%async_computation.1 | async-start | bytes 196608 | tf_op jit(solution)/shard_map/all_to_all | solution.py:343
  41.9 3.7 %collective-permute-start.1 = (bf16[3,64,128]{2,1,0:T(8,128)(2,1)S(1)}, bf16[3,64,128]{2,1,0:T(8,128)(2,1)S(1)}, u32[]{:S(2)}, u32[]{:S(2)}) collective-permute-start(bf16[3,64,128]{2,1,0:T(8,128)(2,1)S(1)} %get-tuple-element.20), channel_id=1, source_target_pairs={{0,1},{1,0},{2,3},{3,2},{4,5},{5,4},{6,7},{7,6},{8,9},{9,8},{10,11... | collective-permute-start | bytes 147464 | tf_op jit(solution)/shard_map/ppermute | solution.py:295
  47.4 20.8 %all-to-all-start.2 = ((bf16[8,48,128]{2,1,0:T(8,128)(2,1)}), bf16[8,48,128]{2,1,0:T(8,128)(2,1)S(1)}, u32[]{:S(2)}, u32[]{:S(2)}) async-start(bf16[8,48,128]{2,1,0:T(8,128)(2,1)} %get-tuple-element.22), calls=%async_computation.2 | async-start | bytes 196608 | tf_op jit(solution)/shard_map/all_to_all | solution.py:343
  69.3 13.3 %all-to-all-start.3 = ((bf16[8,48,128]{2,1,0:T(8,128)(2,1)}), bf16[8,48,128]{2,1,0:T(8,128)(2,1)S(1)}, u32[]{:S(2)}, u32[]{:S(2)}) async-start(bf16[8,48,128]{2,1,0:T(8,128)(2,1)} %shard_map.86), calls=%async_computation.3 | async-start | bytes 196608 | tf_op jit(solution)/shard_map/all_to_all | solution.py:343
  72.8 4.9 %collective-permute-start.2 = (bf16[1,64,256]{2,1,0:T(8,128)(2,1)S(1)}, bf16[1,64,256]{2,1,0:T(8,128)(2,1)S(1)}, u32[]{:S(2)}, u32[]{:S(2)}) collective-permute-start(bf16[1,64,256]{2,1,0:T(8,128)(2,1)S(1)} %get-tuple-element.24), channel_id=1, source_target_pairs={{0,16},{16,0},{32,48},{48,32},{64,80},{80,64},{96,112},{112,96},{1... | collective-permute-start | bytes 98312 | tf_op jit(solution)/shard_map/ppermute | solution.py:298
  76.5 1.3 %collective-permute-start.3 = (bf16[1,64,256]{2,1,0:T(8,128)(2,1)S(1)}, bf16[1,64,256]{2,1,0:T(8,128)(2,1)S(1)}, u32[]{:S(2)}, u32[]{:S(2)}) collective-permute-start(bf16[1,64,256]{2,1,0:T(8,128)(2,1)S(1)} %get-tuple-element.25), channel_id=1, source_target_pairs={{16,32},{32,16},{48,64},{64,48},{80,96},{96,80},{112,128},{128,112... | collective-permute-start | bytes 98312 | tf_op jit(solution)/shard_map/ppermute | solution.py:299
  83.4 6.0 %copy-start.6 = (s32[16]{0:T(128)S(1)}, s32[16]{0:T(128)}, u32[]{:S(2)}) copy-start(s32[16]{0:T(128)} %param.9) | copy-start | bytes 196
  83.4 6.1 %copy-start.5 = (f32[16,492]{1,0:T(8,128)S(1)}, f32[16,492]{1,0:T(8,128)}, u32[]{:S(2)}) copy-start(f32[16,492]{1,0:T(8,128)} %param.10) | copy-start | bytes 94468
  83.4 10.3 %all-to-all-start.4 = ((bf16[4,32,128]{2,1,0:T(8,128)(2,1)}), bf16[4,32,128]{2,1,0:T(8,128)(2,1)S(1)}, u32[]{:S(2)}, u32[]{:S(2)}) async-start(bf16[4,32,128]{2,1,0:T(8,128)(2,1)} %shard_map.88), calls=%async_computation.4 | async-start | bytes 65536 | tf_op jit(solution)/shard_map/all_to_all | solution.py:343
  94.4 23.3 %all-to-all-start.5 = ((bf16[16,32,128]{2,1,0:T(8,128)(2,1)}), bf16[16,32,128]{2,1,0:T(8,128)(2,1)S(1)}, u32[]{:S(2)}, u32[]{:S(2)}) async-start(bf16[16,32,128]{2,1,0:T(8,128)(2,1)} %shard_map.89), calls=%async_computation.5 | async-start | bytes 262144 | tf_op jit(solution)/shard_map/all_to_all | solution.py:343
  102.6 0.8 copy-start.3

commit v3 on v2

--- a/solution.py
+++ b/solution.py
@@ -20,12 +20,37 @@
 LON = ("y", "zh", "core")
 
 
+def pair_of(sector):
+    return (sector + 15) % 16 // 2
+
+
+def member(pair, m):
+    return (2 * pair + 1 + m) % 16
+
+
+def orders_at(zh):
+    out = []
+    for group in range(8):
+        pair = pair_of(group // 2 * 4 + zh * 2 + group % 2)
+        out += [member(pair, m) * 2 + odd for m in range(2) for odd in range(2)]
+    return np.array(out)
+
+
 def table(lon_cols, scale):
-    residues = (np.arange(MODES)[:, None] * np.arange(NLON)[None, :]) % NLON
-    phases = residues.astype(np.float32) * np.float32(2.0 * math.pi / NLON)
-    waves = np.stack([np.cos(phases), -np.sin(phases)], axis=0).astype(np.float32)
-    waves = waves.reshape(2 * MODES, NLON // lon_cols, lon_cols).transpose(1, 0, 2)
-    return (waves * np.float32(scale)).astype(BF16)
+    sectors = []
+    for sector in range(NLON // lon_cols):
+        columns = sector * lon_cols + np.arange(lon_cols)
+        residues = (orders_at(sector // 2 % 2)[:, None] * columns[None, :]) % NLON
+        phases = residues.astype(np.float32) * np.float32(2.0 * math.pi / NLON)
+        sectors.append(np.concatenate([np.cos(phases), -np.sin(phases)], axis=0))
+    return (np.stack(sectors).astype(np.float32) * np.float32(scale)).astype(BF16)
+
+
+def degree_order():
+    out = np.zeros((768, 256), np.float32)
+    for o in range(192):
+        out[o // 24 * 96 + o % 24, o] = 1.0
+    return out.astype(BF16)
 
 
 def first_half(shape):
@@ -49,33 +74,58 @@
     out_ref[...] = rows_ref[...].astype(BF16).reshape(out_ref.shape)
 
 
-def spectra_kernel(waves_ref, leg_ref, out_ref):
+def spectra_kernel(waves_ref, legs_ref, out_ref):
     total = waves_ref[0].astype(F32)
     for n in range(1, waves_ref.shape[0]):
         total += waves_ref[n].astype(F32)
     spectra = total.astype(BF16)
     for x in range(4):
         out_ref[x, :, :LANES] = spectra
-        out_ref[x, :, LANES:] = leg_ref[x]
+        out_ref[x, :, LANES:] = legs_ref[x]
+
+
+def legs_kernel(orders_ref, own_ref, other_ref, pick_ref, out_ref, lines_ref):
+    row = lax.broadcasted_iota(jnp.int32, (32, LANES), 0)
+    degree = lax.broadcasted_iota(jnp.int32, (32, LANES), 1)
+    sides = []
+    for side, ref in enumerate((own_ref, other_ref)):
+        tiles = [ref[3 + n, t * 32 : (t + 1) * 32, :].astype(F32) for n in range(3) for t in range(2)]
+        tiles[0] = jnp.where(degree >= orders_ref[side] + row % 2, tiles[0], 0.0)
+        sides.append(jnp.concatenate(tiles, axis=1))
+    lines = jnp.concatenate(sides, axis=0)
+    turned = [lines] + [pltpu.roll(lines, 768 - 24 * x, 1) for x in range(1, 4)]
+    turned = jnp.concatenate(turned, axis=0).astype(BF16)
+    picked = jnp.dot(turned, pick_ref[...], preferred_element_type=F32)
+    for t in range(2):
+        lines_ref[t] = picked[:, t * LANES : (t + 1) * LANES]
+    for side in range(2):
+        m = orders_ref[2] if side == 0 else 1 - orders_ref[2]
+        for q in range(2):
+            at = pl.multiple_of((m * 2 + q) * 16, 16)
+            for x in range(4):
+                for t in range(2):
+                    v = lines_ref[t, pl.ds(x * 64 + side * 32 + q, 16, stride=2), :]
+                    out_ref[x, pl.ds(at, 16), t * LANES : (t + 1) * LANES] = v.astype(BF16)
 
 
 def analysis_kernel(got_ref, coeff_ref, leg_ref):
-    parts = []
-    for q in range(2):
-        pieces = [got_ref[x, q * 16 : (q + 1) * 16, :] for x in range(4)]
-        both = jnp.concatenate(pieces, axis=0)
-        leg_ref[q] = both[:, LANES:]
-        parts.append(
-            lax.dot_general(
-                both[:, LANES:],
-                both[:, :LANES],
-                (((0,), (0,)), ((), ())),
-                preferred_element_type=F32,
+    for m in range(2):
+        parts = []
+        for q in range(2):
+            n = m * 2 + q
+            both = jnp.concatenate([got_ref[x, n * 16 : (n + 1) * 16, :] for x in range(4)], axis=0)
+            leg_ref[n] = both[:, LANES:]
+            parts.append(
+                lax.dot_general(
+                    both[:, LANES:],
+                    both[:, :LANES],
+                    (((0,), (0,)), ((), ())),
+                    preferred_element_type=F32,
+                )
             )
-        )
-    for n in range(8):
-        rows = jnp.concatenate([p[n * 24 : (n + 1) * 24] for p in parts], axis=0)
-        coeff_ref[n] = rows.astype(BF16)
+        for n in range(8):
+            rows = jnp.concatenate([p[n * 24 : (n + 1) * 24] for p in parts], axis=0)
+            coeff_ref[m * 8 + n] = rows.astype(BF16)
 
 
 def mixing_kernel(coeff_ref, weight_ref, out_ref):
@@ -97,29 +147,26 @@
 
 
 def synthesis_kernel(mixed_ref, leg_ref, out_ref):
-    blocks = [mixed_ref[n].astype(F32) for n in range(8)]
-    for q in range(2):
-        mixed = jnp.concatenate([v[q * 24 : (q + 1) * 24] for v in blocks], axis=0)
-        modes = jnp.dot(
-            leg_ref[q][:, :192], mixed.astype(BF16), preferred_element_type=F32
-        ).astype(BF16)
-        for x in range(4):
-            out_ref[x, q * 16 : (q + 1) * 16, :] = modes[x * 16 : (x + 1) * 16]
-
-
-def modes_kernel(parts_ref, out_ref):
-    total = parts_ref[0].astype(F32)
-    for n in range(1, parts_ref.shape[0]):
-        total += parts_ref[n].astype(F32)
-    modes = total.astype(BF16)
-    for n in range(out_ref.shape[0]):
-        out_ref[n] = modes
+    for m in range(2):
+        blocks = [mixed_ref[m * 8 + n].astype(F32) for n in range(8)]
+        for q in range(2):
+            at = m * 2 + q
+            mixed = jnp.concatenate([v[q * 24 : (q + 1) * 24] for v in blocks], axis=0)
+            modes = jnp.dot(
+                leg_ref[at][:, :192], mixed.astype(BF16), preferred_element_type=F32
+            ).astype(BF16)
+            for x in range(4):
+                for g in range(8):
+                    out_ref[x * 8 + g, at * 16 : (at + 1) * 16, :] = modes[x * 16 : (x + 1) * 16]
 
 
 def final_kernel(modes_ref, table_ref, disco_ref, field_ref, out_ref, rows_ref):
     rows, channels, cols = field_ref.shape
-    for n in range(16):
-        rows_ref[n * 32 : (n + 1) * 32, :] = modes_ref[n].astype(F32)
+    for g in range(8):
+        total = modes_ref[g].astype(F32)
+        for x in range(1, 4):
+            total += modes_ref[x * 8 + g].astype(F32)
+        rows_ref[g * 64 : (g + 1) * 64, :] = total
     half = first_half((MODES, LANES))
     for m in range(rows // 2):
         one = rows_ref[pl.ds(2 * m, MODES, stride=rows), :]
@@ -164,7 +211,13 @@
     return v[:, :LANES], jnp.concatenate([v[:, LANES:], blank], axis=1)
 
 
-def edges_kernel(core_ref, field_ref, near_ref, far_ref):
+def edges_kernel(core_ref, field_ref, leg_ref, near_ref, far_ref, lines_ref):
+    for i in range(leg_ref.shape[0]):
+        lines_ref[2 * i : 2 * i + 2, :] = leg_ref[i].astype(F32)
+    for n in range(3):
+        for t in range(2):
+            at = (2 * n + t) * LANES
+            far_ref[3 + n, t * 32 : (t + 1) * 32, :] = lines_ref[:, at : at + LANES].astype(BF16)
     rows, channels, cols = field_ref.shape
     lane = lax.broadcasted_iota(jnp.int32, (channels, LANES), 1)
     first = core_ref[0] == 0
@@ -279,25 +332,13 @@
         out_ref[row] = mixed[:, :cols]
 
 
-def halo(field):
-    channels = field.shape[1]
-    core = lax.axis_index("core").reshape(1)
-    even = (1 - lax.axis_index("x") % 2).reshape(1)
-    near_pairs = [(i, i ^ 1) for i in range(16)]
-    far_pairs = [(i, (i + 1) % 16 if i % 2 else (i - 1) % 16) for i in range(16)]
+def lat_rows_of(field, scalars, near, far):
+    row = struct(BF16, 1, field.shape[1], 2 * LANES)
+    one, two = call(rows_kernel, (row, row), *scalars, field, near, far, smem=2)
     lat = ("zl", "x")
-    even_pairs = [(i, i ^ 1) for i in range(32)]
-    odd_pairs = [(i, i + 1 if i % 2 else i - 1) for i in range(1, 31)]
-    packed = struct(BF16, 3, channels, LANES)
-    near, far = call(edges_kernel, (packed, packed), core, field, smem=1)
-    far = lax.ppermute(far, LON, far_pairs)
-    near, far = lax.optimization_barrier((near, far))
-    near = lax.ppermute(near, LON, near_pairs)
-    row = struct(BF16, 1, channels, 2 * LANES)
-    one, two = call(rows_kernel, (row, row), core, even, field, near, far, smem=2)
-    one = lax.ppermute(one, lat, even_pairs)
-    two = lax.ppermute(two, lat, odd_pairs)
-    return core, even, near, far, one, two
+    one = lax.ppermute(one, lat, [(i, i ^ 1) for i in range(32)])
+    two = lax.ppermute(two, lat, [(i, i + 1 if i % 2 else i - 1) for i in range(1, 31)])
+    return one, two
 
 
 def disco(field, around, disco_reach, disco_taps, disco_weight):
@@ -343,6 +384,15 @@
     return lax.all_to_all(cells, axes, split_axis=0, concat_axis=0, tiled=True)
 
 
+def line_exchange(cells):
+    groups = [
+        [zl * 16 + member(pair, m) for m in range(2) for zl in range(8)] for pair in range(8)
+    ]
+    return lax.all_to_all(
+        cells, ("zl", *LON), split_axis=0, concat_axis=0, tiled=True, axis_index_groups=groups
+    )
+
+
 def per_device(grid_field, disco_reach, disco_taps, disco_weight, legendre, mixing):
     lat_rows, lon_cols, channels = grid_field.shape
     wide = 2 * channels
@@ -355,36 +405,64 @@
     inverse = lax.dynamic_index_in_dim(inverse, place, 0, keepdims=False)
     spread = [pltpu.VMEM((MODES * lat_rows, wide), F32)]
 
+    core = lax.axis_index("core").reshape(1)
+    even = (1 - lax.axis_index("x") % 2).reshape(1)
+    packed = struct(BF16, 3, channels, LANES)
+    near, mine = call(
+        edges_kernel,
+        (packed, struct(BF16, 6, channels, LANES)),
+        core,
+        field,
+        legendre,
+        smem=1,
+        scratch=[pltpu.VMEM((2 * lat_rows, 768), F32)],
+    )
+    swap = [(i, member(pair_of(i), i % 2)) for i in range(16)]
+    far = lax.ppermute(mine, LON, swap)
+    lines, mine = lax.optimization_barrier((field, mine))
     waves = call(
-        forward_kernel, struct(BF16, 16, 2 * lat_rows, wide), field, forward, scratch=spread
-    )
-    degrees = jnp.arange(legendre.shape[2], dtype=jnp.int32)
-    orders = place * 2 + jnp.arange(2, dtype=jnp.int32)
-    masked = jnp.where(degrees[None, None, :] >= orders[None, :, None], legendre, jnp.zeros((), BF16))
-    masked = masked.reshape(lat_rows, 2, 8, 4, own).transpose(3, 1, 0, 2, 4)
-    masked = masked.reshape(4, 2 * lat_rows, 8 * own)
-    masked = jnp.pad(masked, ((0, 0), (0, 0), (0, 256 - 8 * own)))
+        forward_kernel,
+        struct(BF16, 8, 4 * lat_rows, wide),
+        lines,
+        forward,
+        scratch=spread,
+        flops=10**7,
+    )
+    waves = exchange(waves, ("y", "core"))
+    waves, near = lax.optimization_barrier((waves, near))
+    pair = pair_of(place)
+    mate = 1 - core[0]
+    orders = jnp.stack([member(pair, mate) * 2, member(pair, 1 - mate) * 2, mate])
     weight = jnp.concatenate([mixing[:, 0], mixing[:, 1]], axis=2)
-
-    core, even, near, far, one, two = halo(field)
-    waves = exchange(waves, LON)
-    message = call(spectra_kernel, struct(BF16, 4, 2 * lat_rows, 384), waves, masked)
+    legs = call(
+        legs_kernel,
+        struct(BF16, 4, 4 * lat_rows, 256),
+        orders.astype(jnp.int32),
+        mine,
+        far,
+        jnp.asarray(degree_order()),
+        smem=1,
+        flops=10**7,
+        scratch=[pltpu.VMEM((2, 16 * lat_rows, LANES), F32)],
+    )
+    message = call(spectra_kernel, struct(BF16, 4, 4 * lat_rows, 384), waves, legs)
     message = exchange(message, ("x",))
+    near = lax.ppermute(near, LON, [(i, i ^ 1) for i in range(16)])
     message, near = lax.optimization_barrier((message, near))
     coeffs, leg = call(
         analysis_kernel,
-        (struct(BF16, 8, 2 * own, wide), struct(BF16, 2, 4 * lat_rows, 256)),
+        (struct(BF16, 16, 2 * own, wide), struct(BF16, 4, 4 * lat_rows, 256)),
         message,
     )
-    coeffs = exchange(coeffs, ("zl",))
-    mixed = call(mixing_kernel, struct(BF16, 8, 2 * own, wide), coeffs, weight)
-    mixed = exchange(mixed, ("zl",))
-    mixed, one, two = lax.optimization_barrier((mixed, one, two))
-    parts = call(synthesis_kernel, struct(BF16, 4, 2 * lat_rows, wide), mixed, leg)
-    parts = exchange(parts, ("x",))
-    modes = call(modes_kernel, struct(BF16, 16, 2 * lat_rows, wide), parts)
-    modes = exchange(modes, LON)
+    coeffs = line_exchange(coeffs)
+    one, two = lat_rows_of(field, (core, even), near, far)
+    coeffs, one, two = lax.optimization_barrier((coeffs, one, two))
+    mixed = call(mixing_kernel, struct(BF16, 16, 2 * own, wide), coeffs, weight)
+    mixed = line_exchange(mixed)
     disco_out = disco(field, (core, even, near, far, one, two), disco_reach, disco_taps, disco_weight)
+    mixed, disco_out = lax.optimization_barrier((mixed, disco_out))
+    modes = call(synthesis_kernel, struct(BF16, 32, 4 * lat_rows, wide), mixed, leg)
+    modes = exchange(modes, ("x", "y", "core"))
     out = call(
         final_kernel,
         struct(BF16, lat_rows, channels, lon_cols),

time: 121 us -> 113 us (0.934)
  starting transfers between devices: 71 us -> 61.5 us
  waiting for transfers between devices: 26.4 us -> 28.4 us
    all_to_all x6 -> x3, starting transfers between devices: 51.6 us -> 20 us  [exchange(): return lax.all_to_all(cells, axes, split_axis=0, concat_axis=0, tiled=True)]
    all_to_all x0 -> x2, starting transfers between devices: none -> 17.6 us  [line_exchange(): lax.all_to_all(cells, ('zl', *LON), split_axis=0, concat_axis=0, tiled=Tr...]
    all_to_all x0 -> x2, waiting for transfers between devices: none -> 10.2 us  [line_exchange(): lax.all_to_all(cells, ('zl', *LON), split_axis=0, concat_axis=0, tiled=Tr...]
    all_to_all x6 -> x3, waiting for transfers between devices: 25 us -> 16.5 us  [exchange(): return lax.all_to_all(cells, axes, split_axis=0, concat_axis=0, tiled=True)]
    ppermute x4, starting transfers between devices: 19.4 us -> 23.9 us  [the longest x1 16.8 us: per_device(): far = lax.ppermute(mine, LON, swap)]
    unnamed x14 -> x16, local copies, waits for them, and re-layouts: 1.87 us -> 2.6 us
  transfers between devices with their start and end apart: 10 -> 9, of which waited for: 8 -> 7; matrix products, arithmetic and copies ran while one was open for 2% -> 2% of each run, Pallas kernels for 9% -> 10%
where the time goes in v3:
time: 113 us
  starting transfers between devices  61.5 us (54%)
  waiting for transfers between devices  28.4 us (25%)
  Pallas kernels  17.2 us (15%)
  local copies, waits for them, and re-layouts  4.64 us (4%)
    all_to_all x3, starting transfers between devices, exchange(): return lax.all_to_all(cells, axes, split_axis=0, concat_axis=0, tiled=True)  20 us
    all_to_all x2, starting transfers between devices, line_exchange(): lax.all_to_all(cells, ('zl', *LON), split_axis=0, concat_axis=0, tiled=Tr...  17.6 us
    pallas_call x10, Pallas kernels, call(): pl.pallas_call(kernel, out_shape=out, in_specs=[scalar] * smem + [vmem] *...  17.2 us
    ppermute x1, starting transfers between devices, per_device(): far = lax.ppermute(mine, LON, swap)  16.8 us
    all_to_all x3, waiting for transfers between devices, exchange(): return lax.all_to_all(cells, axes, split_axis=0, concat_axis=0, tiled=True)  16.5 us
    all_to_all x2, waiting for transfers between devices, line_exchange(): lax.all_to_all(cells, ('zl', *LON), split_axis=0, concat_axis=0, tiled=Tr...  10.2 us
    ppermute x1, starting transfers between devices, lat_rows_of(): one = lax.ppermute(one, lat, [(i, i ^ 1) for i in range(32)])  3.37 us
    ppermute x1, starting transfers between devices, per_device(): near = lax.ppermute(near, LON, [(i, i ^ 1) for i in range(16)])  3.04 us
  transfers between devices with their start and end apart: 9, of which 7 were waited for; matrix products, arithmetic and copies ran while one was open for 2% of the time, Pallas kernels for 10%

profile of v3, /device:TPU:1, one launch (start us, length us, event | category | flops | bytes accessed | tf_op | source)
XLA Modules:
  0.0 112.5 jit_solution(11647630949618502688)
XLA Ops:
  0.0 1.0 copy-done
  1.0 0.8 copy-done.3
  1.8 0.2 shard_map.91
  2.1 16.8 %collective-permute-start = (bf16[6,64,128]{2,1,0:T(8,128)(2,1)S(1)}, bf16[6,64,128]{2,1,0:T(8,128)(2,1)S(1)}, u32[]{:S(2)}, u32[]{:S(2)}) collective-permute-start(bf16[6,64,128]{2,1,0:T(8,128)(2,1)S(1)} %get-tuple-element.26.own_ref), channel_id=1, source_target_pairs={{0,15},{1,2},{2,1},{3,4},{4,3},{5,6},{6,5},{7,8},{8,7},{9,10},{10,... | collective-permute-start | bytes 294920 | tf_op jit(solution)/shard_map/ppermute | solution.py:421
  18.9 0.8 dynamic-slice_bitcast_fusion.1.table_ref
  19.7 1.0 shard_map.92
  20.7 5.6 %all-to-all-start = ((bf16[8,64,128]{2,1,0:T(8,128)(2,1)}), bf16[8,64,128]{2,1,0:T(8,128)(2,1)S(1)}, u32[]{:S(2)}, u32[]{:S(2)}) async-start(bf16[8,64,128]{2,1,0:T(8,128)(2,1)} %shard_map.92), calls=%async_computation | async-start | bytes 262144 | tf_op jit(solution)/shard_map/all_to_all | solution.py:384
  26.4 0.9 shard_map.93.legs_ref
  27.3 4.3 %all-to-all-done.waves_ref = bf16[8,64,128]{2,1,0:T(8,128)(2,1)S(1)} async-done(((bf16[8,64,128]{2,1,0:T(8,128)(2,1)}), bf16[8,64,128]{2,1,0:T(8,128)(2,1)S(1)}, u32[]{:S(2)}, u32[]{:S(2)}) %all-to-all-start) | async-done | bytes 131104 | tf_op jit(solution)/shard_map/all_to_all | solution.py:384
  31.6 0.7 shard_map.94
  32.3 4.0 %all-to-all-start.1 = ((bf16[4,64,384]{2,1,0:T(8,128)(2,1)}), bf16[4,64,384]{2,1,0:T(8,128)(2,1)S(1)}, u32[]{:S(2)}, u32[]{:S(2)}) async-start(bf16[4,64,384]{2,1,0:T(8,128)(2,1)} %shard_map.94), calls=%async_computation.1 | async-start | bytes 393216 | tf_op jit(solution)/shard_map/all_to_all | solution.py:384
  36.3 3.0 %collective-permute-start.1 = (bf16[3,64,128]{2,1,0:T(8,128)(2,1)S(1)}, bf16[3,64,128]{2,1,0:T(8,128)(2,1)S(1)}, u32[]{:S(2)}, u32[]{:S(2)}) collective-permute-start(bf16[3,64,128]{2,1,0:T(8,128)(2,1)S(1)} %get-tuple-element.27), channel_id=1, source_target_pairs={{0,1},{1,0},{2,3},{3,2},{4,5},{5,4},{6,7},{7,6},{8,9},{9,8},{10,11... | collective-permute-start | bytes 147464 | tf_op jit(solution)/shard_map/ppermute | solution.py:450
  39.3 0.9 collective-permute-done.1.near_ref
  40.2 1.3 %all-to-all-done.1.got_ref = bf16[4,64,384]{2,1,0:T(8,128)(2,1)S(1)} async-done(((bf16[4,64,384]{2,1,0:T(8,128)(2,1)}), bf16[4,64,384]{2,1,0:T(8,128)(2,1)S(1)}, u32[]{:S(2)}, u32[]{:S(2)}) %all-to-all-start.1) | async-done | bytes 196640 | tf_op jit(solution)/shard_map/all_to_all | solution.py:384
  41.5 0.9 shard_map.95
  42.4 7.5 %all-to-all-start.2 = ((bf16[16,48,128]{2,1,0:T(8,128)(2,1)}), bf16[16,48,128]{2,1,0:T(8,128)(2,1)S(1)}, u32[]{:S(2)}, u32[]{:S(2)}) async-start(bf16[16,48,128]{2,1,0:T(8,128)(2,1)} %get-tuple-element.29), calls=%async_computation.2 | async-start | bytes 393216 | tf_op jit(solution)/shard_map/all_to_all | solution.py:391
  50.0 0.2 pad_maximum_fusion.weight_ref
  50.2 0.1 shard_map.96
  50.3 3.4 %collective-permute-start.2 = (bf16[1,64,256]{2,1,0:T(8,128)(2,1)S(1)}, bf16[1,64,256]{2,1,0:T(8,128)(2,1)S(1)}, u32[]{:S(2)}, u32[]{:S(2)}) collective-permute-start(bf16[1,64,256]{2,1,0:T(8,128)(2,1)S(1)} %get-tuple-element.31), channel_id=1, source_target_pairs={{0,16},{16,0},{32,48},{48,32},{64,80},{80,64},{96,112},{112,96},{1... | collective-permute-start | bytes 98312 | tf_op jit(solution)/shard_map/ppermute | solution.py:339
  53.7 0.7 collective-permute-start.3
  54.5 0.8 collective-permute-done.2.one_ref
  55.3 8.3 %all-to-all-done.2.coeff_ref = bf16[16,48,128]{2,1,0:T(8,128)(2,1)S(1)} async-done(((bf16[16,48,128]{2,1,0:T(8,128)(2,1)}), bf16[16,48,128]{2,1,0:T(8,128)(2,1)S(1)}, u32[]{:S(2)}, u32[]{:S(2)}) %all-to-all-start.2) | async-done | bytes 196640 | tf_op jit(solution)/shard_map/all_to_all | solution.py:391
  63.6 1.1 shard_map.97
  64.8 10.1 %all-to-all-start.3 = ((bf16[16,48,128]{2,1,0:T(8,128)(2,1)}), bf16[16,48,128]{2,1,0:T(8,128)(2,1)S(1)}, u32[]{:S(2)}, u32[]{:S(2)}) async-start(bf16[16,48,128]{2,1,0:T(8,128)(2,1)} %shard_map.97), calls=%async_computation.3 | async-start | bytes 393216 | tf_op jit(solution)/shard_map/all_to_all | solution.py:391
  75.2 0.7 copy-done.5
  76.3 9.6 %shard_map.98.disco_ref = f32[16,64,180]{2,1,0:T(8,128)S(1)} custom-call(s32[1]{0:T(128)} %bitcast.1.core_ref, s32[1]{0:T(128)} %bitcast.6.even_ref, bf16[16,64,180]{2,1,0:T(8,128)(2,1)S(1)} %bitcast.26, bf16[3,64,128]{2,1,0:T(8,128)(2,1)S(1)} %collective-permute-done.1.near_ref, bf16[6,64,128]{2,1,0:T(8,128)(2,1)S(1)} %collective-permute-done.other_ref.far_ref, ...), custom_call_target="tpu_custom_call" | custom-call | flops 1073741824 | bytes 712712 | tf_op jit(solution)/shard_map/pallas_call | solution.py:193
  85.9 1.9 %all-to-all-done.3.mixed_ref = bf16[16,48,128]{2,1,0:T(8,128)(2,1)S(1)} async-done(((bf16[16,48,128]{2,1,0:T(8,128)(2,1)}), bf16[16,48,128]{2,1,0:T(8,128)(2,1)S(1)}, u32[]{:S(2)}, u32[]{:S(2)}) %all-to-all-start.3) | async-done | bytes 196640 | tf_op jit(solution)/shard_map/all_to_all | solution.py:391
  87.7 1.0 shard_map.99
  88.7 10.4 %all-to-all-start.4 = ((bf16[32,64,128]{2,1,0:T(8,128)(2,1)}), bf16[32,64,128]{2,1,0:T(8,128)(2,1)S(1)}, u32[]{:S(2)}, u32[]{:S(2)}) async-start(bf16[32,64,128]{2,1,0:T(8,128)(2,1)} %shard_map.99), calls=%async_computation.4 | async-start | bytes 1048576 | tf_op jit(solution)/shard_map/all_to_all | solution.py:384
  99.2 0.8 dynamic-slice_bitcast_fusion.table_ref
  99.9 11.0 %all-to-all-done.4.modes_ref = bf16[32,64,128]{2,1,0:T(8,128)(2,1)S(1)} async-done(((bf16[32,64,128]{2,1,0:T(8,128)(2,1)}), bf16[32,64,128]{2,1,0:T(8,128)(2,1)S(1)}, u32[]{:S(2)}, u32[]{:S(2)}) %all-to-all-start.4) | async-done | bytes 524320 | tf_op jit(solution)/shard_map/all_to_all | solution.py:384
  110.9 1.6 %shard_map.100 = bf16[16,64,180]{2,1,0:T(8,128)(2,1)} custom-call(bf16[32,64,128]{2,1,0:T(8,128)(2,1)S(1)} %all-to-all-done.4.modes_ref, bf16[64,180]{1,0:T(8,128)(2,1)S(1)} %dynamic-slice_bitcast_fusion.table_ref, f32[16,64,180]{2,1,0:T(8,128)S(1)} %shard_map.98.disco_ref, bf16[16,64,180]{2,1,0:T(8,128)(2,1)S(1)} %bitcast.27), custom_call_target="tpu_custom_call" | custom-call | flops 10000000 | bytes 1653248 | tf_op jit(solution)/shard_map/pallas_call | solution.py:193
  (27 shorter events, 0.8 us)
Async XLA Ops:
  0.0 1.0 copy-start
  1.0 0.8 copy-start.3
  1.8 17.8 %copy-start.1 = (bf16[16,180,64]{1,2,0:T(8,128)(2,1)S(1)}, bf16[16,180,64]{1,2,0:T(8,128)(2,1)}, u32[]{:S(2)}) copy-start(bf16[16,180,64]{1,2,0:T(8,128)(2,1)} %param.9) | copy-start | bytes 1105924
  2.1 24.3 %collective-permute-start = (bf16[6,64,128]{2,1,0:T(8,128)(2,1)S(1)}, bf16[6,64,128]{2,1,0:T(8,128)(2,1)S(1)}, u32[]{:S(2)}, u32[]{:S(2)}) collective-permute-start(bf16[6,64,128]{2,1,0:T(8,128)(2,1)S(1)} %get-tuple-element.26.own_ref), channel_id=1, source_target_pairs={{0,15},{1,2},{2,1},{3,4},{4,3},{5,6},{6,5},{7,8},{8,7},{9,10},{10,... | collective-permute-start | bytes 294920 | tf_op jit(solution)/shard_map/ppermute | solution.py:421
  19.7 6.7 %copy-start.2 = (bf16[768,256]{1,0:T(8,128)(2,1)S(1)}, bf16[768,256]{1,0:T(8,128)(2,1)}, u32[]{:S(2)}) copy-start(bf16[768,256]{1,0:T(8,128)(2,1)} %constant.81.clone.pick_ref) | copy-start | bytes 1179652
  20.7 10.9 %all-to-all-start = ((bf16[8,64,128]{2,1,0:T(8,128)(2,1)}), bf16[8,64,128]{2,1,0:T(8,128)(2,1)S(1)}, u32[]{:S(2)}, u32[]{:S(2)}) async-start(bf16[8,64,128]{2,1,0:T(8,128)(2,1)} %shard_map.92), calls=%async_computation | async-start | bytes 262144 | tf_op jit(solution)/shard_map/all_to_all | solution.py:384
  27.2 22.7 %copy-start.4 = (bf16[24,2,64,64]{3,2,1,0:T(8,128)(2,1)S(1)}, bf16[24,2,64,64]{3,2,1,0:T(8,128)(2,1)}, u32[]{:S(2)}) copy-start(bf16[24,2,64,64]{3,2,1,0:T(8,128)(2,1)} %param.14) | copy-start | bytes 1179652
  32.3 9.2 %all-to-all-start.1 = ((bf16[4,64,384]{2,1,0:T(8,128)(2,1)}), bf16[4,64,384]{2,1,0:T(8,128)(2,1)S(1)}, u32[]{:S(2)}, u32[]{:S(2)}) async-start(bf16[4,64,384]{2,1,0:T(8,128)(2,1)} %shard_map.94), calls=%async_computation.1 | async-start | bytes 393216 | tf_op jit(solution)/shard_map/all_to_all | solution.py:384
  36.3 3.9 %collective-permute-start.1 = (bf16[3,64,128]{2,1,0:T(8,128)(2,1)S(1)}, bf16[3,64,128]{2,1,0:T(8,128)(2,1)S(1)}, u32[]{:S(2)}, u32[]{:S(2)}) collective-permute-start(bf16[3,64,128]{2,1,0:T(8,128)(2,1)S(1)} %get-tuple-element.27), channel_id=1, source_target_pairs={{0,1},{1,0},{2,3},{3,2},{4,5},{5,4},{6,7},{7,6},{8,9},{9,8},{10,11... | collective-permute-start | bytes 147464 | tf_op jit(solution)/shard_map/ppermute | solution.py:450
  42.4 21.2 %all-to-all-start.2 = ((bf16[16,48,128]{2,1,0:T(8,128)(2,1)}), bf16[16,48,128]{2,1,0:T(8,128)(2,1)S(1)}, u32[]{:S(2)}, u32[]{:S(2)}) async-start(bf16[16,48,128]{2,1,0:T(8,128)(2,1)} %get-tuple-element.29), calls=%async_computation.2 | async-start | bytes 393216 | tf_op jit(solution)/shard_map/all_to_all | solution.py:391
  50.2 4.2 %copy-start.6 = (f32[16,492]{1,0:T(8,128)S(1)}, f32[16,492]{1,0:T(8,128)}, u32[]{:S(2)}) copy-start(f32[16,492]{1,0:T(8,128)} %param.11) | copy-start | bytes 94468
  50.3 5.0 %collective-permute-start.2 = (bf16[1,64,256]{2,1,0:T(8,128)(2,1)S(1)}, bf16[1,64,256]{2,1,0:T(8,128)(2,1)S(1)}, u32[]{:S(2)}, u32[]{:S(2)}) collective-permute-start(bf16[1,64,256]{2,1,0:T(8,128)(2,1)S(1)} %get-tuple-element.31), channel_id=1, source_target_pairs={{0,16},{16,0},{32,48},{48,32},{64,80},{80,64},{96,112},{112,96},{1... | collective-permute-start | bytes 98312 | tf_op jit(solution)/shard_map/ppermute | solution.py:339
  53.7 1.6 %collective-permute-start.3 = (bf16[1,64,256]{2,1,0:T(8,128)(2,1)S(1)}, bf16[1,64,256]{2,1,0:T(8,128)(2,1)S(1)}, u32[]{:S(2)}, u32[]{:S(2)}) collective-permute-start(bf16[1,64,256]{2,1,0:T(8,128)(2,1)S(1)} %get-tuple-element.32), channel_id=1, source_target_pairs={{16,32},{32,16},{48,64},{64,48},{80,96},{96,80},{112,128},{128,112... | collective-permute-start | bytes 98312 | tf_op jit(solution)/shard_map/ppermute | solution.py:340
  64.8 10.2 %copy-start.7 = (s32[16]{0:T(128)S(1)}, s32[16]{0:T(128)}, u32[]{:S(2)}) copy-start(s32[16]{0:T(128)} %param.10) | copy-start | bytes 196
  64.8 23.0 %all-to-all-start.3 = ((bf16[16,48,128]{2,1,0:T(8,128)(2,1)}), bf16[16,48,128]{2,1,0:T(8,128)(2,1)S(1)}, u32[]{:S(2)}, u32[]{:S(2)}) async-start(bf16[16,48,128]{2,1,0:T(8,128)(2,1)} %shard_map.97), calls=%async_computation.3 | async-start | bytes 393216 | tf_op jit(solution)/shard_map/all_to_all | solution.py:391
  75.1 0.8 copy-start.5
  88.7 22.2 %all-to-all-start.4 = ((bf16[32,64,128]{2,1,0:T(8,128)(2,1)}), bf16[32,64,128]{2,1,0:T(8,128)(2,1)S(1)}, u32[]{:S(2)}, u32[]{:S(2)}) async-start(bf16[32,64,128]{2,1,0:T(8,128)(2,1)} %shard_map.99), calls=%async_computation.4 | async-start | bytes 1048576 | tf_op jit(solution)/shard_map/all_to_all | solution.py:384

commit v4 on v3

--- a/solution.py
+++ b/solution.py
@@ -18,6 +18,7 @@
 BF16 = jnp.bfloat16
 F32 = jnp.float32
 LON = ("y", "zh", "core")
+EARLY = (1, 4)
 
 
 def pair_of(sector):
@@ -36,11 +37,11 @@
     return np.array(out)
 
 
-def table(lon_cols, scale):
+def table(lon_cols, scale, orders_of):
     sectors = []
     for sector in range(NLON // lon_cols):
         columns = sector * lon_cols + np.arange(lon_cols)
-        residues = (orders_at(sector // 2 % 2)[:, None] * columns[None, :]) % NLON
+        residues = (orders_of(sector)[:, None] * columns[None, :]) % NLON
         phases = residues.astype(np.float32) * np.float32(2.0 * math.pi / NLON)
         sectors.append(np.concatenate([np.cos(phases), -np.sin(phases)], axis=0))
     return (np.stack(sectors).astype(np.float32) * np.float32(scale)).astype(BF16)
@@ -84,48 +85,46 @@
         out_ref[x, :, LANES:] = legs_ref[x]
 
 
-def legs_kernel(orders_ref, own_ref, other_ref, pick_ref, out_ref, lines_ref):
-    row = lax.broadcasted_iota(jnp.int32, (32, LANES), 0)
-    degree = lax.broadcasted_iota(jnp.int32, (32, LANES), 1)
-    sides = []
-    for side, ref in enumerate((own_ref, other_ref)):
-        tiles = [ref[3 + n, t * 32 : (t + 1) * 32, :].astype(F32) for n in range(3) for t in range(2)]
-        tiles[0] = jnp.where(degree >= orders_ref[side] + row % 2, tiles[0], 0.0)
-        sides.append(jnp.concatenate(tiles, axis=1))
-    lines = jnp.concatenate(sides, axis=0)
+def legs_kernel(orders_ref, leg_ref, pick_ref, out_ref, rows_ref, lines_ref):
+    rows = leg_ref.shape[0]
+    for i in range(rows):
+        rows_ref[2 * i : 2 * i + 2, :] = leg_ref[i].astype(F32)
+    row = lax.broadcasted_iota(jnp.int32, (2 * rows, LANES), 0)
+    degree = lax.broadcasted_iota(jnp.int32, (2 * rows, LANES), 1)
+    low = jnp.where(degree >= orders_ref[0] + row % 2, rows_ref[:, :LANES], 0.0)
+    lines = jnp.concatenate([low, rows_ref[:, LANES:]], axis=1)
     turned = [lines] + [pltpu.roll(lines, 768 - 24 * x, 1) for x in range(1, 4)]
     turned = jnp.concatenate(turned, axis=0).astype(BF16)
     picked = jnp.dot(turned, pick_ref[...], preferred_element_type=F32)
     for t in range(2):
         lines_ref[t] = picked[:, t * LANES : (t + 1) * LANES]
-    for side in range(2):
-        m = orders_ref[2] if side == 0 else 1 - orders_ref[2]
-        for q in range(2):
-            at = pl.multiple_of((m * 2 + q) * 16, 16)
-            for x in range(4):
-                for t in range(2):
-                    v = lines_ref[t, pl.ds(x * 64 + side * 32 + q, 16, stride=2), :]
-                    out_ref[x, pl.ds(at, 16), t * LANES : (t + 1) * LANES] = v.astype(BF16)
-
-
-def analysis_kernel(got_ref, coeff_ref, leg_ref):
-    for m in range(2):
-        parts = []
-        for q in range(2):
-            n = m * 2 + q
-            both = jnp.concatenate([got_ref[x, n * 16 : (n + 1) * 16, :] for x in range(4)], axis=0)
-            leg_ref[n] = both[:, LANES:]
-            parts.append(
-                lax.dot_general(
-                    both[:, LANES:],
-                    both[:, :LANES],
-                    (((0,), (0,)), ((), ())),
-                    preferred_element_type=F32,
-                )
+    for q in range(2):
+        for x in range(4):
+            for t in range(2):
+                v = lines_ref[t, pl.ds(x * 2 * rows + q, rows, stride=2), :]
+                out_ref[x, q * rows : (q + 1) * rows, t * LANES : (t + 1) * LANES] = v.astype(BF16)
+
+
+def analysis_kernel(got_ref, far_ref, coeff_ref, leg_ref, pack_ref):
+    parts = []
+    for q in range(2):
+        both = jnp.concatenate([got_ref[x, q * 16 : (q + 1) * 16, :] for x in range(4)], axis=0)
+        leg_ref[q] = both[:, LANES:]
+        for t in range(2):
+            pack_ref[3 + 2 * q + t] = both[:, (t + 1) * LANES : (t + 2) * LANES]
+        parts.append(
+            lax.dot_general(
+                both[:, LANES:],
+                both[:, :LANES],
+                (((0,), (0,)), ((), ())),
+                preferred_element_type=F32,
             )
-        for n in range(8):
-            rows = jnp.concatenate([p[n * 24 : (n + 1) * 24] for p in parts], axis=0)
-            coeff_ref[m * 8 + n] = rows.astype(BF16)
+        )
+    for n in range(8):
+        rows = jnp.concatenate([p[n * 24 : (n + 1) * 24] for p in parts], axis=0)
+        coeff_ref[n] = rows.astype(BF16)
+    for n in range(3):
+        pack_ref[n] = far_ref[n]
 
 
 def mixing_kernel(coeff_ref, weight_ref, out_ref):
@@ -146,21 +145,26 @@
         out_ref[n] = mixed
 
 
-def synthesis_kernel(mixed_ref, leg_ref, out_ref):
-    for m in range(2):
+def synthesis_kernel(mate_ref, mixed_ref, own_ref, other_ref, out_ref):
+    for side in range(2):
+        m = mate_ref[0] if side == 0 else 1 - mate_ref[0]
         blocks = [mixed_ref[m * 8 + n].astype(F32) for n in range(8)]
         for q in range(2):
-            at = m * 2 + q
+            if side == 0:
+                leg = own_ref[q]
+            else:
+                leg = jnp.concatenate([other_ref[3 + 2 * q], other_ref[4 + 2 * q]], axis=1)
             mixed = jnp.concatenate([v[q * 24 : (q + 1) * 24] for v in blocks], axis=0)
             modes = jnp.dot(
-                leg_ref[at][:, :192], mixed.astype(BF16), preferred_element_type=F32
+                leg[:, :192], mixed.astype(BF16), preferred_element_type=F32
             ).astype(BF16)
+            at = pl.multiple_of((m * 2 + q) * 16, 16)
             for x in range(4):
                 for g in range(8):
-                    out_ref[x * 8 + g, at * 16 : (at + 1) * 16, :] = modes[x * 16 : (x + 1) * 16]
-
-
-def final_kernel(modes_ref, table_ref, disco_ref, field_ref, out_ref, rows_ref):
+                    out_ref[x * 8 + g, pl.ds(at, 16), :] = modes[x * 16 : (x + 1) * 16]
+
+
+def final_kernel(modes_ref, table_ref, early_ref, late_ref, field_ref, out_ref, rows_ref):
     rows, channels, cols = field_ref.shape
     for g in range(8):
         total = modes_ref[g].astype(F32)
@@ -180,7 +184,12 @@
             preferred_element_type=F32,
         ).astype(BF16)
         for u in range(2):
-            v = spectral[u * 64 : (u + 1) * 64].astype(F32) + disco_ref[2 * m + u]
+            i = 2 * m + u
+            if EARLY[0] <= i < EARLY[1]:
+                disco_out = early_ref[i - EARLY[0]]
+            else:
+                disco_out = late_ref[i if i < EARLY[0] else i - EARLY[1] + EARLY[0]]
+            v = spectral[u * 64 : (u + 1) * 64].astype(F32) + disco_out
             inner = math.sqrt(2.0 / math.pi) * (v + 0.044715 * (v * v * v))
             act = 0.5 * v * (1.0 + jnp.tanh(inner))
             out_ref[2 * m + u] = (field_ref[2 * m + u].astype(F32) + act).astype(BF16)
@@ -211,13 +220,7 @@
     return v[:, :LANES], jnp.concatenate([v[:, LANES:], blank], axis=1)
 
 
-def edges_kernel(core_ref, field_ref, leg_ref, near_ref, far_ref, lines_ref):
-    for i in range(leg_ref.shape[0]):
-        lines_ref[2 * i : 2 * i + 2, :] = leg_ref[i].astype(F32)
-    for n in range(3):
-        for t in range(2):
-            at = (2 * n + t) * LANES
-            far_ref[3 + n, t * 32 : (t + 1) * 32, :] = lines_ref[:, at : at + LANES].astype(BF16)
+def edges_kernel(core_ref, field_ref, near_ref, far_ref):
     rows, channels, cols = field_ref.shape
     lane = lax.broadcasted_iota(jnp.int32, (channels, LANES), 1)
     first = core_ref[0] == 0
@@ -265,16 +268,18 @@
 
 
 def toeplitz_kernel(
-    core_ref, even_ref, field_ref, near_ref, far_ref, one_ref, two_ref, base_ref, weight_ref,
+    spans, core_ref, even_ref, field_ref, near_ref, far_ref, one_ref, two_ref, base_ref, weight_ref,
     out_ref, ext_ref, rest_ref, band_ref,
 ):
     rows, channels, cols = field_ref.shape
     lane = lax.broadcasted_iota(jnp.int32, (channels, LANES), 1)
-    even = even_ref[0] == 1
+    wanted = [i for first, last in spans for i in range(first, last)]
     for r in range(rows + 2):
+        if not any(i in wanted for i in (r - 2, r - 1, r)):
+            continue
         if r in (0, rows + 1):
             a, b = (one_ref, two_ref) if r else (two_ref, one_ref)
-            row = jnp.where(even, a[0].astype(F32), b[0].astype(F32))
+            row = jnp.where(even_ref[0] == 1, a[0].astype(F32), b[0].astype(F32))
             one, two = row[:, :LANES], row[:, LANES:]
         else:
             g, m = divmod(r - 1, 6)
@@ -284,7 +289,7 @@
         ext_ref[r, :, LANES:] = two.astype(BF16)
         for a in range(3):
             i = r - a
-            if 0 <= i < rows:
+            if i in wanted:
                 part = pltpu.roll(two, 2 * HMAX * a, 1) if a else two
                 inside = (lane >= 2 * HMAX * a) & (lane < 2 * HMAX * (a + 1))
                 rest_ref[i] = jnp.where(inside, part, rest_ref[i] if a else 0.0)
@@ -292,8 +297,7 @@
     r = lax.broadcasted_iota(jnp.int32, (LANES, LANES), 0)
     s = lax.broadcasted_iota(jnp.int32, (LANES, LANES), 1)
 
-    @pl.loop(0, rows)
-    def _(row):
+    def one_row(row, at):
         for k in range(BASES):
             cols_k = slice(k * LANES, (k + 1) * LANES)
             spill = []
@@ -329,21 +333,38 @@
             axis=0,
         )
         mixed = jnp.dot(weight_ref[...], stacked, preferred_element_type=F32)
-        out_ref[row] = mixed[:, :cols]
+        out_ref[at] = mixed[:, :cols]
+
+    done = 0
+    for first, last in spans:
+        pl.loop(first, last)(lambda row, shift=done - first: one_row(row, row + shift))
+        done += last - first
+
+
+def early_kernel(core_ref, field_ref, near_ref, far_ref, base_ref, weight_ref, *refs):
+    toeplitz_kernel(
+        (EARLY,), core_ref, None, field_ref, near_ref, far_ref, None, None, base_ref, weight_ref, *refs
+    )
+
+
+def late_kernel(*refs):
+    toeplitz_kernel(((0, EARLY[0]), (EARLY[1], 16)), *refs)
 
 
 def lat_rows_of(field, scalars, near, far):
     row = struct(BF16, 1, field.shape[1], 2 * LANES)
-    one, two = call(rows_kernel, (row, row), *scalars, field, near, far, smem=2)
+    one, two = call(
+        rows_kernel, (row, row), *scalars, field, near, far, smem=2, flops=2 * 10**10
+    )
     lat = ("zl", "x")
+    one, two, far = lax.optimization_barrier((one, two, far))
     one = lax.ppermute(one, lat, [(i, i ^ 1) for i in range(32)])
     two = lax.ppermute(two, lat, [(i, i + 1 if i % 2 else i - 1) for i in range(1, 31)])
-    return one, two
-
-
-def disco(field, around, disco_reach, disco_taps, disco_weight):
-    lat_rows, channels, lon_cols = field.shape
-    core, even, near, far, one, two = around
+    return far, one, two
+
+
+def taps_of(channels, disco_reach, disco_taps, disco_weight):
+    lat_rows = disco_taps.shape[0]
     offsets = jnp.abs(jnp.arange(TAPS, dtype=jnp.int32) - HMAX)
     within = offsets[None, :] <= disco_reach[:, None]
     coef = jnp.where(
@@ -358,20 +379,21 @@
         axis=2,
     )
     weight = disco_weight.transpose(2, 0, 1).reshape(channels, BASES * channels)
+    return base, weight
+
+
+def disco(kernel, count, field, scalars, around, base, weight):
+    lat_rows, channels, lon_cols = field.shape
     return call(
-        toeplitz_kernel,
-        struct(F32, lat_rows, channels, lon_cols),
-        core,
-        even,
+        kernel,
+        struct(F32, count, channels, lon_cols),
+        *scalars,
         field,
-        near,
-        far,
-        one,
-        two,
+        *around,
         base,
         weight,
-        smem=2,
-        flops=2 * lat_rows * 128 * 512 * 512,
+        smem=len(scalars),
+        flops=2 * count * 128 * 512 * 512,
         scratch=[
             pltpu.VMEM((lat_rows + 2, channels, 2 * LANES), BF16),
             pltpu.VMEM((lat_rows, channels, LANES), F32),
@@ -399,76 +421,86 @@
     own = mixing.shape[0]
     place = lax.axis_index(LON)
     field = grid_field.transpose(0, 2, 1)
-    forward = jnp.asarray(table(lon_cols, 1.0 / math.sqrt(NLON)))
-    forward = lax.dynamic_index_in_dim(forward, place, 0, keepdims=False)
-    inverse = jnp.asarray(table(lon_cols, 1.0 / math.sqrt(MODES)))
-    inverse = lax.dynamic_index_in_dim(inverse, place, 0, keepdims=False)
+    forward = table(lon_cols, 1.0 / math.sqrt(NLON), lambda sector: np.arange(MODES))
+    inverse = table(lon_cols, 1.0 / math.sqrt(MODES), lambda sector: orders_at(sector // 2 % 2))
+    forward = lax.dynamic_index_in_dim(jnp.asarray(forward), place, 0, keepdims=False)
+    inverse = lax.dynamic_index_in_dim(jnp.asarray(inverse), place, 0, keepdims=False)
     spread = [pltpu.VMEM((MODES * lat_rows, wide), F32)]
 
     core = lax.axis_index("core").reshape(1)
     even = (1 - lax.axis_index("x") % 2).reshape(1)
+    waves = call(
+        forward_kernel, struct(BF16, 16, 2 * lat_rows, wide), field, forward, scratch=spread
+    )
+    waves = exchange(waves, LON)
     packed = struct(BF16, 3, channels, LANES)
-    near, mine = call(
-        edges_kernel,
-        (packed, struct(BF16, 6, channels, LANES)),
-        core,
-        field,
-        legendre,
-        smem=1,
-        scratch=[pltpu.VMEM((2 * lat_rows, 768), F32)],
-    )
-    swap = [(i, member(pair_of(i), i % 2)) for i in range(16)]
-    far = lax.ppermute(mine, LON, swap)
-    lines, mine = lax.optimization_barrier((field, mine))
-    waves = call(
-        forward_kernel,
-        struct(BF16, 8, 4 * lat_rows, wide),
-        lines,
-        forward,
-        scratch=spread,
-        flops=10**7,
-    )
-    waves = exchange(waves, ("y", "core"))
-    waves, near = lax.optimization_barrier((waves, near))
-    pair = pair_of(place)
-    mate = 1 - core[0]
-    orders = jnp.stack([member(pair, mate) * 2, member(pair, 1 - mate) * 2, mate])
+    near, far = call(edges_kernel, (packed, packed), core, field, smem=1)
+    near = lax.ppermute(near, LON, [(i, i ^ 1) for i in range(16)])
+    base, taps_weight = taps_of(channels, disco_reach, disco_taps, disco_weight)
     weight = jnp.concatenate([mixing[:, 0], mixing[:, 1]], axis=2)
     legs = call(
         legs_kernel,
-        struct(BF16, 4, 4 * lat_rows, 256),
-        orders.astype(jnp.int32),
-        mine,
-        far,
+        struct(BF16, 4, 2 * lat_rows, 256),
+        (place * 2).astype(jnp.int32).reshape(1),
+        legendre,
         jnp.asarray(degree_order()),
         smem=1,
-        flops=10**7,
-        scratch=[pltpu.VMEM((2, 16 * lat_rows, LANES), F32)],
-    )
-    message = call(spectra_kernel, struct(BF16, 4, 4 * lat_rows, 384), waves, legs)
+        scratch=[
+            pltpu.VMEM((2 * lat_rows, 768), F32),
+            pltpu.VMEM((2, 8 * lat_rows, LANES), F32),
+        ],
+    )
+    waves, near, far, legs, inverse, base, taps_weight = lax.optimization_barrier(
+        (waves, near, far, legs, inverse, base, taps_weight)
+    )
+    message = call(spectra_kernel, struct(BF16, 4, 2 * lat_rows, 384), waves, legs)
     message = exchange(message, ("x",))
-    near = lax.ppermute(near, LON, [(i, i ^ 1) for i in range(16)])
-    message, near = lax.optimization_barrier((message, near))
-    coeffs, leg = call(
+    coeffs, leg, mine = call(
         analysis_kernel,
-        (struct(BF16, 16, 2 * own, wide), struct(BF16, 4, 4 * lat_rows, 256)),
+        (
+            struct(BF16, 8, 2 * own, wide),
+            struct(BF16, 2, 4 * lat_rows, 256),
+            struct(BF16, 7, 4 * lat_rows, LANES),
+        ),
         message,
-    )
-    coeffs = line_exchange(coeffs)
-    one, two = lat_rows_of(field, (core, even), near, far)
-    coeffs, one, two = lax.optimization_barrier((coeffs, one, two))
+        far,
+    )
+    coeffs = exchange(coeffs, ("zl",))
+    swap = [(i, member(pair_of(i), i % 2)) for i in range(16)]
+    far = lax.ppermute(mine, LON, swap)
+    far, one, two = lat_rows_of(field, (core, even), near, far)
     mixed = call(mixing_kernel, struct(BF16, 16, 2 * own, wide), coeffs, weight)
     mixed = line_exchange(mixed)
-    disco_out = disco(field, (core, even, near, far, one, two), disco_reach, disco_taps, disco_weight)
-    mixed, disco_out = lax.optimization_barrier((mixed, disco_out))
-    modes = call(synthesis_kernel, struct(BF16, 32, 4 * lat_rows, wide), mixed, leg)
+    early = disco(
+        early_kernel, EARLY[1] - EARLY[0], field, (core,), (near, far), base, taps_weight
+    )
+    mixed, one, two, early = lax.optimization_barrier((mixed, one, two, early))
+    modes = call(
+        synthesis_kernel,
+        struct(BF16, 32, 4 * lat_rows, wide),
+        1 - core,
+        mixed,
+        leg,
+        far,
+        smem=1,
+    )
     modes = exchange(modes, ("x", "y", "core"))
+    late = disco(
+        late_kernel,
+        lat_rows - EARLY[1] + EARLY[0],
+        field,
+        (core, even),
+        (near, far, one, two),
+        base,
+        taps_weight,
+    )
     out = call(
         final_kernel,
         struct(BF16, lat_rows, channels, lon_cols),
         modes,
         inverse,
-        disco_out,
+        early,
+        late,
         field,
         scratch=spread,
     )

time: 113 us -> 110 us (0.973)
  starting transfers between devices: 61.5 us -> 52 us
  waiting for transfers between devices: 28.4 us -> 36.2 us
    all_to_all x3 -> x4, starting transfers between devices: 20 us -> 39.1 us  [exchange(): return lax.all_to_all(cells, axes, split_axis=0, concat_axis=0, tiled=True)]
    ppermute x1, starting transfers between devices: 16.8 us -> 3.06 us  [per_device(): far = lax.ppermute(mine, LON, swap)]
    all_to_all x2 -> x1, starting transfers between devices: 17.6 us -> 4.91 us  [line_exchange(): lax.all_to_all(cells, ('zl', *LON), split_axis=0, concat_axis=0, tiled=Tr...]
    all_to_all x3 -> x4, waiting for transfers between devices: 16.5 us -> 25 us  [exchange(): return lax.all_to_all(cells, axes, split_axis=0, concat_axis=0, tiled=True)]
    ppermute x1, starting transfers between devices: 3.37 us -> 2.19 us  [lat_rows_of(): one = lax.ppermute(one, lat, [(i, i ^ 1) for i in range(32)])]
    pallas_call x10 -> x11, Pallas kernels: 17.2 us -> 16.3 us  [call(): pl.pallas_call(kernel, out_shape=out, in_specs=[scalar] * smem + [vmem] *...]
    all_to_all x2 -> x1, waiting for transfers between devices: 10.2 us -> 11 us  [line_exchange(): lax.all_to_all(cells, ('zl', *LON), split_axis=0, concat_axis=0, tiled=Tr...]
  transfers between devices with their start and end apart: 9 -> 9, of which waited for: 7 -> 6; matrix products, arithmetic and copies ran while one was open for 2% -> 2% of each run, Pallas kernels for 10% -> 10%
where the time goes in v4:
time: 110 us
  starting transfers between devices  52 us (47%)
  waiting for transfers between devices  36.2 us (33%)
  Pallas kernels  16.3 us (15%)
  local copies, waits for them, and re-layouts  4.39 us (4%)
    all_to_all x4, starting transfers between devices, exchange(): return lax.all_to_all(cells, axes, split_axis=0, concat_axis=0, tiled=True)  39.1 us
    all_to_all x4, waiting for transfers between devices, exchange(): return lax.all_to_all(cells, axes, split_axis=0, concat_axis=0, tiled=True)  25 us
    pallas_call x11, Pallas kernels, call(): pl.pallas_call(kernel, out_shape=out, in_specs=[scalar] * smem + [vmem] *...  16.3 us
    all_to_all x1, waiting for transfers between devices, line_exchange(): lax.all_to_all(cells, ('zl', *LON), split_axis=0, concat_axis=0, tiled=Tr...  11 us
    all_to_all x1, starting transfers between devices, line_exchange(): lax.all_to_all(cells, ('zl', *LON), split_axis=0, concat_axis=0, tiled=Tr...  4.91 us
    ppermute x1, starting transfers between devices, per_device(): far = lax.ppermute(mine, LON, swap)  3.06 us
    unnamed x16, local copies, waits for them, and re-layouts  2.33 us
  transfers between devices with their start and end apart: 9, of which 6 were waited for; matrix products, arithmetic and copies ran while one was open for 2% of the time, Pallas kernels for 10%

profile of v4, /device:TPU:1, one launch (start us, length us, event | category | flops | bytes accessed | tf_op | source)
XLA Modules:
  0.0 109.5 jit_solution(9843350617254462634)
XLA Ops:
  0.0 0.8 dynamic-slice_bitcast_fusion.1.table_ref
  0.8 1.0 copy-done
  1.8 1.0 shard_map.91
  2.8 19.2 %all-to-all-start = ((bf16[16,32,128]{2,1,0:T(8,128)(2,1)}), bf16[16,32,128]{2,1,0:T(8,128)(2,1)S(1)}, u32[]{:S(2)}, u32[]{:S(2)}) async-start(bf16[16,32,128]{2,1,0:T(8,128)(2,1)} %shard_map.91), calls=%async_computation | async-start | bytes 262144 | tf_op jit(solution)/shard_map/all_to_all | solution.py:406
  22.1 0.2 shard_map.92
  22.3 2.0 %collective-permute-start = (bf16[3,64,128]{2,1,0:T(8,128)(2,1)S(1)}, bf16[3,64,128]{2,1,0:T(8,128)(2,1)S(1)}, u32[]{:S(2)}, u32[]{:S(2)}) collective-permute-start(bf16[3,64,128]{2,1,0:T(8,128)(2,1)S(1)} %get-tuple-element.26), channel_id=1, source_target_pairs={{0,1},{1,0},{2,3},{3,2},{4,5},{5,4},{6,7},{7,6},{8,9},{9,8},{10,11... | collective-permute-start | bytes 147464 | tf_op jit(solution)/shard_map/ppermute | solution.py:438
  24.5 0.5 copy-done.7
  25.5 0.8 dynamic-slice_bitcast_fusion.table_ref
  26.5 0.7 copy-done.3
  27.1 0.3 shard_map.93.legs_ref
  27.5 9.6 %all-to-all-done.waves_ref = bf16[16,32,128]{2,1,0:T(8,128)(2,1)S(1)} async-done(((bf16[16,32,128]{2,1,0:T(8,128)(2,1)}), bf16[16,32,128]{2,1,0:T(8,128)(2,1)S(1)}, u32[]{:S(2)}, u32[]{:S(2)}) %all-to-all-start) | async-done | bytes 131104 | tf_op jit(solution)/shard_map/all_to_all | solution.py:406
  37.0 0.7 shard_map.94
  37.7 4.0 %all-to-all-start.1 = ((bf16[4,32,384]{2,1,0:T(8,128)(2,1)}), bf16[4,32,384]{2,1,0:T(8,128)(2,1)S(1)}, u32[]{:S(2)}, u32[]{:S(2)}) async-start(bf16[4,32,384]{2,1,0:T(8,128)(2,1)} %shard_map.94), calls=%async_computation.1 | async-start | bytes 196608 | tf_op jit(solution)/shard_map/all_to_all | solution.py:406
  41.7 4.7 %all-to-all-done.1.got_ref = bf16[4,32,384]{2,1,0:T(8,128)(2,1)S(1)} async-done(((bf16[4,32,384]{2,1,0:T(8,128)(2,1)}), bf16[4,32,384]{2,1,0:T(8,128)(2,1)S(1)}, u32[]{:S(2)}, u32[]{:S(2)}) %all-to-all-start.1) | async-done | bytes 98336 | tf_op jit(solution)/shard_map/all_to_all | solution.py:406
  46.4 0.8 shard_map.95
  47.2 6.1 %all-to-all-start.2 = ((bf16[8,48,128]{2,1,0:T(8,128)(2,1)}), bf16[8,48,128]{2,1,0:T(8,128)(2,1)S(1)}, u32[]{:S(2)}, u32[]{:S(2)}) async-start(bf16[8,48,128]{2,1,0:T(8,128)(2,1)} %get-tuple-element.31), calls=%async_computation.2 | async-start | bytes 196608 | tf_op jit(solution)/shard_map/all_to_all | solution.py:406
  53.4 3.1 %collective-permute-start.1 = (bf16[7,64,128]{2,1,0:T(8,128)(2,1)S(1)}, bf16[7,64,128]{2,1,0:T(8,128)(2,1)S(1)}, u32[]{:S(2)}, u32[]{:S(2)}) collective-permute-start(bf16[7,64,128]{2,1,0:T(8,128)(2,1)S(1)} %get-tuple-element.33), channel_id=1, source_target_pairs={{0,15},{1,2},{2,1},{3,4},{4,3},{5,6},{6,5},{7,8},{8,7},{9,10},{10,... | collective-permute-start | bytes 344072 | tf_op jit(solution)/shard_map/ppermute | solution.py:470
  56.5 0.2 pad_maximum_fusion.weight_ref
  56.7 6.7 %all-to-all-done.2.coeff_ref = bf16[8,48,128]{2,1,0:T(8,128)(2,1)S(1)} async-done(((bf16[8,48,128]{2,1,0:T(8,128)(2,1)}), bf16[8,48,128]{2,1,0:T(8,128)(2,1)S(1)}, u32[]{:S(2)}, u32[]{:S(2)}) %all-to-all-start.2) | async-done | bytes 98336 | tf_op jit(solution)/shard_map/all_to_all | solution.py:406
  63.4 1.1 %shard_map.96 = bf16[16,48,128]{2,1,0:T(8,128)(2,1)} custom-call(bf16[8,48,128]{2,1,0:T(8,128)(2,1)S(1)} %all-to-all-done.2.coeff_ref, bf16[24,64,128]{2,1,0:T(8,128)(2,1)S(1)} %pad_maximum_fusion.weight_ref), custom_call_target="tpu_custom_call" | custom-call | flops 10000000 | bytes 491520 | tf_op jit(solution)/shard_map/pallas_call | solution.py:202
  64.5 4.9 %all-to-all-start.3 = ((bf16[16,48,128]{2,1,0:T(8,128)(2,1)}), bf16[16,48,128]{2,1,0:T(8,128)(2,1)S(1)}, u32[]{:S(2)}, u32[]{:S(2)}) async-start(bf16[16,48,128]{2,1,0:T(8,128)(2,1)} %shard_map.96), calls=%async_computation.3 | async-start | bytes 393216 | tf_op jit(solution)/shard_map/all_to_all | solution.py:413
  69.4 0.1 shard_map.97
  69.5 2.2 %collective-permute-start.2 = (bf16[1,64,256]{2,1,0:T(8,128)(2,1)S(1)}, bf16[1,64,256]{2,1,0:T(8,128)(2,1)S(1)}, u32[]{:S(2)}, u32[]{:S(2)}) collective-permute-start(bf16[1,64,256]{2,1,0:T(8,128)(2,1)S(1)} %get-tuple-element.36), channel_id=1, source_target_pairs={{0,16},{16,0},{32,48},{48,32},{64,80},{80,64},{96,112},{112,96},{1... | collective-permute-start | bytes 98312 | tf_op jit(solution)/shard_map/ppermute | solution.py:361
  71.7 0.7 collective-permute-start.3
  72.4 1.8 %shard_map.98.early_ref = f32[3,64,180]{2,1,0:T(8,128)S(1)} custom-call(s32[1]{0:T(128)} %bitcast.core_ref.refs_0_, bf16[16,64,180]{2,1,0:T(8,128)(2,1)S(1)} %bitcast.24, bf16[3,64,128]{2,1,0:T(8,128)(2,1)S(1)} %collective-permute-done.near_ref.refs_3_, bf16[7,64,128]{2,1,0:T(8,128)(2,1)S(1)} %collective-permute-done.1.far_ref.other_ref.refs_4_, ...), custom_call_target="tpu_custom_call" | custom-call | flops 201326592 | bytes 663556 | tf_op jit(solution)/shard_map/pallas_call | solution.py:202
  74.2 0.3 collective-permute-done.2.refs_5_
  74.5 11.0 %all-to-all-done.3.mixed_ref = bf16[16,48,128]{2,1,0:T(8,128)(2,1)S(1)} async-done(((bf16[16,48,128]{2,1,0:T(8,128)(2,1)}), bf16[16,48,128]{2,1,0:T(8,128)(2,1)S(1)}, u32[]{:S(2)}, u32[]{:S(2)}) %all-to-all-start.3) | async-done | bytes 196640 | tf_op jit(solution)/shard_map/all_to_all | solution.py:413
  85.5 1.0 shard_map.99
  86.5 9.8 %all-to-all-start.4 = ((bf16[32,64,128]{2,1,0:T(8,128)(2,1)}), bf16[32,64,128]{2,1,0:T(8,128)(2,1)S(1)}, u32[]{:S(2)}, u32[]{:S(2)}) async-start(bf16[32,64,128]{2,1,0:T(8,128)(2,1)} %shard_map.99), calls=%async_computation.4 | async-start | bytes 1048576 | tf_op jit(solution)/shard_map/all_to_all | solution.py:406
  96.3 7.6 %shard_map.100.late_ref = f32[13,64,180]{2,1,0:T(8,128)S(1)} custom-call(s32[1]{0:T(128)} %bitcast.core_ref.refs_0_, s32[1]{0:T(128)} %bitcast.9.even_ref.refs_1_, bf16[16,64,180]{2,1,0:T(8,128)(2,1)S(1)} %bitcast.25, bf16[3,64,128]{2,1,0:T(8,128)(2,1)S(1)} %collective-permute-done.near_ref.refs_3_, ...), custom_call_target="tpu_custom_call" | custom-call | flops 872415232 | bytes 729096 | tf_op jit(solution)/shard_map/pallas_call | solution.py:202
  103.8 4.1 %all-to-all-done.4.modes_ref = bf16[32,64,128]{2,1,0:T(8,128)(2,1)S(1)} async-done(((bf16[32,64,128]{2,1,0:T(8,128)(2,1)}), bf16[32,64,128]{2,1,0:T(8,128)(2,1)S(1)}, u32[]{:S(2)}, u32[]{:S(2)}) %all-to-all-start.4) | async-done | bytes 524320 | tf_op jit(solution)/shard_map/all_to_all | solution.py:406
  107.9 1.6 %shard_map.101 = bf16[16,64,180]{2,1,0:T(8,128)(2,1)} custom-call(bf16[32,64,128]{2,1,0:T(8,128)(2,1)S(1)} %all-to-all-done.4.modes_ref, bf16[64,180]{1,0:T(8,128)(2,1)S(1)} %dynamic-slice_bitcast_fusion.table_ref, f32[3,64,180]{2,1,0:T(8,128)S(1)} %shard_map.98.early_ref, f32[13,64,180]{2,1,0:T(8,128)S(1)} %shard_map.100.late_ref, ...), custom_call_target="tpu_custom_call" | custom-call | flops 10000000 | bytes 1653248 | tf_op jit(solution)/shard_map/pallas_call | solution.py:202
  (27 shorter events, 0.8 us)
Async XLA Ops:
  0.8 1.0 copy-start
  1.8 20.3 %copy-start.1 = (bf16[16,180,64]{1,2,0:T(8,128)(2,1)S(1)}, bf16[16,180,64]{1,2,0:T(8,128)(2,1)}, u32[]{:S(2)}) copy-start(bf16[16,180,64]{1,2,0:T(8,128)(2,1)} %param.9) | copy-start | bytes 1105924
  2.8 34.2 %all-to-all-start = ((bf16[16,32,128]{2,1,0:T(8,128)(2,1)}), bf16[16,32,128]{2,1,0:T(8,128)(2,1)S(1)}, u32[]{:S(2)}, u32[]{:S(2)}) async-start(bf16[16,32,128]{2,1,0:T(8,128)(2,1)} %shard_map.91), calls=%async_computation | async-start | bytes 262144 | tf_op jit(solution)/shard_map/all_to_all | solution.py:406
  22.1 2.2 %copy-start.6 = (f32[16,492]{1,0:T(8,128)S(1)}, f32[16,492]{1,0:T(8,128)}, u32[]{:S(2)}) copy-start(f32[16,492]{1,0:T(8,128)} %param.11) | copy-start | bytes 94468
  22.3 5.1 %collective-permute-start = (bf16[3,64,128]{2,1,0:T(8,128)(2,1)S(1)}, bf16[3,64,128]{2,1,0:T(8,128)(2,1)S(1)}, u32[]{:S(2)}, u32[]{:S(2)}) collective-permute-start(bf16[3,64,128]{2,1,0:T(8,128)(2,1)S(1)} %get-tuple-element.26), channel_id=1, source_target_pairs={{0,1},{1,0},{2,3},{3,2},{4,5},{5,4},{6,7},{7,6},{8,9},{9,8},{10,11... | collective-permute-start | bytes 147464 | tf_op jit(solution)/shard_map/ppermute | solution.py:438
  24.4 0.7 copy-start.7
  25.2 1.2 %copy-start.2 = (bf16[768,256]{1,0:T(8,128)(2,1)S(1)}, bf16[768,256]{1,0:T(8,128)(2,1)}, u32[]{:S(2)}) copy-start(bf16[768,256]{1,0:T(8,128)(2,1)} %constant.54.clone.pick_ref) | copy-start | bytes 1179652
  25.5 0.8 copy-start.5
  26.3 0.8 copy-start.3
  26.3 27.0 %copy-start.4 = (bf16[24,2,64,64]{3,2,1,0:T(8,128)(2,1)S(1)}, bf16[24,2,64,64]{3,2,1,0:T(8,128)(2,1)}, u32[]{:S(2)}) copy-start(bf16[24,2,64,64]{3,2,1,0:T(8,128)(2,1)} %param.14) | copy-start | bytes 1179652
  37.7 8.7 %all-to-all-start.1 = ((bf16[4,32,384]{2,1,0:T(8,128)(2,1)}), bf16[4,32,384]{2,1,0:T(8,128)(2,1)S(1)}, u32[]{:S(2)}, u32[]{:S(2)}) async-start(bf16[4,32,384]{2,1,0:T(8,128)(2,1)} %shard_map.94), calls=%async_computation.1 | async-start | bytes 196608 | tf_op jit(solution)/shard_map/all_to_all | solution.py:406
  47.2 16.1 %all-to-all-start.2 = ((bf16[8,48,128]{2,1,0:T(8,128)(2,1)}), bf16[8,48,128]{2,1,0:T(8,128)(2,1)S(1)}, u32[]{:S(2)}, u32[]{:S(2)}) async-start(bf16[8,48,128]{2,1,0:T(8,128)(2,1)} %get-tuple-element.31), calls=%async_computation.2 | async-start | bytes 196608 | tf_op jit(solution)/shard_map/all_to_all | solution.py:406
  53.4 16.0 %collective-permute-start.1 = (bf16[7,64,128]{2,1,0:T(8,128)(2,1)S(1)}, bf16[7,64,128]{2,1,0:T(8,128)(2,1)S(1)}, u32[]{:S(2)}, u32[]{:S(2)}) collective-permute-start(bf16[7,64,128]{2,1,0:T(8,128)(2,1)S(1)} %get-tuple-element.33), channel_id=1, source_target_pairs={{0,15},{1,2},{2,1},{3,4},{4,3},{5,6},{6,5},{7,8},{8,7},{9,10},{10,... | collective-permute-start | bytes 344072 | tf_op jit(solution)/shard_map/ppermute | solution.py:470
  64.5 21.0 %all-to-all-start.3 = ((bf16[16,48,128]{2,1,0:T(8,128)(2,1)}), bf16[16,48,128]{2,1,0:T(8,128)(2,1)S(1)}, u32[]{:S(2)}, u32[]{:S(2)}) async-start(bf16[16,48,128]{2,1,0:T(8,128)(2,1)} %shard_map.96), calls=%async_computation.3 | async-start | bytes 393216 | tf_op jit(solution)/shard_map/all_to_all | solution.py:413
  69.5 5.0 %collective-permute-start.2 = (bf16[1,64,256]{2,1,0:T(8,128)(2,1)S(1)}, bf16[1,64,256]{2,1,0:T(8,128)(2,1)S(1)}, u32[]{:S(2)}, u32[]{:S(2)}) collective-permute-start(bf16[1,64,256]{2,1,0:T(8,128)(2,1)S(1)} %get-tuple-element.36), channel_id=1, source_target_pairs={{0,16},{16,0},{32,48},{48,32},{64,80},{80,64},{96,112},{112,96},{1... | collective-permute-start | bytes 98312 | tf_op jit(solution)/shard_map/ppermute | solution.py:361
  71.7 2.8 %collective-permute-start.3 = (bf16[1,64,256]{2,1,0:T(8,128)(2,1)S(1)}, bf16[1,64,256]{2,1,0:T(8,128)(2,1)S(1)}, u32[]{:S(2)}, u32[]{:S(2)}) collective-permute-start(bf16[1,64,256]{2,1,0:T(8,128)(2,1)S(1)} %get-tuple-element.37), channel_id=1, source_target_pairs={{16,32},{32,16},{48,64},{64,48},{80,96},{96,80},{112,128},{128,112... | collective-permute-start | bytes 98312 | tf_op jit(solution)/shard_map/ppermute | solution.py:362
  86.5 21.4 %all-to-all-start.4 = ((bf16[32,64,128]{2,1,0:T(8,128)(2,1)}), bf16[32,64,128]{2,1,0:T(8,128)(2,1)S(1)}, u32[]{:S(2)}, u32[]{:S(2)}) async-start(bf16[32,64,128]{2,1,0:T(8,128)(2,1)} %shard_map.99), calls=%async_computation.4 | async-start | bytes 1048576 | tf_op jit(solution)/shard_map/all_to_all | solution.py:406

commit v5 on v4

--- a/solution.py
+++ b/solution.py
@@ -106,12 +106,12 @@
 
 
 def analysis_kernel(got_ref, far_ref, coeff_ref, leg_ref, pack_ref):
-    parts = []
+    parts, highs = [], []
     for q in range(2):
         both = jnp.concatenate([got_ref[x, q * 16 : (q + 1) * 16, :] for x in range(4)], axis=0)
         leg_ref[q] = both[:, LANES:]
-        for t in range(2):
-            pack_ref[3 + 2 * q + t] = both[:, (t + 1) * LANES : (t + 2) * LANES]
+        pack_ref[3 + q] = both[:, LANES : 2 * LANES]
+        highs.append(both[:, 2 * LANES :].astype(F32))
         parts.append(
             lax.dot_general(
                 both[:, LANES:],
@@ -125,6 +125,8 @@
         coeff_ref[n] = rows.astype(BF16)
     for n in range(3):
         pack_ref[n] = far_ref[n]
+    high = jnp.where(first_half(highs[0].shape), highs[0], pltpu.roll(highs[1], 64, 1))
+    pack_ref[5] = high.astype(BF16)
 
 
 def mixing_kernel(coeff_ref, weight_ref, out_ref):
@@ -153,7 +155,9 @@
             if side == 0:
                 leg = own_ref[q]
             else:
-                leg = jnp.concatenate([other_ref[3 + 2 * q], other_ref[4 + 2 * q]], axis=1)
+                high = other_ref[5].astype(F32)
+                high = pltpu.roll(high, 64, 1) if q else high
+                leg = jnp.concatenate([other_ref[3 + q], high.astype(BF16)], axis=1)
             mixed = jnp.concatenate([v[q * 24 : (q + 1) * 24] for v in blocks], axis=0)
             modes = jnp.dot(
                 leg[:, :192], mixed.astype(BF16), preferred_element_type=F32
@@ -460,7 +464,7 @@
         (
             struct(BF16, 8, 2 * own, wide),
             struct(BF16, 2, 4 * lat_rows, 256),
-            struct(BF16, 7, 4 * lat_rows, LANES),
+            struct(BF16, 6, 4 * lat_rows, LANES),
         ),
         message,
         far,

time: 110 us -> 110 us (level)
  no operation moved by 1% of the time
where the time goes in v5:
time: 110 us
  starting transfers between devices  52 us (47%)
  waiting for transfers between devices  36.3 us (33%)
  Pallas kernels  16.3 us (15%)
  local copies, waits for them, and re-layouts  4.39 us (4%)
    all_to_all x4, starting transfers between devices, exchange(): return lax.all_to_all(cells, axes, split_axis=0, concat_axis=0, tiled=True)  39.1 us
    all_to_all x4, waiting for transfers between devices, exchange(): return lax.all_to_all(cells, axes, split_axis=0, concat_axis=0, tiled=True)  25 us
    pallas_call x11, Pallas kernels, call(): pl.pallas_call(kernel, out_shape=out, in_specs=[scalar] * smem + [vmem] *...  16.3 us
    all_to_all x1, waiting for transfers between devices, line_exchange(): lax.all_to_all(cells, ('zl', *LON), split_axis=0, concat_axis=0, tiled=Tr...  11 us
    all_to_all x1, starting transfers between devices, line_exchange(): lax.all_to_all(cells, ('zl', *LON), split_axis=0, concat_axis=0, tiled=Tr...  4.91 us
    ppermute x1, starting transfers between devices, per_device(): far = lax.ppermute(mine, LON, swap)  3.06 us
    unnamed x16, local copies, waits for them, and re-layouts  2.33 us
  transfers between devices with their start and end apart: 9, of which 6 were waited for; matrix products, arithmetic and copies ran while one was open for 2% of the time, Pallas kernels for 10%

profile of v5, /device:TPU:1, one launch (start us, length us, event | category | flops | bytes accessed | tf_op | source)
XLA Modules:
  0.0 109.5 jit_solution(1781791020266540420)
XLA Ops:
  0.0 0.8 dynamic-slice_bitcast_fusion.1.table_ref
  0.8 1.0 copy-done
  1.8 1.0 shard_map.91
  2.8 19.2 %all-to-all-start = ((bf16[16,32,128]{2,1,0:T(8,128)(2,1)}), bf16[16,32,128]{2,1,0:T(8,128)(2,1)S(1)}, u32[]{:S(2)}, u32[]{:S(2)}) async-start(bf16[16,32,128]{2,1,0:T(8,128)(2,1)} %shard_map.91), calls=%async_computation | async-start | bytes 262144 | tf_op jit(solution)/shard_map/all_to_all | solution.py:410
  22.1 0.2 shard_map.92
  22.3 2.0 %collective-permute-start = (bf16[3,64,128]{2,1,0:T(8,128)(2,1)S(1)}, bf16[3,64,128]{2,1,0:T(8,128)(2,1)S(1)}, u32[]{:S(2)}, u32[]{:S(2)}) collective-permute-start(bf16[3,64,128]{2,1,0:T(8,128)(2,1)S(1)} %get-tuple-element.26), channel_id=1, source_target_pairs={{0,1},{1,0},{2,3},{3,2},{4,5},{5,4},{6,7},{7,6},{8,9},{9,8},{10,11... | collective-permute-start | bytes 147464 | tf_op jit(solution)/shard_map/ppermute | solution.py:442
  24.5 0.5 copy-done.7
  25.5 0.8 dynamic-slice_bitcast_fusion.table_ref
  26.5 0.7 copy-done.3
  27.1 0.3 shard_map.93.legs_ref
  27.5 9.6 %all-to-all-done.waves_ref = bf16[16,32,128]{2,1,0:T(8,128)(2,1)S(1)} async-done(((bf16[16,32,128]{2,1,0:T(8,128)(2,1)}), bf16[16,32,128]{2,1,0:T(8,128)(2,1)S(1)}, u32[]{:S(2)}, u32[]{:S(2)}) %all-to-all-start) | async-done | bytes 131104 | tf_op jit(solution)/shard_map/all_to_all | solution.py:410
  37.0 0.7 shard_map.94
  37.7 4.0 %all-to-all-start.1 = ((bf16[4,32,384]{2,1,0:T(8,128)(2,1)}), bf16[4,32,384]{2,1,0:T(8,128)(2,1)S(1)}, u32[]{:S(2)}, u32[]{:S(2)}) async-start(bf16[4,32,384]{2,1,0:T(8,128)(2,1)} %shard_map.94), calls=%async_computation.1 | async-start | bytes 196608 | tf_op jit(solution)/shard_map/all_to_all | solution.py:410
  41.7 4.7 %all-to-all-done.1.got_ref = bf16[4,32,384]{2,1,0:T(8,128)(2,1)S(1)} async-done(((bf16[4,32,384]{2,1,0:T(8,128)(2,1)}), bf16[4,32,384]{2,1,0:T(8,128)(2,1)S(1)}, u32[]{:S(2)}, u32[]{:S(2)}) %all-to-all-start.1) | async-done | bytes 98336 | tf_op jit(solution)/shard_map/all_to_all | solution.py:410
  46.4 0.8 shard_map.95
  47.2 6.1 %all-to-all-start.2 = ((bf16[8,48,128]{2,1,0:T(8,128)(2,1)}), bf16[8,48,128]{2,1,0:T(8,128)(2,1)S(1)}, u32[]{:S(2)}, u32[]{:S(2)}) async-start(bf16[8,48,128]{2,1,0:T(8,128)(2,1)} %get-tuple-element.31), calls=%async_computation.2 | async-start | bytes 196608 | tf_op jit(solution)/shard_map/all_to_all | solution.py:410
  53.4 3.1 %collective-permute-start.1 = (bf16[6,64,128]{2,1,0:T(8,128)(2,1)S(1)}, bf16[6,64,128]{2,1,0:T(8,128)(2,1)S(1)}, u32[]{:S(2)}, u32[]{:S(2)}) collective-permute-start(bf16[6,64,128]{2,1,0:T(8,128)(2,1)S(1)} %get-tuple-element.33), channel_id=1, source_target_pairs={{0,15},{1,2},{2,1},{3,4},{4,3},{5,6},{6,5},{7,8},{8,7},{9,10},{10,... | collective-permute-start | bytes 294920 | tf_op jit(solution)/shard_map/ppermute | solution.py:474
  56.5 0.2 pad_maximum_fusion.weight_ref
  56.7 6.7 %all-to-all-done.2.coeff_ref = bf16[8,48,128]{2,1,0:T(8,128)(2,1)S(1)} async-done(((bf16[8,48,128]{2,1,0:T(8,128)(2,1)}), bf16[8,48,128]{2,1,0:T(8,128)(2,1)S(1)}, u32[]{:S(2)}, u32[]{:S(2)}) %all-to-all-start.2) | async-done | bytes 98336 | tf_op jit(solution)/shard_map/all_to_all | solution.py:410
  63.4 1.1 %shard_map.96 = bf16[16,48,128]{2,1,0:T(8,128)(2,1)} custom-call(bf16[8,48,128]{2,1,0:T(8,128)(2,1)S(1)} %all-to-all-done.2.coeff_ref, bf16[24,64,128]{2,1,0:T(8,128)(2,1)S(1)} %pad_maximum_fusion.weight_ref), custom_call_target="tpu_custom_call" | custom-call | flops 10000000 | bytes 491520 | tf_op jit(solution)/shard_map/pallas_call | solution.py:206
  64.5 4.9 %all-to-all-start.3 = ((bf16[16,48,128]{2,1,0:T(8,128)(2,1)}), bf16[16,48,128]{2,1,0:T(8,128)(2,1)S(1)}, u32[]{:S(2)}, u32[]{:S(2)}) async-start(bf16[16,48,128]{2,1,0:T(8,128)(2,1)} %shard_map.96), calls=%async_computation.3 | async-start | bytes 393216 | tf_op jit(solution)/shard_map/all_to_all | solution.py:417
  69.4 0.1 shard_map.97
  69.5 2.2 %collective-permute-start.2 = (bf16[1,64,256]{2,1,0:T(8,128)(2,1)S(1)}, bf16[1,64,256]{2,1,0:T(8,128)(2,1)S(1)}, u32[]{:S(2)}, u32[]{:S(2)}) collective-permute-start(bf16[1,64,256]{2,1,0:T(8,128)(2,1)S(1)} %get-tuple-element.36), channel_id=1, source_target_pairs={{0,16},{16,0},{32,48},{48,32},{64,80},{80,64},{96,112},{112,96},{1... | collective-permute-start | bytes 98312 | tf_op jit(solution)/shard_map/ppermute | solution.py:365
  71.7 0.7 collective-permute-start.3
  72.4 1.8 %shard_map.98.early_ref = f32[3,64,180]{2,1,0:T(8,128)S(1)} custom-call(s32[1]{0:T(128)} %bitcast.core_ref.refs_0_, bf16[16,64,180]{2,1,0:T(8,128)(2,1)S(1)} %bitcast.24, bf16[3,64,128]{2,1,0:T(8,128)(2,1)S(1)} %collective-permute-done.near_ref.refs_3_, bf16[6,64,128]{2,1,0:T(8,128)(2,1)S(1)} %collective-permute-done.1.far_ref.other_ref.refs_4_, ...), custom_call_target="tpu_custom_call" | custom-call | flops 201326592 | bytes 647172 | tf_op jit(solution)/shard_map/pallas_call | solution.py:206
  74.2 0.3 collective-permute-done.2.refs_5_
  74.5 11.0 %all-to-all-done.3.mixed_ref = bf16[16,48,128]{2,1,0:T(8,128)(2,1)S(1)} async-done(((bf16[16,48,128]{2,1,0:T(8,128)(2,1)}), bf16[16,48,128]{2,1,0:T(8,128)(2,1)S(1)}, u32[]{:S(2)}, u32[]{:S(2)}) %all-to-all-start.3) | async-done | bytes 196640 | tf_op jit(solution)/shard_map/all_to_all | solution.py:417
  85.5 1.0 shard_map.99
  86.5 9.7 %all-to-all-start.4 = ((bf16[32,64,128]{2,1,0:T(8,128)(2,1)}), bf16[32,64,128]{2,1,0:T(8,128)(2,1)S(1)}, u32[]{:S(2)}, u32[]{:S(2)}) async-start(bf16[32,64,128]{2,1,0:T(8,128)(2,1)} %shard_map.99), calls=%async_computation.4 | async-start | bytes 1048576 | tf_op jit(solution)/shard_map/all_to_all | solution.py:410
  96.3 7.6 %shard_map.100.late_ref = f32[13,64,180]{2,1,0:T(8,128)S(1)} custom-call(s32[1]{0:T(128)} %bitcast.core_ref.refs_0_, s32[1]{0:T(128)} %bitcast.9.even_ref.refs_1_, bf16[16,64,180]{2,1,0:T(8,128)(2,1)S(1)} %bitcast.25, bf16[3,64,128]{2,1,0:T(8,128)(2,1)S(1)} %collective-permute-done.near_ref.refs_3_, ...), custom_call_target="tpu_custom_call" | custom-call | flops 872415232 | bytes 712712 | tf_op jit(solution)/shard_map/pallas_call | solution.py:206
  103.8 4.1 %all-to-all-done.4.modes_ref = bf16[32,64,128]{2,1,0:T(8,128)(2,1)S(1)} async-done(((bf16[32,64,128]{2,1,0:T(8,128)(2,1)}), bf16[32,64,128]{2,1,0:T(8,128)(2,1)S(1)}, u32[]{:S(2)}, u32[]{:S(2)}) %all-to-all-start.4) | async-done | bytes 524320 | tf_op jit(solution)/shard_map/all_to_all | solution.py:410
  107.9 1.6 %shard_map.101 = bf16[16,64,180]{2,1,0:T(8,128)(2,1)} custom-call(bf16[32,64,128]{2,1,0:T(8,128)(2,1)S(1)} %all-to-all-done.4.modes_ref, bf16[64,180]{1,0:T(8,128)(2,1)S(1)} %dynamic-slice_bitcast_fusion.table_ref, f32[3,64,180]{2,1,0:T(8,128)S(1)} %shard_map.98.early_ref, f32[13,64,180]{2,1,0:T(8,128)S(1)} %shard_map.100.late_ref, ...), custom_call_target="tpu_custom_call" | custom-call | flops 10000000 | bytes 1653248 | tf_op jit(solution)/shard_map/pallas_call | solution.py:206
  (27 shorter events, 0.8 us)
Async XLA Ops:
  0.8 1.0 copy-start
  1.8 20.3 %copy-start.1 = (bf16[16,180,64]{1,2,0:T(8,128)(2,1)S(1)}, bf16[16,180,64]{1,2,0:T(8,128)(2,1)}, u32[]{:S(2)}) copy-start(bf16[16,180,64]{1,2,0:T(8,128)(2,1)} %param.9) | copy-start | bytes 1105924
  2.8 34.2 %all-to-all-start = ((bf16[16,32,128]{2,1,0:T(8,128)(2,1)}), bf16[16,32,128]{2,1,0:T(8,128)(2,1)S(1)}, u32[]{:S(2)}, u32[]{:S(2)}) async-start(bf16[16,32,128]{2,1,0:T(8,128)(2,1)} %shard_map.91), calls=%async_computation | async-start | bytes 262144 | tf_op jit(solution)/shard_map/all_to_all | solution.py:410
  22.1 2.2 %copy-start.6 = (f32[16,492]{1,0:T(8,128)S(1)}, f32[16,492]{1,0:T(8,128)}, u32[]{:S(2)}) copy-start(f32[16,492]{1,0:T(8,128)} %param.11) | copy-start | bytes 94468
  22.3 5.1 %collective-permute-start = (bf16[3,64,128]{2,1,0:T(8,128)(2,1)S(1)}, bf16[3,64,128]{2,1,0:T(8,128)(2,1)S(1)}, u32[]{:S(2)}, u32[]{:S(2)}) collective-permute-start(bf16[3,64,128]{2,1,0:T(8,128)(2,1)S(1)} %get-tuple-element.26), channel_id=1, source_target_pairs={{0,1},{1,0},{2,3},{3,2},{4,5},{5,4},{6,7},{7,6},{8,9},{9,8},{10,11... | collective-permute-start | bytes 147464 | tf_op jit(solution)/shard_map/ppermute | solution.py:442
  24.4 0.7 copy-start.7
  25.2 1.2 %copy-start.2 = (bf16[768,256]{1,0:T(8,128)(2,1)S(1)}, bf16[768,256]{1,0:T(8,128)(2,1)}, u32[]{:S(2)}) copy-start(bf16[768,256]{1,0:T(8,128)(2,1)} %constant.54.clone.pick_ref) | copy-start | bytes 1179652
  25.5 0.8 copy-start.5
  26.3 0.8 copy-start.3
  26.3 27.0 %copy-start.4 = (bf16[24,2,64,64]{3,2,1,0:T(8,128)(2,1)S(1)}, bf16[24,2,64,64]{3,2,1,0:T(8,128)(2,1)}, u32[]{:S(2)}) copy-start(bf16[24,2,64,64]{3,2,1,0:T(8,128)(2,1)} %param.14) | copy-start | bytes 1179652
  37.7 8.7 %all-to-all-start.1 = ((bf16[4,32,384]{2,1,0:T(8,128)(2,1)}), bf16[4,32,384]{2,1,0:T(8,128)(2,1)S(1)}, u32[]{:S(2)}, u32[]{:S(2)}) async-start(bf16[4,32,384]{2,1,0:T(8,128)(2,1)} %shard_map.94), calls=%async_computation.1 | async-start | bytes 196608 | tf_op jit(solution)/shard_map/all_to_all | solution.py:410
  47.2 16.1 %all-to-all-start.2 = ((bf16[8,48,128]{2,1,0:T(8,128)(2,1)}), bf16[8,48,128]{2,1,0:T(8,128)(2,1)S(1)}, u32[]{:S(2)}, u32[]{:S(2)}) async-start(bf16[8,48,128]{2,1,0:T(8,128)(2,1)} %get-tuple-element.31), calls=%async_computation.2 | async-start | bytes 196608 | tf_op jit(solution)/shard_map/all_to_all | solution.py:410
  53.4 16.0 %collective-permute-start.1 = (bf16[6,64,128]{2,1,0:T(8,128)(2,1)S(1)}, bf16[6,64,128]{2,1,0:T(8,128)(2,1)S(1)}, u32[]{:S(2)}, u32[]{:S(2)}) collective-permute-start(bf16[6,64,128]{2,1,0:T(8,128)(2,1)S(1)} %get-tuple-element.33), channel_id=1, source_target_pairs={{0,15},{1,2},{2,1},{3,4},{4,3},{5,6},{6,5},{7,8},{8,7},{9,10},{10,... | collective-permute-start | bytes 294920 | tf_op jit(solution)/shard_map/ppermute | solution.py:474
  64.5 21.0 %all-to-all-start.3 = ((bf16[16,48,128]{2,1,0:T(8,128)(2,1)}), bf16[16,48,128]{2,1,0:T(8,128)(2,1)S(1)}, u32[]{:S(2)}, u32[]{:S(2)}) async-start(bf16[16,48,128]{2,1,0:T(8,128)(2,1)} %shard_map.96), calls=%async_computation.3 | async-start | bytes 393216 | tf_op jit(solution)/shard_map/all_to_all | solution.py:417
  69.5 5.0 %collective-permute-start.2 = (bf16[1,64,256]{2,1,0:T(8,128)(2,1)S(1)}, bf16[1,64,256]{2,1,0:T(8,128)(2,1)S(1)}, u32[]{:S(2)}, u32[]{:S(2)}) collective-permute-start(bf16[1,64,256]{2,1,0:T(8,128)(2,1)S(1)} %get-tuple-element.36), channel_id=1, source_target_pairs={{0,16},{16,0},{32,48},{48,32},{64,80},{80,64},{96,112},{112,96},{1... | collective-permute-start | bytes 98312 | tf_op jit(solution)/shard_map/ppermute | solution.py:365
  71.7 2.8 %collective-permute-start.3 = (bf16[1,64,256]{2,1,0:T(8,128)(2,1)S(1)}, bf16[1,64,256]{2,1,0:T(8,128)(2,1)S(1)}, u32[]{:S(2)}, u32[]{:S(2)}) collective-permute-start(bf16[1,64,256]{2,1,0:T(8,128)(2,1)S(1)} %get-tuple-element.37), channel_id=1, source_target_pairs={{16,32},{32,16},{48,64},{64,48},{80,96},{96,80},{112,128},{128,112... | collective-permute-start | bytes 98312 | tf_op jit(solution)/shard_map/ppermute | solution.py:366
  86.5 21.4 %all-to-all-start.4 = ((bf16[32,64,128]{2,1,0:T(8,128)(2,1)}), bf16[32,64,128]{2,1,0:T(8,128)(2,1)S(1)}, u32[]{:S(2)}, u32[]{:S(2)}) async-start(bf16[32,64,128]{2,1,0:T(8,128)(2,1)} %shard_map.99), calls=%async_computation.4 | async-start | bytes 1048576 | tf_op jit(solution)/shard_map/all_to_all | solution.py:410

commit v6 on v5

--- a/solution.py
+++ b/solution.py
@@ -454,8 +454,8 @@
             pltpu.VMEM((2, 8 * lat_rows, LANES), F32),
         ],
     )
-    waves, near, far, legs, inverse, base, taps_weight = lax.optimization_barrier(
-        (waves, near, far, legs, inverse, base, taps_weight)
+    waves, near, far, legs, inverse, base, taps_weight, weight = lax.optimization_barrier(
+        (waves, near, far, legs, inverse, base, taps_weight, weight)
     )
     message = call(spectra_kernel, struct(BF16, 4, 2 * lat_rows, 384), waves, legs)
     message = exchange(message, ("x",))

time: 110 us -> 109 us (level)
  blocking collectives: 0 us -> 8.46 us
  waiting for transfers between devices: 36.3 us -> 31.6 us
  starting transfers between devices: 52 us -> 47.5 us
    all_to_all x0 -> x1, blocking collectives: none -> 8.46 us  [exchange(): return lax.all_to_all(cells, axes, split_axis=0, concat_axis=0, tiled=True)]
    all_to_all x4 -> x3, waiting for transfers between devices: 25 us -> 19.9 us  [exchange(): return lax.all_to_all(cells, axes, split_axis=0, concat_axis=0, tiled=True)]
    all_to_all x4 -> x3, starting transfers between devices: 39.1 us -> 34.6 us  [exchange(): return lax.all_to_all(cells, axes, split_axis=0, concat_axis=0, tiled=True)]
  transfers between devices with their start and end apart: 9 -> 8, of which waited for: 6 -> 5; matrix products, arithmetic and copies ran while one was open for 2% -> 2% of each run, Pallas kernels for 10% -> 10%
where the time goes in v6:
time: 109 us; the launch traced here: 108 us
  starting transfers between devices  47.5 us (44%)
  waiting for transfers between devices  31.6 us (29%)
  Pallas kernels  15.6 us (14%)
  blocking collectives  8.46 us (8%)
  local copies, waits for them, and re-layouts  4.45 us (4%)
    all_to_all x3, starting transfers between devices, exchange(): return lax.all_to_all(cells, axes, split_axis=0, concat_axis=0, tiled=True)  34.6 us
    all_to_all x3, waiting for transfers between devices, exchange(): return lax.all_to_all(cells, axes, split_axis=0, concat_axis=0, tiled=True)  19.9 us
    pallas_call x11, Pallas kernels, call(): pl.pallas_call(kernel, out_shape=out, in_specs=[scalar] * smem + [vmem] *...  15.6 us
    all_to_all x1, waiting for transfers between devices, line_exchange(): lax.all_to_all(cells, ('zl', *LON), split_axis=0, concat_axis=0, tiled=Tr...  11.4 us
    all_to_all x1, blocking collectives, exchange(): return lax.all_to_all(cells, axes, split_axis=0, concat_axis=0, tiled=True)  8.46 us
    all_to_all x1, starting transfers between devices, line_exchange(): lax.all_to_all(cells, ('zl', *LON), split_axis=0, concat_axis=0, tiled=Tr...  4.61 us
    ppermute x1, starting transfers between devices, per_device(): far = lax.ppermute(mine, LON, swap)  3.41 us
    unnamed x16, local copies, waits for them, and re-layouts  2.39 us
  transfers between devices with their start and end apart: 8, of which 5 were waited for; matrix products, arithmetic and copies ran while one was open for 2% of the time, Pallas kernels for 10%

profile of v6, /device:TPU:1, one launch (start us, length us, event | category | flops | bytes accessed | tf_op | source)
XLA Modules:
  0.0 108.4 jit_solution(7867560960791816403)
XLA Ops:
  0.0 0.8 dynamic-slice_bitcast_fusion.1.table_ref
  0.8 1.0 copy-done
  1.8 1.0 shard_map.91
  2.9 19.2 %all-to-all-start = ((bf16[16,32,128]{2,1,0:T(8,128)(2,1)}), bf16[16,32,128]{2,1,0:T(8,128)(2,1)S(1)}, u32[]{:S(2)}, u32[]{:S(2)}) async-start(bf16[16,32,128]{2,1,0:T(8,128)(2,1)} %shard_map.91), calls=%async_computation | async-start | bytes 262144 | tf_op jit(solution)/shard_map/all_to_all | solution.py:410
  22.1 0.2 shard_map.92
  22.3 2.0 %collective-permute-start = (bf16[3,64,128]{2,1,0:T(8,128)(2,1)S(1)}, bf16[3,64,128]{2,1,0:T(8,128)(2,1)S(1)}, u32[]{:S(2)}, u32[]{:S(2)}) collective-permute-start(bf16[3,64,128]{2,1,0:T(8,128)(2,1)S(1)} %get-tuple-element.27), channel_id=1, source_target_pairs={{0,1},{1,0},{2,3},{3,2},{4,5},{5,4},{6,7},{7,6},{8,9},{9,8},{10,11... | collective-permute-start | bytes 147464 | tf_op jit(solution)/shard_map/ppermute | solution.py:442
  24.4 0.1 reshape.45
  24.5 0.6 copy-done.7
  25.5 0.2 pad_maximum_fusion.weight_ref
  25.7 0.1 pad_maximum_fusion.1.base_ref.refs_7_
  25.9 0.8 dynamic-slice_bitcast_fusion.table_ref
  26.8 0.7 copy-done.3
  27.5 0.3 shard_map.93.legs_ref
  27.8 9.2 %all-to-all-done.waves_ref = bf16[16,32,128]{2,1,0:T(8,128)(2,1)S(1)} async-done(((bf16[16,32,128]{2,1,0:T(8,128)(2,1)}), bf16[16,32,128]{2,1,0:T(8,128)(2,1)S(1)}, u32[]{:S(2)}, u32[]{:S(2)}) %all-to-all-start) | async-done | bytes 131104 | tf_op jit(solution)/shard_map/all_to_all | solution.py:410
  37.1 8.5 %all_to_all.25.got_ref = bf16[4,32,384]{2,1,0:T(8,128)(2,1)S(1)} all-to-all(bf16[4,32,384]{2,1,0:T(8,128)(2,1)S(1)} %shard_map.94), channel_id=1, replica_groups=mesh['zl'=8,'x'=4,'y'=4,'zh'=2,'core'=2] {'x'}, dimensions={0} | all-to-all | bytes 196608 | tf_op jit(solution)/shard_map/all_to_all | solution.py:410
  45.5 0.8 shard_map.95
  46.4 6.1 %all-to-all-start.2 = ((bf16[8,48,128]{2,1,0:T(8,128)(2,1)}), bf16[8,48,128]{2,1,0:T(8,128)(2,1)S(1)}, u32[]{:S(2)}, u32[]{:S(2)}) async-start(bf16[8,48,128]{2,1,0:T(8,128)(2,1)} %get-tuple-element.32), calls=%async_computation.2 | async-start | bytes 196608 | tf_op jit(solution)/shard_map/all_to_all | solution.py:410
  52.5 3.4 %collective-permute-start.1 = (bf16[6,64,128]{2,1,0:T(8,128)(2,1)S(1)}, bf16[6,64,128]{2,1,0:T(8,128)(2,1)S(1)}, u32[]{:S(2)}, u32[]{:S(2)}) collective-permute-start(bf16[6,64,128]{2,1,0:T(8,128)(2,1)S(1)} %get-tuple-element.35), channel_id=1, source_target_pairs={{0,15},{1,2},{2,1},{3,4},{4,3},{5,6},{6,5},{7,8},{8,7},{9,10},{10,... | collective-permute-start | bytes 294920 | tf_op jit(solution)/shard_map/ppermute | solution.py:474
  55.9 6.6 %all-to-all-done.2.coeff_ref = bf16[8,48,128]{2,1,0:T(8,128)(2,1)S(1)} async-done(((bf16[8,48,128]{2,1,0:T(8,128)(2,1)}), bf16[8,48,128]{2,1,0:T(8,128)(2,1)S(1)}, u32[]{:S(2)}, u32[]{:S(2)}) %all-to-all-start.2) | async-done | bytes 98336 | tf_op jit(solution)/shard_map/all_to_all | solution.py:410
  62.5 1.1 %shard_map.96 = bf16[16,48,128]{2,1,0:T(8,128)(2,1)} custom-call(bf16[8,48,128]{2,1,0:T(8,128)(2,1)S(1)} %all-to-all-done.2.coeff_ref, bf16[24,64,128]{2,1,0:T(8,128)(2,1)S(1)} %pad_maximum_fusion.weight_ref), custom_call_target="tpu_custom_call" | custom-call | flops 10000000 | bytes 491520 | tf_op jit(solution)/shard_map/pallas_call | solution.py:206
  63.7 4.6 %all-to-all-start.3 = ((bf16[16,48,128]{2,1,0:T(8,128)(2,1)}), bf16[16,48,128]{2,1,0:T(8,128)(2,1)S(1)}, u32[]{:S(2)}, u32[]{:S(2)}) async-start(bf16[16,48,128]{2,1,0:T(8,128)(2,1)} %shard_map.96), calls=%async_computation.3 | async-start | bytes 393216 | tf_op jit(solution)/shard_map/all_to_all | solution.py:417
  68.3 0.1 shard_map.97
  68.4 2.2 %collective-permute-start.2 = (bf16[1,64,256]{2,1,0:T(8,128)(2,1)S(1)}, bf16[1,64,256]{2,1,0:T(8,128)(2,1)S(1)}, u32[]{:S(2)}, u32[]{:S(2)}) collective-permute-start(bf16[1,64,256]{2,1,0:T(8,128)(2,1)S(1)} %get-tuple-element.38), channel_id=1, source_target_pairs={{0,16},{16,0},{32,48},{48,32},{64,80},{80,64},{96,112},{112,96},{1... | collective-permute-start | bytes 98312 | tf_op jit(solution)/shard_map/ppermute | solution.py:365
  70.6 0.7 collective-permute-start.3
  71.3 1.8 %shard_map.98.early_ref = f32[3,64,180]{2,1,0:T(8,128)S(1)} custom-call(s32[1]{0:T(128)} %bitcast.core_ref.refs_0_, bf16[16,64,180]{2,1,0:T(8,128)(2,1)S(1)} %bitcast.24, bf16[3,64,128]{2,1,0:T(8,128)(2,1)S(1)} %collective-permute-done.near_ref.refs_3_, bf16[6,64,128]{2,1,0:T(8,128)(2,1)S(1)} %collective-permute-done.1.far_ref.other_ref.refs_4_, ...), custom_call_target="tpu_custom_call" | custom-call | flops 201326592 | bytes 647172 | tf_op jit(solution)/shard_map/pallas_call | solution.py:206
  73.1 0.3 collective-permute-done.2.refs_5_
  73.4 11.4 %all-to-all-done.3.mixed_ref = bf16[16,48,128]{2,1,0:T(8,128)(2,1)S(1)} async-done(((bf16[16,48,128]{2,1,0:T(8,128)(2,1)}), bf16[16,48,128]{2,1,0:T(8,128)(2,1)S(1)}, u32[]{:S(2)}, u32[]{:S(2)}) %all-to-all-start.3) | async-done | bytes 196640 | tf_op jit(solution)/shard_map/all_to_all | solution.py:417
  84.8 1.0 shard_map.99
  85.8 9.3 %all-to-all-start.4 = ((bf16[32,64,128]{2,1,0:T(8,128)(2,1)}), bf16[32,64,128]{2,1,0:T(8,128)(2,1)S(1)}, u32[]{:S(2)}, u32[]{:S(2)}) async-start(bf16[32,64,128]{2,1,0:T(8,128)(2,1)} %shard_map.99), calls=%async_computation.4 | async-start | bytes 1048576 | tf_op jit(solution)/shard_map/all_to_all | solution.py:410
  95.1 7.6 %shard_map.100.late_ref = f32[13,64,180]{2,1,0:T(8,128)S(1)} custom-call(s32[1]{0:T(128)} %bitcast.core_ref.refs_0_, s32[1]{0:T(128)} %bitcast.9.even_ref.refs_1_, bf16[16,64,180]{2,1,0:T(8,128)(2,1)S(1)} %bitcast.25, bf16[3,64,128]{2,1,0:T(8,128)(2,1)S(1)} %collective-permute-done.near_ref.refs_3_, ...), custom_call_target="tpu_custom_call" | custom-call | flops 872415232 | bytes 712712 | tf_op jit(solution)/shard_map/pallas_call | solution.py:206
  102.7 4.1 %all-to-all-done.4.modes_ref = bf16[32,64,128]{2,1,0:T(8,128)(2,1)S(1)} async-done(((bf16[32,64,128]{2,1,0:T(8,128)(2,1)}), bf16[32,64,128]{2,1,0:T(8,128)(2,1)S(1)}, u32[]{:S(2)}, u32[]{:S(2)}) %all-to-all-start.4) | async-done | bytes 524320 | tf_op jit(solution)/shard_map/all_to_all | solution.py:410
  106.7 1.6 %shard_map.101 = bf16[16,64,180]{2,1,0:T(8,128)(2,1)} custom-call(bf16[32,64,128]{2,1,0:T(8,128)(2,1)S(1)} %all-to-all-done.4.modes_ref, bf16[64,180]{1,0:T(8,128)(2,1)S(1)} %dynamic-slice_bitcast_fusion.table_ref, f32[3,64,180]{2,1,0:T(8,128)S(1)} %shard_map.98.early_ref, f32[13,64,180]{2,1,0:T(8,128)S(1)} %shard_map.100.late_ref, ...), custom_call_target="tpu_custom_call" | custom-call | flops 10000000 | bytes 1653248 | tf_op jit(solution)/shard_map/pallas_call | solution.py:206
  (26 shorter events, 0.6 us)
Async XLA Ops:
  0.8 1.0 copy-start
  1.8 20.3 %copy-start.1 = (bf16[16,180,64]{1,2,0:T(8,128)(2,1)S(1)}, bf16[16,180,64]{1,2,0:T(8,128)(2,1)}, u32[]{:S(2)}) copy-start(bf16[16,180,64]{1,2,0:T(8,128)(2,1)} %param.9) | copy-start | bytes 1105924
  1.8 22.7 %copy-start.4 = (bf16[24,2,64,64]{3,2,1,0:T(8,128)(2,1)S(1)}, bf16[24,2,64,64]{3,2,1,0:T(8,128)(2,1)}, u32[]{:S(2)}) copy-start(bf16[24,2,64,64]{3,2,1,0:T(8,128)(2,1)} %param.14) | copy-start | bytes 1179652
  2.9 34.2 %all-to-all-start = ((bf16[16,32,128]{2,1,0:T(8,128)(2,1)}), bf16[16,32,128]{2,1,0:T(8,128)(2,1)S(1)}, u32[]{:S(2)}, u32[]{:S(2)}) async-start(bf16[16,32,128]{2,1,0:T(8,128)(2,1)} %shard_map.91), calls=%async_computation | async-start | bytes 262144 | tf_op jit(solution)/shard_map/all_to_all | solution.py:410
  22.1 2.2 %copy-start.6 = (f32[16,492]{1,0:T(8,128)S(1)}, f32[16,492]{1,0:T(8,128)}, u32[]{:S(2)}) copy-start(f32[16,492]{1,0:T(8,128)} %param.11) | copy-start | bytes 94468
  22.3 5.5 %collective-permute-start = (bf16[3,64,128]{2,1,0:T(8,128)(2,1)S(1)}, bf16[3,64,128]{2,1,0:T(8,128)(2,1)S(1)}, u32[]{:S(2)}, u32[]{:S(2)}) collective-permute-start(bf16[3,64,128]{2,1,0:T(8,128)(2,1)S(1)} %get-tuple-element.27), channel_id=1, source_target_pairs={{0,1},{1,0},{2,3},{3,2},{4,5},{5,4},{6,7},{7,6},{8,9},{9,8},{10,11... | collective-permute-start | bytes 147464 | tf_op jit(solution)/shard_map/ppermute | solution.py:442
  24.5 0.7 copy-start.7
  25.7 1.1 copy-start.2
  25.9 0.8 copy-start.5
  26.7 0.8 copy-start.3
  46.4 16.1 %all-to-all-start.2 = ((bf16[8,48,128]{2,1,0:T(8,128)(2,1)}), bf16[8,48,128]{2,1,0:T(8,128)(2,1)S(1)}, u32[]{:S(2)}, u32[]{:S(2)}) async-start(bf16[8,48,128]{2,1,0:T(8,128)(2,1)} %get-tuple-element.32), calls=%async_computation.2 | async-start | bytes 196608 | tf_op jit(solution)/shard_map/all_to_all | solution.py:410
  52.5 15.8 %collective-permute-start.1 = (bf16[6,64,128]{2,1,0:T(8,128)(2,1)S(1)}, bf16[6,64,128]{2,1,0:T(8,128)(2,1)S(1)}, u32[]{:S(2)}, u32[]{:S(2)}) collective-permute-start(bf16[6,64,128]{2,1,0:T(8,128)(2,1)S(1)} %get-tuple-element.35), channel_id=1, source_target_pairs={{0,15},{1,2},{2,1},{3,4},{4,3},{5,6},{6,5},{7,8},{8,7},{9,10},{10,... | collective-permute-start | bytes 294920 | tf_op jit(solution)/shard_map/ppermute | solution.py:474
  63.7 21.1 %all-to-all-start.3 = ((bf16[16,48,128]{2,1,0:T(8,128)(2,1)}), bf16[16,48,128]{2,1,0:T(8,128)(2,1)S(1)}, u32[]{:S(2)}, u32[]{:S(2)}) async-start(bf16[16,48,128]{2,1,0:T(8,128)(2,1)} %shard_map.96), calls=%async_computation.3 | async-start | bytes 393216 | tf_op jit(solution)/shard_map/all_to_all | solution.py:417
  68.4 5.0 %collective-permute-start.2 = (bf16[1,64,256]{2,1,0:T(8,128)(2,1)S(1)}, bf16[1,64,256]{2,1,0:T(8,128)(2,1)S(1)}, u32[]{:S(2)}, u32[]{:S(2)}) collective-permute-start(bf16[1,64,256]{2,1,0:T(8,128)(2,1)S(1)} %get-tuple-element.38), channel_id=1, source_target_pairs={{0,16},{16,0},{32,48},{48,32},{64,80},{80,64},{96,112},{112,96},{1... | collective-permute-start | bytes 98312 | tf_op jit(solution)/shard_map/ppermute | solution.py:365
  70.6 2.8 %collective-permute-start.3 = (bf16[1,64,256]{2,1,0:T(8,128)(2,1)S(1)}, bf16[1,64,256]{2,1,0:T(8,128)(2,1)S(1)}, u32[]{:S(2)}, u32[]{:S(2)}) collective-permute-start(bf16[1,64,256]{2,1,0:T(8,128)(2,1)S(1)} %get-tuple-element.39), channel_id=1, source_target_pairs={{16,32},{32,16},{48,64},{64,48},{80,96},{96,80},{112,128},{128,112... | collective-permute-start | bytes 98312 | tf_op jit(solution)/shard_map/ppermute | solution.py:366
  85.8 20.9 %all-to-all-start.4 = ((bf16[32,64,128]{2,1,0:T(8,128)(2,1)}), bf16[32,64,128]{2,1,0:T(8,128)(2,1)S(1)}, u32[]{:S(2)}, u32[]{:S(2)}) async-start(bf16[32,64,128]{2,1,0:T(8,128)(2,1)} %shard_map.99), calls=%async_computation.4 | async-start | bytes 1048576 | tf_op jit(solution)/shard_map/all_to_all | solution.py:410
